TPU v7x, 32 devices: a whole 2x2x4 slice. The times are simulated.
32 devices in a mesh: seq: 8 (over y, x, core), stream: 4 (over z).
Axes of the slice: x: 2, y: 2, z: 4, core: 2. Of those that a mesh axis runs over, the one named last changes fastest.
Arguments:
- tokens: bfloat16 [4, 1024, 1024], P('stream', 'seq'), may hold values from -6 to 6
- grad_out: bfloat16 [4, 1024, 1024], P('stream', 'seq'), may hold values from -6 to 6
- doc_lengths: int32 [4, 8], P('stream'), may hold values from 1 to 512, 1024 in all within a row
- gain_in: float32 [1024], replicated, may hold values from 0.5 to 1.5
- in_weight: bfloat16 [1024, 6144], replicated, may hold values from -0.1875 to 0.1875
- small_weight: float32 [1024, 24], replicated, may hold values from -0.1875 to 0.1875
- gate_bias: float32 [8], replicated, may hold values from -1 to 1
- decay_rate: float32 [8], replicated, may hold values from 0.0009765625 to 0.1
- conv_weight: float32 [4, 5120], replicated, may hold values from -3 to 3
- gain_head: float32 [128], replicated, may hold values from 0.5 to 1.5
- out_weight: bfloat16 [1024, 1024], replicated, may hold values from -0.1875 to 0.1875
- gain_mid: float32 [1024], replicated, may hold values from 0.5 to 1.5
- gate_up_weight: bfloat16 [1024, 5632], replicated, may hold values from -0.1875 to 0.1875
- down_weight: bfloat16 [2816, 1024], replicated, may hold values from -0.109375 to 0.109375
Outputs:
- output: bfloat16 [4, 1024, 1024], P('stream', 'seq')
- grad_input: float32 [4, 1024, 1024], P('stream', 'seq')
- grad_gain_in: float32 [1024], replicated
- grad_in_weight: float32 [1024, 6144], P(('seq', 'stream'))
- grad_small_weight: float32 [1024, 24], replicated
- grad_gate_bias: float32 [8], replicated
- grad_decay_rate: float32 [8], replicated
- grad_conv_weight: float32 [4, 5120], replicated
- grad_gain_head: float32 [128], replicated
- grad_out_weight: float32 [1024, 1024], P(('seq', 'stream'))
- grad_gain_mid: float32 [1024], replicated
- grad_gate_up_weight: float32 [1024, 5632], P(('seq', 'stream'))
- grad_down_weight: float32 [2816, 1024], P(('seq', 'stream'))
Inputs may be any that keep to these rules, and one draw needn't show every extreme that they name: `doc_lengths`: each row holds the lengths of the 8 consecutive documents of one domain sequence, 1 or more each, summing to 1024; the longest is exactly 512.
All inputs are finite; a program needn't handle non-finite values.
Results may differ from a plain program's by a relative error of at most 0.014.
The roundings to bfloat16 on the way count: a program that leaves them out, or rounds other values in their place, can miss the bound.
Values may be sent and summed in bfloat16 or wider, within the bound.
A program may use at most 256 MiB of HBM per device.

v0:
```python
import jax
import jax.numpy as jnp
from jax import lax
from jax.sharding import PartitionSpec as P

D = 1024
H = 8
HD = 128
FF = 2816
NH = 2
CONV = 4
SPAN = 64


highest = lax.Precision.HIGHEST


def from_behind(block, axis, distance):
    devices = range(lax.axis_size(axis))
    route = [(i - distance, i) for i in devices if i - distance in devices]
    return lax.ppermute(block, axis, route)


def carried_in(array, axis, combine, identity):
    length, place = (lax.axis_size(axis), lax.axis_index(axis))
    everything = jax.tree.map(
        lambda part, kind: lax.all_gather(part.astype(kind), axis),
        array,
        (jnp.bfloat16, jnp.bfloat16),
    )
    start = jax.tree.map(
        lambda part, zero: jnp.broadcast_to(jnp.asarray(zero, part.dtype), part.shape),
        array,
        identity,
    )

    def carried_turn(k, before):
        reached = k < place
        new = combine(
            before, jax.tree.map(lambda part, own: part[k].astype(own.dtype), everything, array)
        )
        return jax.tree.map(lambda a, b: jnp.where(reached, a, b), new, before)

    return lax.fori_loop(0, length, carried_turn, start)


def prefix_2(array, axis, combine, identity):
    length, place = (lax.axis_size(axis), lax.axis_index(axis))
    everything = jax.tree.map(
        lambda part, kind: lax.all_gather(part.astype(kind), axis),
        array,
        jax.tree.map(lambda a: jnp.bfloat16 if a.dtype == jnp.float32 else a.dtype, array),
    )
    start = jax.tree.map(
        lambda part, zero: jnp.broadcast_to(jnp.asarray(zero, part.dtype), part.shape),
        array,
        identity,
    )

    def prefix_turn(k, before):
        at = length - 1 - k
        reached = at > place
        new = combine(
            before, jax.tree.map(lambda part, own: part[at].astype(own.dtype), everything, array)
        )
        return jax.tree.map(lambda a, b: jnp.where(reached, a, b), new, before)

    return lax.fori_loop(0, length, prefix_turn, start)


def rms_scale(values, gain):
    return values * lax.rsqrt(jnp.mean(values * values, axis=-1, keepdims=True) + 1e-06) * gain


def solve_lower(matrix, target):
    return jax.scipy.linalg.solve_triangular(matrix, target, lower=True, unit_diagonal=True)


def block_core(state, key_rows, value_rows, betas, log_gates, resets):
    width = resets.shape[0]
    places = jnp.arange(width, dtype=jnp.int32)
    counted = jnp.cumsum(resets)
    joined = (counted[:, None] == counted[None, :]) & (places[None, :] <= places[:, None])
    before = (joined & (places[None, :] < places[:, None])).astype(jnp.float32)
    cumul = jnp.cumsum(log_gates, axis=0).T
    decays = (
        jnp.exp(jnp.where(joined[None], cumul[:, :, None] - cumul[:, None, :], 0.0))
        * joined.astype(jnp.float32)[None]
    )
    head_decay = jnp.exp(cumul) * (counted == 0).astype(jnp.float32)[None, :]
    products = jnp.einsum("ihk,jhk->hij", key_rows, key_rows, precision=highest)
    beta_heads = betas.T
    strict_lower = beta_heads[:, :, None] * decays * products * before[None]
    from_state = jnp.einsum("hvk,ihk->hiv", state, key_rows, precision=highest)
    target = beta_heads[:, :, None] * (
        jnp.transpose(value_rows, (1, 0, 2)) - head_decay[:, :, None] * from_state
    )
    new_values = jax.vmap(solve_lower)(strict_lower, target)
    return (new_values, decays, head_decay)


def block_end(state, key_rows, new_values, decays, head_decay):
    carried = head_decay[:, -1][:, None, None] * state
    return carried + jnp.einsum(
        "hj,hjv,jhk->hvk", decays[:, -1, :], new_values, key_rows, precision=highest
    )


def block_out(state, queries, key_rows, new_values, decays, head_decay):
    chosen = decays[:, NH - 1 :: NH, :]
    head_chosen = head_decay[:, NH - 1 :: NH]
    scores = jnp.einsum("rhk,jhk->hrj", queries, key_rows, precision=highest) * chosen
    from_state = jnp.einsum("hvk,rhk->rhv", state, queries, precision=highest)
    return head_chosen.T[:, :, None] * from_state + jnp.einsum(
        "hrj,hjv->rhv", scores, new_values, precision=highest
    )


def run_outputs(start_state, prepared, resets):

    def advance(state, block):
        queries, key_rows, value_rows, betas, log_gates, reset_flags = block
        new_values, decays, head_decay = block_core(
            state, key_rows, value_rows, betas, log_gates, reset_flags
        )
        return (
            block_end(state, key_rows, new_values, decays, head_decay),
            block_out(state, queries, key_rows, new_values, decays, head_decay),
        )

    end_state, outputs = lax.scan(jax.checkpoint(advance), start_state, prepared + (resets,))
    return (outputs.reshape(-1, H, HD), end_state)


def run_transition(prepared, resets, identity_maps, state_zero):
    queries, key_rows, value_rows, betas, log_gates = prepared

    def advance(states_pair, block):
        key_block, value_block, beta_block, log_block, reset_block = block

        def single(state, values):
            new_values, decays, head_decay = block_core(
                state, key_block, values, beta_block, log_block, reset_block
            )
            return block_end(state, key_block, new_values, decays, head_decay)

        return (
            jax.vmap(single)(states_pair, jnp.stack([jnp.zeros_like(value_block), value_block])),
            None,
        )

    finished, _ = lax.scan(
        advance,
        jnp.stack([identity_maps, state_zero]),
        (key_rows, value_rows, betas, log_gates, resets),
    )
    return (finished[0], finished[1])


def compose(earlier, later):
    first_map, first_add = earlier
    second_map, second_add = later
    joined_map = jnp.einsum("hab,hbc->hac", first_map, second_map, precision=highest)
    joined_add = jnp.einsum("hvb,hbc->hvc", first_add, second_map, precision=highest) + second_add
    return (joined_map, joined_add)


def doc_masks(lengths, first_position, count_tokens):
    offsets = jnp.cumsum(lengths) - lengths
    positions = first_position - (CONV - 1) + jnp.arange(count_tokens + CONV - 1, dtype=jnp.int32)
    doc_ids = jnp.sum((offsets[None, :] <= positions[:, None]).astype(jnp.int32), axis=1) - 1
    current = doc_ids[CONV - 1 :]
    same_doc = jnp.stack(
        [
            (doc_ids[CONV - 1 - lag_step : CONV - 1 - lag_step + count_tokens] == current).astype(
                jnp.float32
            )
            for lag_step in range(CONV)
        ]
    )
    starts = jnp.any(offsets[None, :] == positions[CONV - 1 :, None], axis=1).astype(jnp.int32)
    flags = jnp.concatenate([starts[:, None], jnp.zeros((count_tokens, NH - 1), jnp.int32)], axis=1)
    return (same_doc, flags.reshape(count_tokens // SPAN, NH * SPAN))


def mix_inputs(extended, small, conv_weight, gate_bias, decay_rate, same_doc):
    count_tokens = extended.shape[0] - (CONV - 1)
    mixed = extended[CONV - 1 :] * conv_weight[CONV - 1]
    for lag_step in range(1, CONV):
        earlier = extended[CONV - 1 - lag_step : CONV - 1 - lag_step + count_tokens]
        mixed = mixed + earlier * conv_weight[CONV - 1 - lag_step] * same_doc[lag_step][:, None]
    active = jax.nn.silu(mixed)
    queries = active[:, :D].reshape(count_tokens, H, HD)
    key_rows = active[:, D : D + NH * D].reshape(count_tokens * NH, H, HD)
    key_rows = key_rows * lax.rsqrt(jnp.sum(key_rows * key_rows, axis=-1, keepdims=True) + 1e-06)
    value_rows = active[:, D + NH * D :].reshape(count_tokens * NH, H, HD)
    betas = (2.0 * jax.nn.sigmoid(small[:, : NH * H])).reshape(count_tokens * NH, H)
    log_first = -decay_rate * jax.nn.softplus(small[:, NH * H :] + gate_bias)
    log_gates = jnp.concatenate(
        [log_first[:, None, :], jnp.zeros((count_tokens, NH - 1, H), jnp.float32)], axis=1
    )
    blocks = count_tokens // SPAN
    return (
        queries.reshape(blocks, SPAN, H, HD),
        key_rows.reshape(blocks, NH * SPAN, H, HD),
        value_rows.reshape(blocks, NH * SPAN, H, HD),
        betas.reshape(blocks, NH * SPAN, H),
        log_gates.reshape(blocks, NH * SPAN, H),
    )


def gate_piece(outputs, gate_raw, gain_head):
    count_tokens = outputs.shape[0]
    scaled = (
        outputs * lax.rsqrt(jnp.mean(outputs * outputs, axis=-1, keepdims=True) + 1e-06) * gain_head
    )
    return (scaled * jax.nn.silu(gate_raw.reshape(count_tokens, H, HD))).reshape(
        count_tokens, H * HD
    )


def swish_gate(gate_up):
    return jax.nn.silu(gate_up[:, :FF]) * gate_up[:, FF:]


def on_device(
    tokens,
    grad_out,
    doc_lengths,
    gain_in,
    in_weight,
    small_weight,
    gate_bias,
    decay_rate,
    conv_weight,
    gain_head,
    out_weight,
    gain_mid,
    gate_up_weight,
    down_weight,
):
    token_values = tokens[0].astype(jnp.float32)
    count_tokens = token_values.shape[0]
    channels = (1 + 2 * NH) * D
    seq_index = lax.axis_index("seq")
    same_doc, reset_flags = doc_masks(doc_lengths[0], seq_index * count_tokens, count_tokens)
    normed_full, input_pull = jax.vjp(rms_scale, token_values, gain_in)
    normed = normed_full.astype(jnp.bfloat16)
    projected = jnp.dot(normed, in_weight, preferred_element_type=jnp.float32).astype(jnp.bfloat16)
    small = jnp.dot(normed.astype(jnp.float32), small_weight, precision=highest)
    received = from_behind(projected[count_tokens - (CONV - 1) :, :channels], "seq", 1)
    extended = jnp.concatenate([received, projected[:, :channels]], axis=0).astype(jnp.float32)

    def prepare(extended_rows, small_rows, conv_taps, bias_values, rate_values):
        return mix_inputs(extended_rows, small_rows, conv_taps, bias_values, rate_values, same_doc)

    prepared, prepare_pull = jax.vjp(prepare, extended, small, conv_weight, gate_bias, decay_rate)
    identity_maps = jnp.broadcast_to(jnp.eye(HD, dtype=jnp.float32), (H, HD, HD))
    state_zero = jnp.zeros((H, HD, HD), jnp.float32)
    transfer_map, transfer_add = run_transition(prepared, reset_flags, identity_maps, state_zero)
    prefix = carried_in((transfer_map, transfer_add), "seq", compose, (identity_maps, state_zero))
    incoming = prefix[1]

    def mixer(start_state, prepared_values):
        return run_outputs(start_state, prepared_values, reset_flags)

    (outputs, _), mixer_pull = jax.vjp(mixer, incoming, prepared)
    gate_raw = projected[:, channels:].astype(jnp.float32)
    gated_full, gate_pull = jax.vjp(gate_piece, outputs, gate_raw, gain_head)
    gated = gated_full.astype(jnp.bfloat16)
    attention = jnp.dot(gated, out_weight, preferred_element_type=jnp.float32)
    residual = token_values + attention
    mid_full, mid_pull = jax.vjp(rms_scale, residual, gain_mid)
    normed_mid = mid_full.astype(jnp.bfloat16)
    gate_up = jnp.dot(normed_mid, gate_up_weight, preferred_element_type=jnp.float32)
    hidden_full, hidden_pull = jax.vjp(swish_gate, gate_up)
    hidden = hidden_full.astype(jnp.bfloat16)
    result = (residual + jnp.dot(hidden, down_weight, preferred_element_type=jnp.float32)).astype(
        jnp.bfloat16
    )
    cotangent = grad_out[0]
    grad_down = jnp.einsum("tf,td->fd", hidden, cotangent, preferred_element_type=jnp.float32)
    grad_hidden = jnp.einsum(
        "td,fd->tf", cotangent, down_weight, preferred_element_type=jnp.float32
    )
    grad_gate_up_full = hidden_pull(grad_hidden)[0]
    grad_gate_up_low = grad_gate_up_full.astype(jnp.bfloat16)
    grad_gate_up = jnp.einsum(
        "td,tf->df", normed_mid, grad_gate_up_low, preferred_element_type=jnp.float32
    )
    grad_mid = jnp.einsum(
        "tf,df->td", grad_gate_up_low, gate_up_weight, preferred_element_type=jnp.float32
    )
    grad_residual_part, grad_gain_mid = mid_pull(grad_mid)
    grad_residual = cotangent.astype(jnp.float32) + grad_residual_part
    grad_residual_low = grad_residual.astype(jnp.bfloat16)
    grad_out_weight = jnp.einsum(
        "tc,td->cd", gated, grad_residual_low, preferred_element_type=jnp.float32
    )
    grad_gated = jnp.einsum(
        "td,cd->tc", grad_residual_low, out_weight, preferred_element_type=jnp.float32
    )
    grad_outputs, grad_gate_raw, grad_gain_head = gate_pull(grad_gated)
    own_part = mixer_pull((grad_outputs, state_zero))[0]
    flipped = jnp.transpose(transfer_map, (0, 2, 1))
    suffix = prefix_2((flipped, own_part), "seq", compose, (identity_maps, state_zero))
    carried = suffix[1]
    grad_prepared = mixer_pull((grad_outputs, carried))[1]
    grad_extended, grad_small, grad_conv, grad_bias, grad_rate = prepare_pull(grad_prepared)
    returned = from_behind(grad_extended[: CONV - 1].astype(jnp.bfloat16), "seq", -1).astype(
        jnp.float32
    )
    own_rows = grad_extended[CONV - 1 :]
    grad_conv_input = jnp.concatenate(
        [own_rows[: count_tokens - (CONV - 1)], own_rows[count_tokens - (CONV - 1) :] + returned],
        axis=0,
    )
    grad_projected = jnp.concatenate([grad_conv_input, grad_gate_raw], axis=1).astype(jnp.bfloat16)
    grad_in_weight = jnp.einsum(
        "td,tc->dc", normed, grad_projected, preferred_element_type=jnp.float32
    )
    grad_normed = jnp.einsum(
        "tc,dc->td", grad_projected, in_weight, preferred_element_type=jnp.float32
    )
    grad_normed = grad_normed + jnp.einsum("tc,dc->td", grad_small, small_weight, precision=highest)
    grad_small_weight = jnp.einsum(
        "td,tc->dc", normed.astype(jnp.float32), grad_small, precision=highest
    )
    grad_input_part, grad_gain_in = input_pull(grad_normed)
    grad_input = grad_residual + grad_input_part
    summed = (
        lax.psum_scatter(grad_in_weight, ("seq", "stream"), scatter_dimension=0, tiled=True),
        lax.psum_scatter(grad_out_weight, ("seq", "stream"), scatter_dimension=0, tiled=True),
        lax.psum_scatter(grad_gate_up, ("seq", "stream"), scatter_dimension=0, tiled=True),
        lax.psum_scatter(grad_down, ("seq", "stream"), scatter_dimension=0, tiled=True),
    )
    small_sums = lax.psum(
        (
            grad_gain_in,
            grad_small_weight,
            grad_bias,
            grad_rate,
            grad_conv,
            grad_gain_head,
            grad_gain_mid,
        ),
        ("seq", "stream"),
    )
    return (
        result[None],
        grad_input[None],
        small_sums[0],
        summed[0],
        small_sums[1],
        small_sums[2],
        small_sums[3],
        small_sums[4],
        small_sums[5],
        summed[1],
        small_sums[6],
        summed[2],
        summed[3],
    )


def solution(mesh):
    placed = (
        P("stream", "seq", None),
        P("stream", "seq", None),
        P("stream", None),
        P(),
        P(),
        P(),
        P(),
        P(),
        P(),
        P(),
        P(),
        P(),
        P(),
        P(),
    )
    return jax.shard_map(
        on_device,
        mesh=mesh,
        in_specs=placed,
        out_specs=(
            P("stream", "seq", None),
            P("stream", "seq", None),
            P(),
            P(("seq", "stream"), None),
            P(),
            P(),
            P(),
            P(),
            P(),
            P(("seq", "stream"), None),
            P(),
            P(("seq", "stream"), None),
            P(("seq", "stream"), None),
        ),
        check_vma=False,
    )
```

profile of v0, /device:TPU:0, one launch (start us, length us, event | category | flops | bytes accessed | tf_op | source)
XLA Modules:
  0.0 2424.8 jit_solution(3702594666526442061)
XLA Ops:
  9.1 6.6 convolution_convert_fusion
  45.9 201.2 %while.95 = (s32[]{:T(128)}, f32[2,8,128,128]{3,2,0,1:T(8,128)}, f32[2,128,8]{2,1,0:T(8,128)S(1)}, s32[2,128]{1,0:T(2,128)S(1)}, f32[2,128,8]{1,2,0:T(8,128)}, /...) while((s32[]{:T(128)}, f32[2,8,128,128]{3,2,0,1:T(8,128)}, ...), condition=%wide.region_8.9_spmd, body=%wide.region_5.8_spmd.sunk | while | flops 1412612352 | bytes 22122224 | solution.py:152
  49.6 80.0 %custom-call.27 = f32[8,1,128,128]{2,3,1,0:T(8,128)} custom-call(f32[8,1,128,128]{3,2,1,0:T(8,128)} %fusion.424), custom_call_target="InvertDiagBlocksLowerTriangular" | custom-call | tf_op jit(solution)/shard_map/while/body/eval_jaxpr/vmap(vmap(jit(_solve_triangular)))/triangular_solve | solution.py:76
  150.2 80.0 %custom-call.27 = f32[8,1,128,128]{2,3,1,0:T(8,128)} custom-call(f32[8,1,128,128]{3,2,1,0:T(8,128)} %fusion.424), custom_call_target="InvertDiagBlocksLowerTriangular" | custom-call | tf_op jit(solution)/shard_map/while/body/eval_jaxpr/vmap(vmap(jit(_solve_triangular)))/triangular_solve | solution.py:76
  258.6 20.6 all-gather.9.cloned.1.call-done
  279.2 30.4 %all-gather.7.cloned.1.call-done = bf16[8,8,128,128]{3,2,1,0:T(8,128)(2,1)} async-done(((bf16[1,8,128,128]{3,2,1,0:T(8,128)(2,1)}), bf16[8,8,128,128]{3,2,1,0:T(8,128)(2,1)}) %all-gather.7.cloned.1.call-update) | async-done | bytes 2097168 | tf_op jit(solution)/shard_map/all_gather | solution.py:27
  309.6 50.7 %while.98 = (s32[]{:T(128)}, f32[8,128,128]{1,2,0:T(8,128)}, s32[]{:T(128)}, bf16[8,8,128,128]{3,2,1,0:T(8,128)(2,1)}, bf16[8,8,128,128]{3,2,1,0:T(8,128)(2,1)}, /*index=5*/s32[]{:T(128)}, s32[]{:T(128)}) while((s32[]{:T(128)}, f32[8,128,128]{1,2,0:T(8,128)}, s32[]{:T(128)}, bf16[8,8,128,128]{3,2,1,0:T(8,128)(2,1)}, ...), condition=%wide.region_10.11_spmd.clone, body=%wide.region_9.10_spmd.clone.sunk | while | flops 201981952 | bytes 4196459 | solution.py:44
  362.3 204.1 %while.97 = (s32[]{:T(128)}, f32[8,128,128]{2,1,0:T(8,128)}, f32[2,64,8,128]{3,1,2,0:T(8,128)}, f32[2,8,128,128]{3,2,1,0:T(8,128)}, f32[2,128,8]{2,1,0:T(8,128)S...) while((s32[]{:T(128)}, f32[8,128,128]{2,1,0:T(8,128)}, ...), condition=%wide.region_14.16_spmd.clone, body=%wide.region_11.15_spmd.clone.sunk | while | flops 1110032640 | bytes 34474176 | solution.py:131
  372.0 80.0 %custom-call.29 = f32[8,1,128,128]{2,3,1,0:T(8,128)} custom-call(f32[8,1,128,128]{3,2,1,0:T(8,128)} %fusion.498), custom_call_target="InvertDiagBlocksLowerTriangular" | custom-call | tf_op jit(solution)/shard_map/jvp()/while/body/eval_jaxpr/vmap(jit(_solve_triangular))/triangular_solve/custom-call.0 | solution.py:76
  474.0 80.0 %custom-call.29 = f32[8,1,128,128]{2,3,1,0:T(8,128)} custom-call(f32[8,1,128,128]{3,2,1,0:T(8,128)} %fusion.498), custom_call_target="InvertDiagBlocksLowerTriangular" | custom-call | tf_op jit(solution)/shard_map/jvp()/while/body/eval_jaxpr/vmap(jit(_solve_triangular))/triangular_solve/custom-call.0 | solution.py:76
  574.6 6.6 fusion.224
  584.6 9.9 multiply_reduce_fusion.11
  598.6 191.9 %while.99 = (s32[]{:T(128)}, f32[8,128,128]{2,1,0:T(8,128)}, f32[2,64,8,128]{3,1,2,0:T(8,128)}, f32[2,128,8,128]{3,1,2,0:T(8,128)S(1)}, f32[2,128,8]{1,2,0:T(8,1...) while((s32[]{:T(128)}, f32[8,128,128]{2,1,0:T(8,128)}, ...), condition=%wide.region_22.25_spmd.clone, body=%wide.region_19.24_spmd.clone.sunk | while | flops 1110360320 | bytes 17712480 | solution.py:131
  606.9 79.2 %custom-call.30 = f32[8,1,128,128]{2,3,1,0:T(8,128)} custom-call(f32[8,1,128,128]{3,2,1,0:T(8,128)S(1)} %fusion.523), custom_call_target="InvertDiagBlocksLowerTriangular" | custom-call | tf_op jit(solution)/shard_map/transpose(jvp())/while/body/eval_jaxpr/checkpoint/vmap(jit(_solve_triangular))/triangular_solve/custom-call.2 | solution.py:76
  703.1 79.2 %custom-call.30 = f32[8,1,128,128]{2,3,1,0:T(8,128)} custom-call(f32[8,1,128,128]{3,2,1,0:T(8,128)S(1)} %fusion.523), custom_call_target="InvertDiagBlocksLowerTriangular" | custom-call | tf_op jit(solution)/shard_map/transpose(jvp())/while/body/eval_jaxpr/checkpoint/vmap(jit(_solve_triangular))/triangular_solve/custom-call.2 | solution.py:76
  794.7 25.7 %all-gather.13.cloned.1.call-done = bf16[64,128,128]{2,1,0:T(8,128)(2,1)} async-done(((bf16[8,128,128]{2,1,0:T(8,128)(2,1)}), bf16[64,128,128]{2,1,0:T(8,128)(2,1)}) %all-gather.13.cloned.1.call-update) | async-done | bytes 2097168 | tf_op jit(solution)/shard_map/all_gather | solution.py:50
  820.4 21.6 while.100
  846.4 274.3 %while.96 = (s32[]{:T(128)}, f32[8,128,128]{2,1,0:T(8,128)S(1)}, f32[2,64,8,128]{3,2,1,0:T(8,128)}, f32[2,128,8,128]{3,2,1,0:T(8,128)}, f32[2,128,8,128]{3,2,1,0...) while((s32[]{:T(128)}, f32[8,128,128]{2,1,0:T(8,128)S(1)}, ...), condition=%wide.region_36.39_spmd, body=%wide.region_25.38_spmd.sunk | while | flops 3230909184 | bytes 103531600 | solution.py:131
  864.6 80.0 %custom-call.28 = f32[8,1,128,128]{2,3,1,0:T(8,128)} custom-call(f32[8,1,128,128]{3,2,1,0:T(8,128)} %get-tuple-element.1767), custom_call_target="InvertDiagBlocksLowerTriangular" | custom-call | tf_op jit(solution)/shard_map/transpose(jvp())/while/body/eval_jaxpr/checkpoint/vmap(jit(_solve_triangular))/triangular_solve/custom-call.2 | solution.py:76
  955.8 5.1 pad.165
  1001.5 80.0 %custom-call.28 = f32[8,1,128,128]{2,3,1,0:T(8,128)} custom-call(f32[8,1,128,128]{3,2,1,0:T(8,128)} %get-tuple-element.1767), custom_call_target="InvertDiagBlocksLowerTriangular" | custom-call | tf_op jit(solution)/shard_map/transpose(jvp())/while/body/eval_jaxpr/checkpoint/vmap(jit(_solve_triangular))/triangular_solve/custom-call.2 | solution.py:76
  1092.7 5.1 pad.165
  1144.1 6.0 fusion.191
  1158.5 10.6 fusion.174
  1170.7 11.1 fusion.195
  1187.9 9.1 fusion.176
  1197.1 42.2 %all-reduce.23 = (f32[1024]{0:T(1024)}, f32[8]{0:T(128)}, f32[8]{0:T(128)}, f32[128]{0:T(128)}, f32[1024]{0:T(1024)}) all-reduce(f32[1024]{0:T(1024)S(1)} %get-tuple-element.1251, f32[8]{0:T(128)S(1)} %get-tuple-element.1361, f32[8]{0:T(128)S(1)} %neg.70, ...), channel_id=1, replica_groups=mesh['seq'=8,'stream'=4] {'seq','stream'}, use_global_device_ids=true, to_apply=%region_40.43 | all-reduce | flops 2192 | bytes 17536 | tf_op jit(solution)/shard_map/psum | solution.py:337
  1240.3 22.5 all-reduce.27.cloned.1.call-done
  1262.8 152.3 %reduce-scatter.7.cloned.1.call-done = f32[32,1024]{1,0:T(8,128)} async-done(((f32[1024,1024]{1,0:T(8,128)}), f32[32,1024]{1,0:T(8,128)}) %reduce-scatter.7.cloned.1.call-update) | async-done | bytes 131088 | tf_op jit(solution)/shard_map/reduce_scatter | solution.py:333
  1415.1 252.9 %reduce-scatter.11.cloned.1.call-done = f32[88,1024]{1,0:T(8,128)} async-done(((f32[2816,1024]{1,0:T(8,128)}), f32[88,1024]{1,0:T(8,128)}) %reduce-scatter.11.cloned.1.call-update) | async-done | bytes 360464 | tf_op jit(solution)/shard_map/reduce_scatter | solution.py:335
  1668.0 249.9 %reduce-scatter.5.cloned.1.call-done = f32[32,6144]{1,0:T(8,128)} async-done(((f32[1024,6144]{1,0:T(8,128)}), f32[32,6144]{1,0:T(8,128)}) %reduce-scatter.5.cloned.1.call-update) | async-done | bytes 786448 | tf_op jit(solution)/shard_map/reduce_scatter | solution.py:332
  1917.9 497.0 %reduce-scatter.9.cloned.1.call-done = f32[32,5632]{1,0:T(8,128)} async-done(((f32[1024,5632]{1,0:T(8,128)}), f32[32,5632]{1,0:T(8,128)}) %reduce-scatter.9.cloned.1.call-update) | async-done | bytes 720912 | tf_op jit(solution)/shard_map/reduce_scatter | solution.py:334
  (856 shorter events, 403.4 us)
Async XLA Ops:
  7.2 566.7 %copy-start = (bf16[1024,1024]{1,0:T(8,128)(2,1)S(1)}, bf16[1024,1024]{1,0:T(8,128)(2,1)}, u32[]{:S(2)}) copy-start(bf16[1024,1024]{1,0:T(8,128)(2,1)} %param.40) | copy-start | bytes 6291460
  7.2 272.0 %all-gather.9.cloned.1.call-start = ((), (), s32[]{:S(2)}) async-start(), calls=%async_computation.5 | async-start | bytes 2359296 | tf_op jit(solution)/shard_map/all_gather | solution.py:27
  9.0 12.6 copy-start.110
  9.0 12.1 copy-start.133
  9.0 12.2 copy-start.134
  9.0 12.6 copy-start.42
  9.0 12.6 copy-start.80
  9.1 12.6 copy-start.96
  9.1 13.1 copy-start.98
  9.1 13.8 copy-start.124
  17.5 11.6 collective-permute-start
  249.2 60.4 %all-gather.7.cloned.1.call-start = ((), (), s32[]{:S(2)}) async-start(), calls=%async_computation.4 | async-start | bytes 2359296 | tf_op jit(solution)/shard_map/all_gather | solution.py:27
  249.9 544.8 %all-gather.11.cloned.1.call-start = ((), (), s32[]{:S(2)}) async-start(), calls=%async_computation.10 | async-start | bytes 2359296 | tf_op jit(solution)/shard_map/all_gather | solution.py:50
  258.0 562.3 %all-gather.13.cloned.1.call-start = ((), (), s32[]{:S(2)}) async-start(), calls=%async_computation.11 | async-start | bytes 2359296 | tf_op jit(solution)/shard_map/all_gather | solution.py:50
  574.4 20.1 copy-start.23
  574.6 19.9 copy-start.108
  792.3 470.5 %all-reduce.27.cloned.1.call-start = ((), (), s32[]{:S(2)}) async-start(), calls=%async_computation.12 | async-start | bytes 360448 | tf_op jit(solution)/shard_map/psum | solution.py:337
  846.6 11.6 copy-start.2
  848.1 15.2 copy-start.65
  863.3 83.1 %copy-start.7 = (f32[8,128,128]{2,1,0:T(8,128)}, f32[8,128,128]{2,1,0:T(8,128)S(1)}, u32[]{:S(2)}) copy-start(f32[8,128,128]{2,1,0:T(8,128)S(1)} %fusion.466) | copy-start | bytes 1572868 | tf_op jit(solution)/shard_map/transpose(jvp())/while
  946.5 16.9 copy-start.12
  983.5 11.6 copy-start.2
  985.0 15.2 copy-start.65
  1000.2 83.1 %copy-start.7 = (f32[8,128,128]{2,1,0:T(8,128)}, f32[8,128,128]{2,1,0:T(8,128)S(1)}, u32[]{:S(2)}) copy-start(f32[8,128,128]{2,1,0:T(8,128)S(1)} %fusion.466) | copy-start | bytes 1572868 | tf_op jit(solution)/shard_map/transpose(jvp())/while
  1083.3 16.9 copy-start.12
  1140.0 275.1 %reduce-scatter.7.cloned.1.call-start = ((), (), s32[]{:S(2)}) async-start(), calls=%async_computation.7 | async-start | bytes 4325376 | tf_op jit(solution)/shard_map/reduce_scatter | solution.py:333
  1142.9 525.1 %reduce-scatter.11.cloned.1.call-start = ((), (), s32[]{:S(2)}) async-start(), calls=%async_computation.9 | async-start | bytes 11894784 | tf_op jit(solution)/shard_map/reduce_scatter | solution.py:335
  1150.1 767.9 %reduce-scatter.5.cloned.1.call-start = ((), (), s32[]{:S(2)}) async-start(), calls=%async_computation.6 | async-start | bytes 25952256 | tf_op jit(solution)/shard_map/reduce_scatter | solution.py:332
  1155.2 3.2 collective-permute-start.1
  1169.2 1245.8 %reduce-scatter.9.cloned.1.call-start = ((), (), s32[]{:S(2)}) async-start(), calls=%async_computation.8 | async-start | bytes 23789568 | tf_op jit(solution)/shard_map/reduce_scatter | solution.py:334
  1187.9 51.4 %copy-start.132 = (f32[128]{0:T(128)S(1)}, f32[128]{0:T(128)}, u32[]{:S(2)}) copy-start(f32[128]{0:T(128)} %copy-done.131) | copy-start | bytes 1540
  1187.9 1230.1 %copy-start.1 = (bf16[1024,1024]{1,0:T(8,128)(2,1)S(1)}, bf16[1024,1024]{1,0:T(8,128)(2,1)}, u32[]{:S(2)}) copy-start(bf16[1024,1024]{1,0:T(8,128)(2,1)} %param.40) | copy-start | bytes 6291460
  (168 other events, 627.3 us)
Sparse Core Ops, SparseCore 0:
  249.3 29.8 all-gather.8
  281.6 27.8 all-gather.6
  311.5 27.8 all-gather.10
  792.4 27.8 all-gather.12
  1140.2 122.5 all-reduce.26
  1265.5 149.5 reduce-scatter.6
  1418.0 250.0 reduce-scatter.10
  1675.0 242.8 reduce-scatter.4
  1920.9 493.9 reduce-scatter.8
where the time goes:
time: 2430 us; the launch traced here: 2420 us
  waiting for transfers between devices  1250 us (51%)
  other arithmetic  693 us (29%)
  matrix products  233 us (10%)
  local copies, waits for them, and re-layouts  179 us (7%)
  blocking collectives  42.2 us (2%)
    another operation x28, other arithmetic, solve_lower(): jax.scipy.linalg.solve_triangular(matrix, target, lower=True, unit_diagon...  642 us
    reduce_scatter x1, waiting for transfers between devices, on_device(): lax.psum_scatter(grad_gate_up, ('seq', 'stream'), scatter_dimension=0, ti...  497 us
    reduce_scatter x1, waiting for transfers between devices, on_device(): lax.psum_scatter(grad_down, ('seq', 'stream'), scatter_dimension=0, tiled...  253 us
    reduce_scatter x1, waiting for transfers between devices, on_device(): lax.psum_scatter(grad_in_weight, ('seq', 'stream'), scatter_dimension=0,...  250 us
    reduce_scatter x1, waiting for transfers between devices, on_device(): lax.psum_scatter(grad_out_weight, ('seq', 'stream'), scatter_dimension=0,...  152 us
    all_gather x2, waiting for transfers between devices, carried_in(): lax.all_gather(part.astype(kind), axis)  51 us
  transfers between devices with their start and end apart: 11, of which 9 were waited for; matrix products, arithmetic and copies ran while one was open for 23% of the time, Pallas kernels for 0%

commit v1 on v0

v1 whole, which is shorter than its diff:
```python
import functools

import jax
import jax.numpy as jnp
from jax import lax
from jax.experimental import pallas as pl
from jax.experimental.pallas import tpu as pltpu
from jax.sharding import PartitionSpec as P

D = 1024
H = 8
HD = 128
FF = 2816
NH = 2
CONV = 4
GROUPS = 2 + 2 * NH
MIXED = GROUPS - 1
DOCS = 8
EPS = 1e-06

f32 = jnp.float32
bf16 = jnp.bfloat16


def dot(a, b, dims):
    return lax.dot_general(
        a.astype(bf16), b.astype(bf16), ((dims[:1], dims[1:]), ((), ())), preferred_element_type=f32
    )


def nn(a, b):
    return dot(a, b, (1, 0))


def nt(a, b):
    return dot(a, b, (1, 1))


def tn(a, b):
    return dot(a, b, (0, 0))


def halves(x):
    high = x.astype(bf16)
    return high, (x - high.astype(f32)).astype(bf16)


def nt_fine(a, b):
    (a_high, a_low), (b_high, b_low) = halves(a), halves(b)
    return nt(a_high, b_high) + (nt(a_high, b_low) + nt(a_low, b_high))


def nn_exact(ones, x):
    high, low = halves(x)
    lowest = (x - high.astype(f32) - low.astype(f32)).astype(bf16)
    return nn(ones, high) + (nn(ones, low) + nn(ones, lowest))


def sigmoid(x):
    return 1.0 / (1.0 + jnp.exp(-x))


def softplus(x):
    return jnp.maximum(x, 0.0) + jnp.log(1.0 + jnp.exp(-jnp.abs(x)))


def doc_at(starts, positions):
    total = jnp.full(positions.shape, -1, jnp.int32)
    for start in starts:
        total = total + (start <= positions).astype(jnp.int32)
    return total


def doc_starts(lengths_ref):
    starts, at = [], jnp.int32(0)
    for j in range(DOCS):
        starts.append(at)
        at = at + lengths_ref[0, j]
    return starts


def stack2(a, b):
    return jnp.concatenate([a, b], axis=0)


def beside(a, b):
    return jnp.concatenate([a, b], axis=1)


def quad(a, b, c, d):
    return stack2(beside(a, b), beside(c, d))


def conv_of(block, taps, docs, T):
    total = block[8:] * taps[CONV - 1 : CONV]
    for lag in range(1, CONV):
        same = (docs[0] == docs[lag]).astype(f32)
        total = total + block[8 - lag : 8 - lag + T] * (taps[CONV - 1 - lag : CONV - lag] * same)
    return total


def chunk_gates(raw, consts, starts, first, T):
    lane = lax.broadcasted_iota(jnp.int32, (T, HD), 1)
    row = lax.broadcasted_iota(jnp.int32, (T, HD), 0)
    logits = raw + (pltpu.roll(raw, HD - 3, 1) + pltpu.roll(raw, HD - 6, 1))
    bias, rate = consts[0:1], consts[1:2]
    shifted = logits + bias
    gate = -rate * softplus(shifted)
    lower = (lax.broadcasted_iota(jnp.int32, (T, T), 1) <= lax.broadcasted_iota(jnp.int32, (T, T), 0))
    cumul = nn_exact(lower.astype(bf16), jnp.where(lane == 2, gate, 0.0))
    beta = 2.0 * sigmoid(logits)
    b0, b1 = beta[:, 0:1], beta[:, 1:2]
    g = cumul[:, 2:3]
    g_row = jnp.transpose(cumul)[2:3, :]
    g_last = cumul[T - 1 : T, 2:3]
    position = first + row[:, 0:1]
    docs = [doc_at(starts, position - lag) for lag in range(CONV)]
    doc = docs[0]
    doc_row = doc_at(starts, first + lax.broadcasted_iota(jnp.int32, (1, T), 1))
    doc_before = doc_at(starts, jnp.full((1, 1), first - 1, jnp.int32))
    doc_last = doc_at(starts, jnp.full((1, 1), first + (T - 1), jnp.int32))
    joined = lower & (doc == doc_row)
    decay = jnp.where(joined, jnp.exp(jnp.where(joined, g - g_row, 0.0)), 0.0)
    place_i = lax.broadcasted_iota(jnp.int32, (T, T), 0)
    place_j = lax.broadcasted_iota(jnp.int32, (T, T), 1)
    strict = jnp.where(place_i == place_j, 0.0, decay)
    from_start = jnp.exp(g) * (doc == doc_before).astype(f32)
    to_end = jnp.exp(jnp.minimum(g_last - g, 0.0)) * (doc == doc_last).astype(f32)
    whole = jnp.exp(g_last) * (doc_last == doc_before).astype(f32)
    return dict(
        logits=logits, shifted=shifted, gate=gate, beta=beta, b=stack2(b0, b1), docs=docs,
        decay=decay, decays=quad(strict, strict, decay, strict), hd=from_start,
        hd2=stack2(from_start, from_start), to_end=stack2(to_end, to_end), whole=whole,
    )


def key_scale(raw):
    return lax.rsqrt(jnp.sum(raw * raw, axis=-1, keepdims=True) + EPS)


def chunk_inputs(block, taps, docs, T):
    conv = conv_of(block, taps, docs, T)
    sig = sigmoid(conv)
    active = conv * sig
    cut = [active[:, i * HD : (i + 1) * HD] for i in range(MIXED)]
    scales = (key_scale(cut[1]), key_scale(cut[2]))
    keys = stack2(cut[1] * scales[0], cut[2] * scales[1])
    values = stack2(cut[3], cut[4])
    return conv, sig, cut[0], keys, values, stack2(*scales)


def inverses(lowers, T):
    size = NH * T
    row = lax.broadcasted_iota(jnp.int32, (size, size), 0)
    col = lax.broadcasted_iota(jnp.int32, (size, size), 1)
    token_i, token_j = row & (T - 1), col & (T - 1)
    differ = token_i ^ token_j
    eye = (row == col).astype(f32)
    found = [jnp.where(row == col, 1.0, jnp.where(differ == 0, -a, 0.0)) for a in lowers]
    step = 1
    while step < T:
        level = (differ >= step) & (differ < 2 * step)
        parts = [nn(jnp.where(level, a, 0.0), x) for a, x in zip(lowers, found)]
        found = [x - nn(x, part) for x, part in zip(found, parts)]
        step *= 2
    a_cut = [halves(a) for a in lowers]
    x_cut = [halves(x) for x in found]
    errors = [
        eye - x - (nn(a[0], xc[0]) + (nn(a[0], xc[1]) + nn(a[1], xc[0])))
        for a, x, xc in zip(a_cut, found, x_cut)
    ]
    return [x + nn(xc[0], e) for x, xc, e in zip(found, x_cut, errors)]


def head_gate(mixed, raw, gain):
    scale = lax.rsqrt(jnp.mean(mixed * mixed, axis=-1, keepdims=True) + EPS)
    return mixed * scale, scale, sigmoid(raw)


def forward_kernel(T, per, lengths, proj, small, taps_ref, consts, gain, gated, mixed_out, states, news, invs,
                   xbuf, ubuf, wbuf, qbuf, pbuf, dbuf, gates):
    count = proj.shape[0] // T
    width = MIXED * HD
    starts = doc_starts(lengths)
    taps = taps_ref[...]
    xbuf[0:8, :] = jnp.zeros((8, width), f32)

    def fill(c, _):
        xbuf[pl.ds(pl.multiple_of(8 + c * T, 8), T), :] = proj[pl.ds(pl.multiple_of(c * T, T), T), :width].astype(f32)
        return 0

    lax.fori_loop(0, count, fill, 0)

    def intra(turn, _):
        kept, lowers = [], []
        for i in range(per):
            c = turn * per + i
            first = pl.multiple_of(c * T, T)
            gate = chunk_gates(small[pl.ds(first, T), :], consts, starts, first, T)
            block = xbuf[pl.ds(first, T + 8), :]
            conv, sig, query, keys, values, scales = chunk_inputs(block, taps, gate["docs"], T)
            keys_low = keys.astype(bf16)
            lowers.append(gate["b"] * (nt(keys_low, keys_low) * gate["decays"]))
            kept.append((c, first, gate, query, keys, keys_low, values))
        found = inverses(lowers, T)
        for (c, first, gate, query, keys, keys_low, values), inverse in zip(kept, found):
            two = pl.multiple_of(c * (NH * T), NH * T)
            low = inverse.astype(bf16)
            invs[c] = low
            right = gate["b"] * beside(values, gate["hd2"] * keys)
            both = nn(low, right)
            ubuf[pl.ds(two, NH * T), :] = both[:, :HD]
            wbuf[pl.ds(two, NH * T), :] = both[:, HD:].astype(bf16)
            query_low = query.astype(bf16)
            qbuf[pl.ds(first, T), :] = query_low
            pbuf[pl.ds(first, T), :] = (nt_fine(query, keys) * beside(gate["decay"], gate["decay"])).astype(bf16)
            dbuf[pl.ds(two, NH * T), :] = (gate["to_end"] * keys).astype(bf16)
            lane = lax.broadcasted_iota(jnp.int32, (T, HD), 1)
            gates[pl.ds(first, T), :] = jnp.where(lane == 0, gate["hd"], gate["whole"])
        return 0

    lax.fori_loop(0, count // per, intra, 0)

    def across(c, state):
        first = pl.multiple_of(c * T, T)
        two = pl.multiple_of(c * (NH * T), NH * T)
        state_low = state.astype(bf16)
        states[c] = state_low
        new = ubuf[pl.ds(two, NH * T), :] - nn(wbuf[pl.ds(two, NH * T), :], state_low)
        new_low = new.astype(bf16)
        news[pl.ds(two, NH * T), :] = new_low
        gate = gates[pl.ds(first, T), :]
        mixed = gate[:, 0:1] * nn(qbuf[pl.ds(first, T), :], state_low) + nn(pbuf[pl.ds(first, T), :], new_low)
        mixed_out[pl.ds(first, T), :] = mixed
        raw = proj[pl.ds(first, T), width:].astype(f32)
        normal, _, sig = head_gate(mixed, raw, None)
        gated[pl.ds(first, T), :] = ((normal * gain[0:1]) * (raw * sig)).astype(bf16)
        return gate[0:1, 1:2] * state + tn(dbuf[pl.ds(two, NH * T), :], new_low)

    lax.fori_loop(0, count, across, jnp.zeros((HD, HD), f32))


def backward_kernel(T, lengths, proj, small, taps_ref, consts, gain, mixed_in, states, news, invs, grad_gated,
                    gp, gconv_w, sums, xbuf, gbuf):
    count = proj.shape[0] // T
    width = MIXED * HD
    starts = doc_starts(lengths)
    taps = taps_ref[...]
    xbuf[0:8, :] = jnp.zeros((8, width), f32)
    gbuf[...] = jnp.zeros((8, width), f32)

    def fill(c, _):
        xbuf[pl.ds(pl.multiple_of(8 + c * T, 8), T), :] = proj[pl.ds(pl.multiple_of(c * T, T), T), :width].astype(f32)
        return 0

    lax.fori_loop(0, count, fill, 0)
    lane = lax.broadcasted_iota(jnp.int32, (T, HD), 1)
    place_i = lax.broadcasted_iota(jnp.int32, (T, T), 0)
    place_j = lax.broadcasted_iota(jnp.int32, (T, T), 1)
    upper = (place_j >= place_i).astype(bf16)
    under = (place_j < place_i)

    def turn(k, carry):
        state_grad, gain_grad, gate_sums = carry
        c = count - 1 - k
        first = pl.multiple_of(c * T, T)
        two = pl.multiple_of(c * (NH * T), NH * T)
        gate = chunk_gates(small[pl.ds(first, T), :], consts, starts, first, T)
        block = xbuf[pl.ds(first, T + 8), :]
        conv, sig, query, keys, values, scales = chunk_inputs(block, taps, gate["docs"], T)
        keys_low, query_low = keys.astype(bf16), query.astype(bf16)
        b, hd, hd2, to_end = gate["b"], gate["hd"], gate["hd2"], gate["to_end"]
        decay2 = beside(gate["decay"], gate["decay"])
        pairs = nt(keys_low, keys_low) * gate["decays"]
        scores = nt_fine(query, keys) * decay2
        state = states[c]
        new = news[pl.ds(two, NH * T), :]
        inverse = invs[c]
        mixed = mixed_in[pl.ds(first, T), :]
        raw = proj[pl.ds(first, T), width:].astype(f32)
        normal, scale, zsig = head_gate(mixed, raw, None)
        incoming = grad_gated[pl.ds(first, T), :]
        passed = incoming * (raw * zsig)
        gain_grad = gain_grad + jnp.sum(passed * normal, axis=0, keepdims=True)
        grad_z = incoming * (normal * gain[0:1]) * (zsig * (1.0 + raw * (1.0 - zsig)))
        e = passed * gain[0:1]
        grad_mixed = scale * (e - normal * jnp.mean(e * normal, axis=-1, keepdims=True))
        gm = grad_mixed.astype(bf16)
        ended = (to_end * keys).astype(bf16)
        grad_low = state_grad.astype(bf16)
        grad_new = tn(scores, gm) + nn(ended, grad_low)
        grad_right = tn(inverse, grad_new)
        moved = b * grad_right
        next_grad = gate["whole"] * state_grad + tn(hd * query, gm) - tn(hd2 * keys, moved)
        grad_right_low, moved_low = grad_right.astype(bf16), moved.astype(bf16)
        grad_ended = nt(new, grad_low)
        grad_scores = nt(gm, new)
        grad_lower = jnp.where(gate["decays"] != 0.0, -nt(grad_right_low, new), 0.0)
        from_grad = nt(gm, state)
        scored = grad_scores * decay2
        grad_query = hd * from_grad + nn(scored, keys_low)
        paired = (b * grad_lower) * gate["decays"]
        keyed = nn(keys_low, state)
        grad_keys = (
            tn(scored, query_low) + to_end * grad_ended - hd2 * nt(moved_low, state)
            + nn(paired, keys_low) + tn(paired, keys_low)
        )
        lower_pairs = grad_lower * pairs
        grad_b = jnp.sum(grad_right * (values - hd2 * keyed), axis=-1, keepdims=True) + jnp.sum(
            lower_pairs, axis=-1, keepdims=True
        )
        four = b * lower_pairs
        both = grad_scores * scores
        joint = (four[:T, :T] + four[:T, T:]) + (four[T:, :T] + four[T:, T:]) + (both[:, :T] + both[:, T:])
        crossing = jnp.sum(jnp.where(under, nn_exact(upper, joint), 0.0), axis=-1, keepdims=True)
        start_part = -hd2 * jnp.sum(moved * keyed, axis=-1, keepdims=True)
        start_part = start_part[:T] + start_part[T:] + hd * jnp.sum(query * from_grad, axis=-1, keepdims=True)
        end_part = to_end * jnp.sum(grad_ended * keys, axis=-1, keepdims=True)
        end_part = end_part[:T] + end_part[T:]
        sums_in = jnp.where(lane == 0, start_part, jnp.where(lane == 1, end_part, 0.0))
        after = nn_exact(upper, sums_in)
        before = nn_exact(under.astype(bf16), sums_in)
        whole_part = gate["whole"] * jnp.sum(state_grad * state.astype(f32), keepdims=True)
        grad_gate = crossing + after[:, 0:1] + before[:, 1:2] + whole_part
        beta = gate["beta"]
        grad_beta = jnp.where(lane == 0, grad_b[:T], grad_b[T:]) * (beta * (1.0 - 0.5 * beta))
        grad_decay = -grad_gate * consts[1:2] * sigmoid(gate["shifted"])
        grad_small = jnp.where(lane < 2, grad_beta, jnp.where(lane == 2, grad_decay, 0.0))
        gate_sums = gate_sums + stack2(
            jnp.sum(grad_small, axis=0, keepdims=True),
            jnp.sum(jnp.where(lane == 2, grad_gate * -softplus(gate["shifted"]), 0.0), axis=0, keepdims=True),
        )
        high, low = halves(grad_small)
        gp[pl.ds(first, T), GROUPS * HD :] = (high.astype(f32) + pltpu.roll(low.astype(f32), 3, 1)).astype(bf16)
        gp[pl.ds(first, T), width : GROUPS * HD] = grad_z.astype(bf16)
        projected_out = jnp.sum(keys * grad_keys, axis=-1, keepdims=True)
        grad_raw = (grad_keys - keys * projected_out) * scales
        slope = sig * (1.0 + conv * (1.0 - sig))
        grad_active = jnp.concatenate([grad_query, grad_raw[:T], grad_raw[T:], moved[:T], moved[T:]], axis=1)
        grad_conv = grad_active * slope
        after_block = stack2(grad_conv, gbuf[...])
        gbuf[...] = grad_conv[:8]
        position = first + lax.broadcasted_iota(jnp.int32, (T, 1), 0)
        total = grad_conv * taps[CONV - 1 : CONV]
        taps_grads = [None] * CONV
        taps_grads[CONV - 1] = jnp.sum(grad_conv * block[8:], axis=0, keepdims=True)
        for lag in range(1, CONV):
            same = (doc_at(starts, position + lag) == gate["docs"][0]).astype(f32)
            total = total + after_block[lag : lag + T] * (taps[CONV - 1 - lag : CONV - lag] * same)
            same = (gate["docs"][lag] == gate["docs"][0]).astype(f32)
            taps_grads[CONV - 1 - lag] = jnp.sum(
                grad_conv * (block[8 - lag : 8 - lag + T] * same), axis=0, keepdims=True
            )
        gp[pl.ds(first, T), :width] = total.astype(bf16)
        gconv_w[...] += jnp.concatenate(taps_grads, axis=0)
        return next_grad, gain_grad, gate_sums

    gconv_w[...] = jnp.zeros(gconv_w.shape, f32)
    _, gain_grad, gate_sums = lax.fori_loop(
        0, count, turn, (jnp.zeros((HD, HD), f32), jnp.zeros((1, HD), f32), jnp.zeros((2, HD), f32))
    )
    sums[...] = jnp.concatenate([gain_grad, gate_sums, jnp.zeros((5, HD), f32)], axis=0)


VMEM = pl.BlockSpec(memory_space=pltpu.VMEM)
SMEM = pl.BlockSpec(memory_space=pltpu.SMEM)
LIMIT = 56 * 1024 * 1024


def run_forward(T, lengths, proj, small, taps, consts, gain):
    rows = proj.shape[0]
    count = rows // T
    shape = jax.ShapeDtypeStruct
    return pl.pallas_call(
        functools.partial(forward_kernel, T, 4 if count % 4 == 0 else 1),
        out_shape=(
            shape((rows, HD), bf16), shape((rows, HD), f32), shape((count, HD, HD), bf16),
            shape((NH * rows, HD), bf16), shape((count, NH * T, NH * T), bf16),
        ),
        in_specs=[SMEM] + [VMEM] * 5,
        out_specs=[VMEM] * 5,
        scratch_shapes=[
            pltpu.VMEM((rows + 8, MIXED * HD), f32), pltpu.VMEM((NH * rows, HD), f32),
            pltpu.VMEM((NH * rows, HD), bf16), pltpu.VMEM((rows, HD), bf16), pltpu.VMEM((rows, NH * T), bf16),
            pltpu.VMEM((NH * rows, HD), bf16), pltpu.VMEM((rows, HD), f32),
        ],
        compiler_params=pltpu.CompilerParams(vmem_limit_bytes=LIMIT),
        name="mixer_forward",
    )(lengths, proj, small, taps, consts, gain)


def run_backward(T, lengths, proj, small, taps, consts, gain, mixed, states, news, invs, grad_gated):
    rows = proj.shape[0]
    shape = jax.ShapeDtypeStruct
    return pl.pallas_call(
        functools.partial(backward_kernel, T),
        out_shape=(
            shape((rows, (GROUPS + 1) * HD), bf16), shape((CONV, MIXED * HD), f32), shape((8, HD), f32),
        ),
        in_specs=[SMEM] + [VMEM] * 10,
        out_specs=[VMEM] * 3,
        scratch_shapes=[
            pltpu.VMEM((rows + 8, MIXED * HD), f32), pltpu.VMEM((8, MIXED * HD), f32),
        ],
        compiler_params=pltpu.CompilerParams(vmem_limit_bytes=LIMIT),
        name="mixer_backward",
    )(lengths, proj, small, taps, consts, gain, mixed, states, news, invs, grad_gated)


def norm_scale(values):
    return lax.rsqrt(jnp.mean(values * values, axis=-1, keepdims=True) + EPS)


def norm_back(values, scale, gain, grad):
    normal = values * scale
    e = grad * gain
    return scale * (e - normal * jnp.mean(e * normal, axis=-1, keepdims=True)), jnp.sum(grad * normal, axis=0)


def take(array, start, size, axis):
    return lax.dynamic_slice_in_dim(array, start, size, axis)


def mm(a, b, dims="ij,jk->ik"):
    return jnp.einsum(dims, a, b, preferred_element_type=f32)


def on_device(tokens, grad_out, doc_lengths, gain_in, in_weight, small_weight, gate_bias, decay_rate, conv_weight,
              gain_head, out_weight, gain_mid, gate_up_weight, down_weight):
    seq, stream = lax.axis_size("seq"), lax.axis_size("stream")
    s = lax.axis_index("seq")
    rep = max(1, seq // H)
    head, part = s // rep, s % rep
    T = tokens.shape[1]
    rows = D // seq
    piece = D // (seq * stream)
    shard = FF // seq

    values = tokens[0].astype(f32)
    scale_in = norm_scale(values)
    normed = (values * scale_in * gain_in).astype(bf16)
    normed_all = lax.all_gather(normed, "seq", tiled=True)
    out_all = lax.all_gather(grad_out[0], "seq", tiled=True)

    w_head = take(in_weight.reshape(D, GROUPS, H, HD), head, 1, 2).reshape(D, GROUPS * HD)
    s_head = take(small_weight.reshape(D, NH + 1, H), head, 1, 2).reshape(D, NH + 1)
    s_high, s_low = halves(s_head)
    s_lowest = (s_head - s_high.astype(f32) - s_low.astype(f32)).astype(bf16)
    s_wide = jnp.pad(jnp.concatenate([s_high, s_low, s_lowest], axis=1), ((0, 0), (0, HD - 3 * (NH + 1))))
    taps = take(conv_weight.reshape(CONV, MIXED, H, HD), head, 1, 2).reshape(CONV, MIXED * HD)
    consts = jnp.zeros((8, HD), f32).at[0, 2].set(gate_bias[head]).at[1, 2].set(decay_rate[head])
    gain = gain_head.reshape(1, HD)

    proj = mm(normed_all, w_head).astype(bf16)
    small = mm(normed_all, s_wide)
    gated_h, mixed, states, news, invs = run_forward(T, doc_lengths, proj, small, taps, consts, gain)

    gated = lax.all_to_all(gated_h.reshape(seq, T, HD), "seq", 0, 0)[::rep]
    gated = jnp.transpose(gated, (1, 0, 2)).reshape(T, D)
    residual = values + mm(gated, out_weight)
    scale_mid = norm_scale(residual)
    normed_mid = (residual * scale_mid * gain_mid).astype(bf16)
    mid_all = lax.all_gather(normed_mid, "seq", tiled=True)

    def feed(rows_in, cotangent, w_gate, w_up, w_down):
        gate, up = mm(rows_in, w_gate), mm(rows_in, w_up)
        sig = jax.nn.sigmoid(gate)
        hidden = (gate * sig * up).astype(bf16)
        grad_hidden = mm(cotangent, w_down, "ij,kj->ik")
        grad_gate = (grad_hidden * up * (sig * (1.0 + gate * (1.0 - sig)))).astype(bf16)
        return hidden, grad_gate, (grad_hidden * (gate * sig)).astype(bf16)

    hidden, g_gate, g_up = feed(normed_mid, grad_out[0], gate_up_weight[:, :FF], gate_up_weight[:, FF:], down_weight)
    result = (residual + mm(hidden, down_weight)).astype(bf16)
    grad_mid = mm(g_gate, gate_up_weight[:, :FF], "ij,kj->ik") + mm(g_up, gate_up_weight[:, FF:], "ij,kj->ik")
    back_mid, grad_gain_mid = norm_back(residual, scale_mid, gain_mid, grad_mid)
    grad_residual = grad_out[0].astype(f32) + back_mid
    low_all = lax.all_gather(grad_residual.astype(bf16), "seq", tiled=True)

    at = s * shard
    w_down = take(down_weight, at, shard, 0)
    hidden_s, g_gate_s, g_up_s = feed(
        mid_all, out_all, take(gate_up_weight, at, shard, 1), take(gate_up_weight, FF + at, shard, 1), w_down
    )
    grad_down = lax.psum_scatter(
        mm(hidden_s, out_all, "ji,jk->ik").astype(bf16), "stream", scatter_dimension=0, tiled=True
    )
    up_part = jnp.stack([mm(mid_all, g_gate_s, "ji,jk->ik"), mm(mid_all, g_up_s, "ji,jk->ik")], axis=1).astype(bf16)
    up_part = jnp.swapaxes(up_part.reshape(seq, stream, piece, 2 * shard), 0, 1)
    up_part = lax.psum_scatter(up_part, "stream", scatter_dimension=0, tiled=False)
    up_part = lax.all_to_all(up_part, "seq", 0, 0)
    grad_gate_up = jnp.transpose(up_part.reshape(seq, piece, 2, shard), (1, 2, 0, 3)).reshape(piece, 2 * FF)

    w_out = take(out_weight, head * HD, HD, 0)
    grad_gated = mm(low_all, w_out, "ij,kj->ik")
    mine = take(gated_h, part * rows, rows, 1) if rep > 1 else gated_h
    grad_out_weight = lax.psum_scatter(
        mm(mine, low_all, "ji,jk->ik").astype(bf16), "stream", scatter_dimension=0, tiled=True
    )
    gp, grad_taps, sums = run_backward(
        T, doc_lengths, proj, small, taps, consts, gain, mixed, states, news, invs, grad_gated
    )
    back = lax.all_to_all(gp.reshape(seq, T, (GROUPS + 1) * HD), "seq", 0, 0)[::rep]
    in_part = mm(normed_all, gp, "ji,jk->ik")
    tail = in_part[:, GROUPS * HD :]
    grad_small_h = tail[:, : NH + 1] + tail[:, NH + 1 : 2 * (NH + 1)]
    in_part = jnp.swapaxes(in_part[:, : GROUPS * HD].astype(bf16).reshape(seq, stream, piece, GROUPS * HD), 0, 1)
    in_part = lax.psum_scatter(in_part, "stream", scatter_dimension=0, tiled=False)
    in_part = lax.all_to_all(in_part, "seq", 0, 0)[::rep]
    grad_in_weight = jnp.transpose(in_part.reshape(H, piece, GROUPS, HD), (1, 2, 0, 3)).reshape(piece, GROUPS * D)

    grad_proj = jnp.transpose(back[:, :, : GROUPS * HD].reshape(H, T, GROUPS, HD), (1, 2, 0, 3)).reshape(T, GROUPS * D)
    grad_logits = back[:, :, GROUPS * HD :].astype(f32)
    grad_logits = grad_logits[:, :, : NH + 1] + grad_logits[:, :, NH + 1 : 2 * (NH + 1)]
    grad_logits = jnp.transpose(grad_logits, (1, 2, 0)).reshape(T, (NH + 1) * H)
    grad_normed = mm(grad_proj, in_weight, "ij,kj->ik") + jnp.einsum(
        "ij,kj->ik", grad_logits, small_weight, precision=lax.Precision.HIGHEST
    )
    back_in, grad_gain_in = norm_back(values, scale_in, gain_in, grad_normed)
    grad_input = grad_residual + back_in

    own = (part == 0).astype(f32)
    flat = jnp.concatenate(
        [
            grad_gain_in, grad_gain_mid,
            own * jnp.concatenate([sums[0], sums[1], sums[2], grad_small_h.T.reshape(-1), grad_taps.reshape(-1)]),
        ]
    )
    every = lax.all_gather(flat, ("seq", "stream"))
    lanes = [jnp.sum(every[:, i : i + D], axis=0) for i in (0, D)]
    every = jnp.sum(every[:, 2 * D :].reshape(seq, stream, -1), axis=1).reshape(H, rep, -1).sum(axis=1)
    heads = every[:, : 3 * HD].reshape(H, 3, HD)
    at = 3 * HD
    grad_small = jnp.transpose(every[:, at : at + 3 * D].reshape(H, NH + 1, D), (2, 1, 0)).reshape(D, (NH + 1) * H)
    at += 3 * D
    grad_conv = jnp.transpose(every[:, at:].reshape(H, CONV, MIXED, HD), (1, 2, 0, 3)).reshape(CONV, MIXED * D)
    return (
        result[None], grad_input[None], lanes[0], grad_in_weight.astype(f32), grad_small, heads[:, 1, 2],
        heads[:, 2, 2], grad_conv, jnp.sum(heads[:, 0], axis=0), grad_out_weight.astype(f32), lanes[1],
        grad_gate_up.astype(f32), grad_down.astype(f32),
    )


def solution(mesh):
    rows, whole, split = P("stream", "seq", None), P(), P(("seq", "stream"), None)
    return jax.shard_map(
        on_device,
        mesh=mesh,
        in_specs=(rows, rows, P("stream", None)) + (whole,) * 11,
        out_specs=(rows, rows, whole, split, whole, whole, whole, whole, whole, split, whole, split, split),
        check_vma=False,
    )
```

time: 2430 us -> 406 us (0.17)
  waiting for transfers between devices: 1250 us -> 73.6 us
  other arithmetic: 693 us -> 12.9 us
  matrix products: 233 us -> 69.5 us
  local copies, waits for them, and re-layouts: 179 us -> 63.2 us
  blocking collectives: 42.2 us -> 91.6 us
  Pallas kernels: 0 us -> 46.5 us
    reduce_scatter x4 -> x2, waiting for transfers between devices: 1150 us -> 14.3 us  [the longest x1 14.3 us: on_device(): lax.psum_scatter(mm(hidden_s, out_all, 'ji,jk->ik').astype(bf16), 'stream...]
    another operation x62 -> x3, other arithmetic: 653 us -> 1.9 us  [the longest x1 1.26 us: on_device(): jnp.stack([mm(mid_all, g_gate_s, 'ji,jk->ik'), mm(mid_all, g_up_s, 'ji,jk...]
    dot_general x95 -> x20, matrix products: 216 us -> 69.5 us  [the longest x19 67.9 us: mm(): return jnp.einsum(dims, a, b, preferred_element_type=f32)]
    all_gather x0 -> x1, blocking collectives: none -> 91.6 us  [on_device(): every = lax.all_gather(flat, ('seq', 'stream'))]
    all_gather x4, waiting for transfers between devices: 76.7 us -> 21.9 us  [the longest x1 18.9 us: on_device(): low_all = lax.all_gather(grad_residual.astype(bf16), 'seq', tiled=True)]
    pallas_call x0 -> x2, Pallas kernels: none -> 46.5 us  [the longest x1 26.5 us: run_backward(): pl.pallas_call(functools.partial(backward_kernel, T), out_shape=(shape((r...]
    psum x1 -> x0, blocking collectives: 42.2 us -> none  [on_device(): lax.psum((grad_gain_in, grad_small_weight, grad_bias, grad_rate, grad_con...]
    unnamed x9 -> x8, waiting for transfers between devices: 0.83 us -> 29.1 us
  transfers between devices with their start and end apart: 11 -> 11, of which waited for: 9 -> 7; matrix products, arithmetic and copies ran while one was open for 23% -> 33% of each run, Pallas kernels for 0% -> 12%
where the time goes in v1:
time: 406 us; the launch traced here: 400 us
  blocking collectives  91.6 us (23%)
  waiting for transfers between devices  73.6 us (18%)
  matrix products  69.5 us (17%)
  local copies, waits for them, and re-layouts  63.2 us (16%)
  Pallas kernels  46.5 us (11%)
  starting transfers between devices  26.6 us (7%)
  between operations  16.3 us (4%)
  other arithmetic  12.9 us (3%)
    all_gather x1, blocking collectives, on_device(): every = lax.all_gather(flat, ('seq', 'stream'))  91.6 us
    dot_general x19, matrix products, mm(): return jnp.einsum(dims, a, b, preferred_element_type=f32)  67.9 us
    unnamed x8, waiting for transfers between devices  29.1 us
    pallas_call x1, Pallas kernels, run_backward(): pl.pallas_call(functools.partial(backward_kernel, T), out_shape=(shape((r...  26.5 us
    unnamed x93, local copies, waits for them, and re-layouts  26.4 us
    pallas_call x1, Pallas kernels, run_forward(): pl.pallas_call(functools.partial(forward_kernel, T, 4 if count % 4 == 0 e...  20 us
    all_gather x1, waiting for transfers between devices, on_device(): low_all = lax.all_gather(grad_residual.astype(bf16), 'seq', tiled=True)  18.9 us
    reduce_scatter x1, waiting for transfers between devices, on_device(): lax.psum_scatter(mm(hidden_s, out_all, 'ji,jk->ik').astype(bf16), 'stream...  14.3 us
  transfers between devices with their start and end apart: 11, of which 7 were waited for; matrix products, arithmetic and copies ran while one was open for 33% of the time, Pallas kernels for 12%

profile of v1, /device:TPU:0, one launch (start us, length us, event | category | flops | bytes accessed | tf_op | source)
XLA Modules:
  0.0 400.1 jit_solution(11675903913537526175)
XLA Ops:
  12.0 16.7 %copy.66 = bf16[1024,6144]{0,1:T(8,128)(2,1)} copy(bf16[1024,6144]{1,0:T(8,128)(2,1)} %param.22) | data formatting | bytes 25165824 | tf_op args[4]
  28.7 2.9 constant_dynamic-slice_fusion.1
  38.2 2.9 all-gather.8.cloned.1.call-done
  41.1 5.2 %convolution_convert_fusion.proj = bf16[1024,768]{1,0:T(8,128)(2,1)} fusion(bf16[1024,1024]{1,0:T(8,128)(2,1)} %all-gather.8.cloned.1.call-done, bf16[1024,768]{0,1:T(8,128)(2,1)} %bitcast.170), kind=kOutput, calls=%fused_computation.13 | convolution fusion | flops 1611399168 | bytes 5242880 | tf_op jit(solution)/shard_map/ij,jk->ik/dot_general | solution.py:425
  47.8 20.0 %mixer_forward.1 = (bf16[1024,128]{1,0:T(8,128)(2,1)}, f32[1024,128]{1,0:T(8,128)}, bf16[8,128,128]{2,1,0:T(8,128)(2,1)}, bf16[2048,128]{1,0:T(8,128)(2,1)}, bf16[8,256,256]{2,1,0:T(8,128)(2,1)}) custom-call(s32[1,8]{1,0:T(1,128)} %lengths.3, bf16[1024,768]{1,0:T(8,128)(2,1)} %convolution_convert_fusion.proj, f32[1024,128]{1,0:T(8,128)} %fusion.50.small, ...), custom_call_target="tpu_custom_call" | custom-call | tf_op jit(solution)/shard_map/mixer_forward/pallas_call | solution.py:374
  69.6 3.4 all-to-all-start
  73.3 5.8 %fusion.58 = f32[128,2816]{1,0:T(8,128)} fusion(bf16[2816,1024]{1,0:T(8,128)(2,1)} %param.31, bf16[1,128,1024]{2,1,0:T(8,128)(2,1)S(1)} %copy-done.4), kind=kOutput, calls=%fused_computation.79 | convolution fusion | flops 738197504 | bytes 7471104 | tf_op jit(solution)/shard_map/ij,kj->ik/dot_general | solution.py:425
  80.7 3.6 fusion.2
  84.4 4.1 %fusion.6 = f32[128,2816]{1,0:T(8,128)S(1)} fusion(bf16[128,1024]{1,0:T(8,128)(2,1)S(1)} %multiply_convert_fusion.12, bf16[1024,5632]{1,0:T(8,128)(2,1)} %param.30), kind=kOutput, calls=%fused_computation.6 | convolution fusion | flops 738197504 | bytes 7471104 | tf_op jit(solution)/shard_map/ij,jk->ik/dot_general | solution.py:425
  88.5 6.0 %fusion = f32[128,1024]{1,0:T(8,128)S(1)} fusion(bf16[1024,5632]{1,0:T(8,128)(2,1)} %param.30, f32[128,2816]{1,0:T(8,128)S(1)} %copy-done.9, f32[128,2816]{1,0:T(8,128)S(1)} %fusion.6), kind=kOutput, calls=%fused_computation | convolution fusion | flops 740360192 | bytes 9175040 | tf_op jit(solution)/shard_map/ij,kj->ik/dot_general | solution.py:425
  99.7 4.0 %fusion.12 = f32[1024,352]{0,1:T(8,128)} fusion(bf16[1,1024,1024]{2,1,0:T(8,128)(2,1)} %all-gather.14.cloned.1.call-done, bf16[2816,1024]{1,0:T(8,128)(2,1)} %param.31, s32[]{:T(128)S(6)} %select_n.28), kind=kOutput, calls=%fused_computation.14 | convolution fusion | flops 738197504 | bytes 4259844 | tf_op jit(solution)/shard_map/ij,kj->ik/dot_general | solution.py:425
  103.7 4.5 %fusion.26 = bf16[1,128,1024]{2,1,0:T(8,128)(2,1)} fusion(f32[128,1024]{1,0:T(8,128)S(1)} %get-tuple-element.68, bf16[2816,1024]{1,0:T(8,128)(2,1)} %param.31, f32[128,2816]{1,0:T(8,128)S(1)} %copy-done.28, f32[128,2816]{1,0:T(8,128)S(1)} %copy-done.30), kind=kOutput, calls=%fused_computation.37 | convolution fusion | flops 740622336 | bytes 9437184 | tf_op jit(solution)/shard_map/ij,jk->ik/dot_general | solution.py:425
  108.2 18.9 %all-gather.10.cloned.1.call-done = bf16[1024,1024]{1,0:T(8,128)(2,1)} async-done(((bf16[128,1024]{1,0:T(8,128)(2,1)}), bf16[1024,1024]{1,0:T(8,128)(2,1)}) %all-gather.10.cloned.1.call-update) | async-done | bytes 2097168 | tf_op jit(solution)/shard_map/all_gather | solution.py:478
  127.1 3.1 fusion.60.grad_gated
  130.2 26.5 %mixer_backward.1 = (bf16[1024,896]{1,0:T(8,128)(2,1)}, f32[4,640]{1,0:T(4,128)}, f32[8,128]{1,0:T(8,128)}) custom-call(s32[1,8]{1,0:T(1,128)} %lengths.3, bf16[1024,768]{1,0:T(8,128)(2,1)} %convolution_convert_fusion.proj, f32[1024,128]{1,0:T(8,128)} %fusion.50.small, f32[4,640]{1,0:T(4,128)} %bitcast.180, f32[8,128]{1,0:T(8,128)} %copy-done.16, ...), custom_call_target="tpu_custom_call" | custom-call | tf_op jit(solution)/shard_map/mixer_backward/pallas_call | solution.py:395
  156.8 3.8 copy.69
  160.6 4.4 %all-to-all-start.1 = ((bf16[8,128,896]{1,2,0:T(8,128)(2,1)}), bf16[8,128,896]{1,2,0:T(8,128)(2,1)}, u32[]{:S(2)}, u32[]{:S(2)}) async-start(bf16[8,128,896]{1,2,0:T(8,128)(2,1)} %copy.69), calls=%async_computation.1 | async-start | bytes 3670016 | tf_op jit(solution)/shard_map/all_to_all | solution.py:503
  165.0 10.3 %reduce-scatter.7.cloned.1.call-start = ((), (), s32[]{:S(2)}) async-start(), calls=%async_computation.8 | async-start | bytes 327680 | tf_op jit(solution)/shard_map/reduce_scatter | solution.py:497
  176.7 3.3 fusion.31
  180.0 3.1 fusion.33
  186.2 3.8 fusion.89
  192.3 3.6 fusion.21
  199.1 4.3 %copy.77 = bf16[1024,2,352]{2,1,0:T(2,128)(2,1)S(1)} copy(bf16[1024,2,352]{0,2,1:T(8,128)(2,1)} %pad_maximum_fusion) | data formatting | bytes 2883584 | tf_op jit(solution)/shard_map/stack | solution.py:488
  207.1 14.3 %reduce-scatter.9.cloned.1.call-done = bf16[88,1024]{1,0:T(8,128)(2,1)} async-done(((bf16[352,1024]{1,0:T(8,128)(2,1)}), bf16[88,1024]{1,0:T(8,128)(2,1)}) %reduce-scatter.9.cloned.1.call-update) | async-done | bytes 180240 | tf_op jit(solution)/shard_map/reduce_scatter | solution.py:485
  225.7 9.5 %fusion.88 = f32[128,1024]{1,0:T(8,128)S(1)} fusion(bf16[128,6144]{0,1:T(8,128)(2,1)S(1)} %bitcast.162, bf16[1024,6144]{1,0:T(8,128)(2,1)} %param.22), kind=kOutput, calls=%fused_computation.134 | convolution fusion | flops 1610612736 | bytes 14680064 | tf_op jit(solution)/shard_map/ij,kj->ik/dot_general | solution.py:425
  238.9 91.6 %all-gather.2 = f32[32,1,8064]{2,1,0:T(1,128)S(1)} all-gather(f32[1,1,8064]{2,1,0:T(1,128)S(1)} %reshape.242), channel_id=2, replica_groups=mesh['seq'=8,'stream'=4] {'seq','stream'}, dimensions={0}, use_global_device_ids=true | all-gather | bytes 1064448 | tf_op jit(solution)/shard_map/all_gather | solution.py:529
  334.0 27.8 %all-reduce.6.cloned.1.call-done = (bf16[4,8,32,768]{3,2,0,1:T(8,128)(2,1)}, bf16[4,8,32,704]{3,2,0,1:T(8,128)(2,1)}) async-done(((bf16[4,8,32,768]{3,2,0,1:T(8,128)(2,1)}, bf16[4,8,32,704]{3,2,0,1:T(8,128)(2,1)}), (bf16[4,8,32,768]{3,2,0,1:T(8,128)(2,1)}, bf16[4,8,32,704]{3,2,0,1:T(8,128)(2,1)})) %all-reduce.6.cloned.1.call-update) | async-done | bytes 3014672
  361.8 2.4 dynamic-slice_bitcast_fusion
  364.2 4.2 %all-to-all-start.3 = ((bf16[8,32,704]{2,1,0:T(8,128)(2,1)}), bf16[8,32,704]{2,1,0:T(8,128)(2,1)S(1)}, u32[]{:S(2)}, u32[]{:S(2)}) async-start(bf16[8,32,704]{2,1,0:T(8,128)(2,1)} %dynamic-slice_bitcast_fusion), calls=%async_computation.4 | async-start | bytes 786432 | tf_op jit(solution)/shard_map/all_to_all | solution.py:491
  368.4 2.4 dynamic-slice_bitcast_fusion.1
  370.8 5.9 %all-to-all-done.3 = bf16[8,32,704]{2,1,0:T(8,128)(2,1)S(1)} async-done(((bf16[8,32,704]{2,1,0:T(8,128)(2,1)}), bf16[8,32,704]{2,1,0:T(8,128)(2,1)S(1)}, u32[]{:S(2)}, u32[]{:S(2)}) %all-to-all-start.3) | async-done | bytes 360480 | tf_op jit(solution)/shard_map/all_to_all | solution.py:491
  376.8 3.7 all-to-all-start.2
  (170 shorter events, 57.8 us)
Async XLA Ops:
  7.2 72.7 %copy-start = (bf16[1024,1024]{1,0:T(8,128)(2,1)S(1)}, bf16[1024,1024]{1,0:T(8,128)(2,1)}, u32[]{:S(2)}) copy-start(bf16[1024,1024]{1,0:T(8,128)(2,1)} %param.28) | copy-start | bytes 6291460
  7.2 33.9 %all-gather.8.cloned.1.call-start = ((), (), s32[]{:S(2)}) async-start(), calls=%async_computation.6 | async-start | bytes 2359296 | tf_op jit(solution)/shard_map/all_gather | solution.py:442
  10.3 89.4 %all-gather.14.cloned.1.call-start = ((), (), s32[]{:S(2)}) async-start(), calls=%async_computation.11 | async-start | bytes 2359296 | tf_op jit(solution)/shard_map/all_gather | solution.py:443
  28.7 4.2 %copy-start.22 = (f32[8]{0:T(128)S(1)}, f32[8]{0:T(128)}, u32[]{:S(2)}) copy-start(f32[8]{0:T(128)} %param.24) | copy-start | bytes 100
  28.7 5.3 %copy-start.23 = (f32[8]{0:T(128)S(1)}, f32[8]{0:T(128)}, u32[]{:S(2)}) copy-start(f32[8]{0:T(128)} %param.25) | copy-start | bytes 100
  38.2 8.1 %copy-start.16 = (f32[8,128]{1,0:T(8,128)}, f32[8,128]{1,0:T(8,128)S(1)}, u32[]{:S(2)}) copy-start(f32[8,128]{1,0:T(8,128)S(1)} %scatter.9.consts) | copy-start | bytes 12292
  41.1 5.2 %copy-start.18 = (bf16[1024,1024]{1,0:T(8,128)(2,1)S(1)}, bf16[1024,1024]{1,0:T(8,128)(2,1)}, u32[]{:S(2)}) copy-start(bf16[1024,1024]{1,0:T(8,128)(2,1)} %all-gather.8.cloned.1.call-done) | copy-start | bytes 6291460
  47.8 25.5 %copy-start.4 = (bf16[1,128,1024]{2,1,0:T(8,128)(2,1)S(1)}, bf16[1,128,1024]{2,1,0:T(8,128)(2,1)}, u32[]{:S(2)}) copy-start(bf16[1,128,1024]{2,1,0:T(8,128)(2,1)} %param.19) | copy-start | bytes 786436
  69.6 10.3 %all-to-all-start = ((bf16[8,128,128]{1,2,0:T(8,128)(2,1)}), bf16[8,128,128]{1,2,0:T(8,128)(2,1)S(1)}, u32[]{:S(2)}, u32[]{:S(2)}) async-start(bf16[8,128,128]{1,2,0:T(8,128)(2,1)} %copy.68), calls=%async_computation | async-start | bytes 524288 | tf_op jit(solution)/shard_map/all_to_all | solution.py:458
  73.0 6.9 %copy-start.3 = (bf16[1,128,1024]{2,1,0:T(8,128)(2,1)S(1)}, bf16[1,128,1024]{2,1,0:T(8,128)(2,1)}, u32[]{:S(2)}) copy-start(bf16[1,128,1024]{2,1,0:T(8,128)(2,1)} %param.18) | copy-start | bytes 786436
  73.0 54.1 %all-gather.10.cloned.1.call-start = ((), (), s32[]{:S(2)}) async-start(), calls=%async_computation.7 | async-start | bytes 2359296 | tf_op jit(solution)/shard_map/all_gather | solution.py:478
  84.4 10.2 %copy-start.27 = (f32[128,2816]{1,0:T(8,128)}, f32[128,2816]{1,0:T(8,128)S(1)}, u32[]{:S(2)}) copy-start(f32[128,2816]{1,0:T(8,128)S(1)} %fusion.2) | copy-start | bytes 4325380
  84.4 4.1 %copy-start.9 = (f32[128,2816]{1,0:T(8,128)S(1)}, f32[128,2816]{1,0:T(8,128)}, u32[]{:S(2)}) copy-start(f32[128,2816]{1,0:T(8,128)} %fusion.58) | copy-start | bytes 4325380
  84.4 10.2 %slice-start = ((s8[11534336]{0:T(1024)(128)(4,1)}), s8[4194304]{0:T(1024)(128)(4,1)S(1)}, s32[]{:S(2)}) async-start(s8[11534336]{0:T(1024)(128)(4,1)} %bitcast.189), calls=%async_computation.13 | async-start | bytes 8388608
  84.4 10.2 %slice-start.1 = ((s8[11534336]{0:T(1024)(128)(4,1)}), s8[4194304]{0:T(1024)(128)(4,1)S(1)}, s32[]{:S(2)}) async-start(s8[11534336]{0:T(1024)(128)(4,1)} %bitcast.189), calls=%async_computation.14 | async-start | bytes 8388608
  88.5 6.1 %copy-start.29 = (f32[128,2816]{1,0:T(8,128)}, f32[128,2816]{1,0:T(8,128)S(1)}, u32[]{:S(2)}) copy-start(f32[128,2816]{1,0:T(8,128)S(1)} %fusion.6) | copy-start | bytes 4325380
  88.5 6.1 %slice-start.2 = ((s8[11534336]{0:T(1024)(128)(4,1)}), s8[3145728]{0:T(1024)(128)(4,1)S(1)}, s32[]{:S(2)}) async-start(s8[11534336]{0:T(1024)(128)(4,1)} %bitcast.189), calls=%async_computation.15 | async-start | bytes 6291456
  98.5 78.2 %all-gather.12.cloned.1.call-start = ((), (), s32[]{:S(2)}) async-start(), calls=%async_computation.9 | async-start | bytes 2359296 | tf_op jit(solution)/shard_map/all_gather | solution.py:463
  160.6 14.8 %copy-start.2 = (bf16[1024,1024]{1,0:T(8,128)(2,1)S(1)}, bf16[1024,1024]{1,0:T(8,128)(2,1)}, u32[]{:S(2)}) copy-start(bf16[1024,1024]{1,0:T(8,128)(2,1)} %all-gather.10.cloned.1.call-done) | copy-start | bytes 6291460
  160.6 14.8 %copy-start.10 = (bf16[1024,128]{1,0:T(8,128)(2,1)S(1)}, bf16[1024,128]{1,0:T(8,128)(2,1)}, u32[]{:S(2)}) copy-start(bf16[1024,128]{1,0:T(8,128)(2,1)} %get-tuple-element.45) | copy-start | bytes 786436
  160.6 62.5 %all-to-all-start.1 = ((bf16[8,128,896]{1,2,0:T(8,128)(2,1)}), bf16[8,128,896]{1,2,0:T(8,128)(2,1)}, u32[]{:S(2)}, u32[]{:S(2)}) async-start(bf16[8,128,896]{1,2,0:T(8,128)(2,1)} %copy.69), calls=%async_computation.1 | async-start | bytes 3670016 | tf_op jit(solution)/shard_map/all_to_all | solution.py:503
  165.0 40.6 %reduce-scatter.7.cloned.1.call-start = ((), (), s32[]{:S(2)}) async-start(), calls=%async_computation.8 | async-start | bytes 327680 | tf_op jit(solution)/shard_map/reduce_scatter | solution.py:497
  176.6 44.8 %reduce-scatter.9.cloned.1.call-start = ((), (), s32[]{:S(2)}) async-start(), calls=%async_computation.10 | async-start | bytes 901120 | tf_op jit(solution)/shard_map/reduce_scatter | solution.py:485
  180.0 4.3 %copy-start.19 = (bf16[1,1024,1024]{2,1,0:T(8,128)(2,1)S(1)}, bf16[1,1024,1024]{2,1,0:T(8,128)(2,1)}, u32[]{:S(2)}) copy-start(bf16[1,1024,1024]{2,1,0:T(8,128)(2,1)} %all-gather.14.cloned.1.call-done) | copy-start | bytes 6291460
  186.2 175.6 %all-reduce.6.cloned.1.call-start = ((), (), s32[]{:S(2)}) async-start(), calls=%async_computation.12 | async-start | bytes 6291456
  192.3 4.3 %copy-start.34 = (f32[1024,352]{0,1:T(8,128)S(1)}, f32[1024,352]{0,1:T(8,128)}, u32[]{:S(2)}) copy-start(f32[1024,352]{0,1:T(8,128)} %copy-done.33) | copy-start | bytes 4325380
  225.7 9.6 %copy-start.12 = (f32[1024,24]{0,1:T(8,128)S(1)}, f32[1024,24]{0,1:T(8,128)}, u32[]{:S(2)}) copy-start(f32[1024,24]{0,1:T(8,128)} %param.23) | copy-start | bytes 294916
  225.7 9.6 %copy-start.14 = (f32[1024]{0:T(1024)S(1)}, f32[1024]{0:T(1024)}, u32[]{:S(2)}) copy-start(f32[1024]{0:T(1024)} %param.21) | copy-start | bytes 12292
  364.2 19.4 %copy-start.5 = (f32[128,1024]{1,0:T(8,128)S(1)}, f32[128,1024]{1,0:T(8,128)}, u32[]{:S(2)}) copy-start(f32[128,1024]{1,0:T(8,128)} %get-tuple-element.70) | copy-start | bytes 1572868
  364.2 19.4 %copy-start.7 = (f32[128,1024]{1,0:T(8,128)S(1)}, f32[128,1024]{1,0:T(8,128)}, u32[]{:S(2)}) copy-start(f32[128,1024]{1,0:T(8,128)} %copy-done.6) | copy-start | bytes 1572868
  364.2 12.5 %all-to-all-start.3 = ((bf16[8,32,704]{2,1,0:T(8,128)(2,1)}), bf16[8,32,704]{2,1,0:T(8,128)(2,1)S(1)}, u32[]{:S(2)}, u32[]{:S(2)}) async-start(bf16[8,32,704]{2,1,0:T(8,128)(2,1)} %dynamic-slice_bitcast_fusion), calls=%async_computation.4 | async-start | bytes 786432 | tf_op jit(solution)/shard_map/all_to_all | solution.py:491
  376.8 11.9 %all-to-all-start.2 = ((bf16[8,32,768]{2,1,0:T(8,128)(2,1)}), bf16[8,32,768]{2,1,0:T(8,128)(2,1)S(1)}, u32[]{:S(2)}, u32[]{:S(2)}) async-start(bf16[8,32,768]{2,1,0:T(8,128)(2,1)} %dynamic-slice_bitcast_fusion.1), calls=%async_computation.2 | async-start | bytes 786432 | tf_op jit(solution)/shard_map/all_to_all | solution.py:509
  (17 other events, 46.2 us)
Sparse Core Ops, SparseCore 0:
  10.5 30.5 all-gather.7
  43.0 27.8 all-gather.13
  98.6 28.4 all-gather.9
  128.9 27.8 all-gather.11
  176.7 20.7 reduce-scatter.6
  200.3 21.0 reduce-scatter.8
  223.9 137.8 all-reduce.5

commit v2 on v1

v2 whole, which is shorter than its diff:
```python
import functools

import jax
import jax.numpy as jnp
from jax import lax
from jax.experimental import pallas as pl
from jax.experimental.pallas import tpu as pltpu
from jax.sharding import PartitionSpec as P

D = 1024
H = 8
HD = 128
FF = 2816
NH = 2
CONV = 4
GROUPS = 2 + 2 * NH
MIXED = GROUPS - 1
SMALL = NH + 1
DOCS = 8
TILE = 256
EPS = 1e-06

f32 = jnp.float32
bf16 = jnp.bfloat16
MESH = pl.DeviceIdType.MESH
DMA = pltpu.SemaphoreType.DMA
VMEM = pl.BlockSpec(memory_space=pltpu.VMEM)
SMEM = pl.BlockSpec(memory_space=pltpu.SMEM)
ANY = pl.BlockSpec(memory_space=pl.ANY)
LIMIT = 56 * 1024 * 1024
shape = jax.ShapeDtypeStruct


def dot(a, b, dims):
    if isinstance(a, tuple) and isinstance(b, tuple):
        return dot(a[0], b[0], dims) + (dot(a[0], b[1], dims) + dot(a[1], b[0], dims))
    if isinstance(a, tuple):
        return dot(a[0], b, dims) + dot(a[1], b, dims)
    if isinstance(b, tuple):
        return dot(a, b[0], dims) + dot(a, b[1], dims)
    return lax.dot_general(
        a.astype(bf16), b.astype(bf16), ((dims[:1], dims[1:]), ((), ())), preferred_element_type=f32
    )


def nn(a, b):
    return dot(a, b, (1, 0))


def nt(a, b):
    return dot(a, b, (1, 1))


def tn(a, b):
    return dot(a, b, (0, 0))


def halves(x):
    high = x.astype(bf16)
    return high, (x - high.astype(f32)).astype(bf16)


def thirds(x):
    high, low = halves(x)
    return high, low, (x - high.astype(f32) - low.astype(f32)).astype(bf16)


def keep(ref, at, x):
    ref[0, at], ref[1, at] = halves(x)


def kept(ref, at):
    return ref[0, at], ref[1, at]


def nn_exact(ones, x):
    high, low, lowest = thirds(x)
    return nn(ones, high) + (nn(ones, low) + nn(ones, lowest))


def sigmoid(x):
    return 1.0 / (1.0 + jnp.exp(-x))


def softplus(x):
    return jnp.maximum(x, 0.0) + jnp.log(1.0 + jnp.exp(-jnp.abs(x)))


def norm_scale(values):
    return lax.rsqrt(jnp.mean(values * values, axis=-1, keepdims=True) + EPS)


def norm_back(values, scale, gain, grad):
    normal = values * scale
    e = grad * gain
    back = scale * (e - normal * jnp.mean(e * normal, axis=-1, keepdims=True))
    return back, jnp.sum(grad * normal, axis=0, keepdims=True)


def iota(dims, axis):
    return lax.broadcasted_iota(jnp.int32, dims, axis)


def doc_at(starts, positions):
    total = jnp.full(positions.shape, -1, jnp.int32)
    for start in starts:
        total = total + (start <= positions).astype(jnp.int32)
    return total


def doc_starts(lengths_ref):
    starts, at = [], jnp.int32(0)
    for j in range(DOCS):
        starts.append(at)
        at = at + lengths_ref[0, j]
    return starts


def stack2(a, b):
    return jnp.concatenate([a, b], axis=0)


def beside(a, b):
    return jnp.concatenate([a, b], axis=1)


def quad(a, b, c, d):
    return stack2(beside(a, b), beside(c, d))


def rows_of(i, size):
    return pl.ds(pl.multiple_of(i * size, size), size)


def greet(axis, peers):
    barrier = pltpu.get_barrier_semaphore()
    for peer in peers:
        pl.semaphore_signal(barrier, inc=1, device_id={axis: peer}, device_id_type=MESH)
    return lambda: pl.semaphore_wait(barrier, len(peers))


def remote(src, dst, send, receive, axis, peer):
    return pltpu.make_async_remote_copy(src, dst, send, receive, device_id={axis: peer}, device_id_type=MESH)


class Gather:
    def __init__(self, n, T, src, dst, sems):
        self.n, self.T, self.src, self.dst = n, T, src, dst
        self.ss, self.rs, self.fs, self.fr = sems
        self.me = lax.axis_index("seq")
        self.sib = self.me + 1 - 2 * lax.rem(self.me, 2)

    def at(self, device):
        return self.dst.at[rows_of(device, self.T)]

    def direct(self, k):
        peer = self.sib if k == 0 else lax.rem(self.me + 2 * k, self.n)
        return remote(self.src, self.at(self.me), self.ss.at[k], self.rs.at[k], "seq", peer)

    def passed(self, k):
        block = self.at(lax.rem(self.me - 2 * k + self.n, self.n))
        return remote(block, block, self.fs.at[k], self.fr.at[k], "seq", self.sib)

    def start(self):
        for k in (*range(1, self.n // 2), 0):
            self.direct(k).start()

    def forward(self):
        for k in range(1, self.n // 2):
            self.direct(k).wait_recv()
            self.passed(k).start()

    def finish(self):
        for k in range(self.n // 2):
            self.direct(k).wait_send()
            if k:
                self.passed(k).wait_send()


def gather_sems(n):
    return [DMA((n // 2,)) for _ in range(4)]


def conv_of(block, taps, docs, T):
    total = block[8:] * taps[CONV - 1 : CONV]
    for lag in range(1, CONV):
        same = (docs[0] == docs[lag]).astype(f32)
        total = total + block[8 - lag : 8 - lag + T] * (taps[CONV - 1 - lag : CONV - lag] * same)
    return total


def chunk_gates(logits, bias, rate, starts, first, T):
    lane = iota((T, HD), 1)
    shifted = logits + bias
    gate = -rate * softplus(shifted)
    place_i, place_j = iota((T, T), 0), iota((T, T), 1)
    lower = place_j <= place_i
    cumul = nn_exact(lower.astype(bf16), jnp.where(lane == NH, gate, 0.0))
    beta = 2.0 * sigmoid(logits)
    b0, b1 = beta[:, 0:1], beta[:, 1:2]
    g = cumul[:, NH : NH + 1]
    g_row = jnp.transpose(cumul)[NH : NH + 1, :]
    g_last = cumul[T - 1 : T, NH : NH + 1]
    position = first + iota((T, 1), 0)
    docs = [doc_at(starts, position - lag) for lag in range(CONV)]
    doc = docs[0]
    doc_row = doc_at(starts, first + iota((1, T), 1))
    doc_before = doc_at(starts, jnp.full((1, 1), first - 1, jnp.int32))
    doc_last = doc_at(starts, jnp.full((1, 1), first + (T - 1), jnp.int32))
    joined = lower & (doc == doc_row)
    decay = jnp.where(joined, jnp.exp(jnp.where(joined, g - g_row, 0.0)), 0.0)
    strict = jnp.where(place_i == place_j, 0.0, decay)
    from_start = jnp.exp(g) * (doc == doc_before).astype(f32)
    to_end = jnp.exp(jnp.minimum(g_last - g, 0.0)) * (doc == doc_last).astype(f32)
    whole = jnp.exp(g_last) * (doc_last == doc_before).astype(f32)
    return dict(
        shifted=shifted, beta=beta, b=stack2(b0, b1), docs=docs, decay=decay,
        decays=quad(strict, strict, decay, strict), hd=from_start, hd2=stack2(from_start, from_start),
        to_end=stack2(to_end, to_end), whole=whole,
    )


def key_scale(raw):
    return lax.rsqrt(jnp.sum(raw * raw, axis=-1, keepdims=True) + EPS)


def chunk_inputs(block, taps, docs, T):
    conv = conv_of(block, taps, docs, T)
    sig = sigmoid(conv)
    active = conv * sig
    cut = [active[:, i * HD : (i + 1) * HD] for i in range(MIXED)]
    scales = (key_scale(cut[1]), key_scale(cut[2]))
    keys = stack2(cut[1] * scales[0], cut[2] * scales[1])
    values = stack2(cut[3], cut[4])
    return conv, sig, cut[0], keys, values, stack2(*scales)


def inverses(lowers, T):
    size = NH * T
    row, col = iota((size, size), 0), iota((size, size), 1)
    differ = (row & (T - 1)) ^ (col & (T - 1))
    eye = (row == col).astype(f32)
    found = [jnp.where(row == col, 1.0, jnp.where(differ == 0, -a, 0.0)) for a in lowers]
    step = 1
    while step < T:
        level = (differ >= step) & (differ < 2 * step)
        parts = [nn(jnp.where(level, a, 0.0), x) for a, x in zip(lowers, found)]
        found = [x - nn(x, part) for x, part in zip(found, parts)]
        step *= 2
    a_cut = [halves(a) for a in lowers]
    x_cut = [halves(x) for x in found]
    errors = [
        eye - x - (nn(a[0], xc[0]) + (nn(a[0], xc[1]) + nn(a[1], xc[0])))
        for a, x, xc in zip(a_cut, found, x_cut)
    ]
    return [x + nn(xc[0], e) for x, xc, e in zip(found, x_cut, errors)]


def head_gate(mixed, raw):
    scale = norm_scale(mixed)
    return mixed * scale, scale, sigmoid(raw)


def head_taps(taps_ref, head):
    cuts = [taps_ref[:, pl.ds(pl.multiple_of(i * D + head * HD, HD), HD)] for i in range(MIXED)]
    return jnp.concatenate(cuts, axis=1)


def intra_turn(T, per, starts, bias, rate, taps, small, xbuf, invs, ubuf, wbuf, qbuf, pbuf, dbuf, gates, turn, _):
    held, lowers = [], []
    for i in range(per):
        c = turn * per + i
        first = pl.multiple_of(c * T, T)
        gate = chunk_gates(small[pl.ds(first, T), :], bias, rate, starts, first, T)
        block = xbuf[pl.ds(first, T + 8), :]
        conv, sig, query, keys, values, scales = chunk_inputs(block, taps, gate["docs"], T)
        key_pair = halves(keys)
        lowers.append(gate["b"] * (nt(key_pair, key_pair) * gate["decays"]))
        held.append((c, gate, query, keys, key_pair, values))
    found = inverses(lowers, T)
    for (c, gate, query, keys, key_pair, values), inverse in zip(held, found):
        at, two = rows_of(c, T), rows_of(c, NH * T)
        pair = halves(inverse)
        invs[0, c], invs[1, c] = pair
        both = nn(pair, halves(gate["b"] * beside(values, gate["hd2"] * keys)))
        ubuf[two, :] = both[:, :HD]
        keep(wbuf, two, both[:, HD:])
        query_pair = halves(query)
        qbuf[0, at], qbuf[1, at] = query_pair
        keep(pbuf, at, nt(query_pair, key_pair) * beside(gate["decay"], gate["decay"]))
        keep(dbuf, two, gate["to_end"] * keys)
        gates[at, :] = jnp.where(iota((T, HD), 1) == 0, gate["hd"], gate["whole"])
    return 0


def across_turn(T, gain, proj, mixed_out, states, news, head_rows, ubuf, wbuf, qbuf, pbuf, dbuf, gates, done, c, state):
    at, two = rows_of(c, T), rows_of(c, NH * T)
    state_pair = halves(state)
    states[0, c], states[1, c] = state_pair
    new = ubuf[two, :] - nn(kept(wbuf, two), state_pair)
    new_pair = halves(new)
    news[0, two], news[1, two] = new_pair
    gate = gates[at, :]
    mixed = gate[:, 0:1] * nn(kept(qbuf, at), state_pair) + nn(kept(pbuf, at), new_pair)
    mixed_out[at, :] = mixed
    raw = proj[at, MIXED * HD :].astype(f32)
    normal, _, sig = head_gate(mixed, raw)
    head_rows[at, :] = ((normal * gain[...]) * (raw * sig)).astype(bf16)
    done(c)
    return gate[0:1, 1:2] * state + tn(kept(dbuf, two), new_pair)


def forward_kernel(
    n, rep, T, per, lengths, bias_ref, rate_ref, tokens, cotangent, gain_in, w_in, w_small, taps_ref, gain,
    gated, normed, out_all, proj, small, mixed_out, states, news, invs, head_rows,
    own, w_head, w_wide, xbuf, ubuf, wbuf, qbuf, pbuf, dbuf, gates,
    w_sems, own_sem, a_ss, a_rs, *sems,
):
    me = lax.axis_index("seq")
    head = me // rep
    wait_for_all = greet("seq", [lax.rem(me + k, n) for k in range(1, n)])
    width = MIXED * HD
    loads = [
        pltpu.make_async_copy(
            w_in.at[:, pl.ds(pl.multiple_of(i * D + head * HD, HD), HD)], w_head.at[:, i * HD : (i + 1) * HD], w_sems.at[i]
        )
        for i in range(GROUPS)
    ]
    for load in loads:
        load.start()
    values = tokens[...].astype(f32)
    own[...] = (values * norm_scale(values) * gain_in[...]).astype(bf16)
    local = pltpu.make_async_copy(own, normed.at[rows_of(me, T)], own_sem)
    local.start()
    wait_for_all()
    first_gather = Gather(n, T, own, normed, sems[:4])
    first_gather.start()
    second_gather = Gather(n, T, cotangent, out_all, sems[4:8])

    starts = doc_starts(lengths)
    bias, rate = bias_ref[head], rate_ref[head]
    taps = head_taps(taps_ref, head)
    xbuf[0:8, :] = jnp.zeros((8, width), f32)
    w_wide[...] = jnp.zeros((D, HD), bf16)
    chosen = jnp.where((iota((D, SMALL * H), 1) & (H - 1)) == head, w_small[...], 0.0)
    for i, piece in enumerate(thirds(chosen)):
        w_wide[:, i * SMALL * H : (i + 1) * SMALL * H] = piece
    group = iota((HD, HD), 0) >> 3
    lane = iota((HD, HD), 1)
    picks = ((group == lane) | (group == lane + SMALL) | (group == lane + 2 * SMALL)) & (lane < SMALL)
    picks = picks.astype(bf16)
    for load in loads:
        load.wait()
    local.wait()
    for k in range(n // 2):
        if k == 1:
            first_gather.forward()
        if k:
            first_gather.passed(k).wait_recv()
        else:
            first_gather.direct(0).wait_recv()
        at = rows_of(lax.rem(me // 2 - k + n // 2, n // 2), 2 * T)
        block = normed[at, :]
        result = nn(block, w_head[...]).astype(bf16)
        proj[at, :] = result
        xbuf[pl.ds(pl.multiple_of(8 + lax.rem(me // 2 - k + n // 2, n // 2) * (2 * T), 8), 2 * T), :] = result[:, :width].astype(f32)
        raw = thirds(nn(block, w_wide[...]))
        small[at, :] = nn(raw[0], picks) + (nn(raw[1], picks) + nn(raw[2], picks))
    first_gather.finish()
    keep = pltpu.make_async_copy(cotangent, out_all.at[rows_of(me, T)], own_sem)
    keep.start()
    second_gather.start()

    intra = functools.partial(
        intra_turn, T, per, starts, bias, rate, taps, small, xbuf, invs, ubuf, wbuf, qbuf, pbuf, dbuf, gates
    )
    lax.fori_loop(0, n // per, intra, 0)
    second_gather.forward()
    column = pl.ds(pl.multiple_of(head * HD, HD), HD)

    def row_copy(c):
        return remote(head_rows.at[rows_of(c, T)], gated.at[:, column], a_ss.at[c], a_rs.at[head], "seq", c)

    def send_rows(c):
        @pl.when((c != me) & (lax.rem(me, rep) == 0))
        def _():
            row_copy(c).start()

    across = functools.partial(
        across_turn, T, gain, proj, mixed_out, states, news, head_rows, ubuf, wbuf, qbuf, pbuf, dbuf, gates, send_rows
    )
    lax.fori_loop(0, n, across, jnp.zeros((HD, HD), f32))

    @pl.when(lax.rem(me, rep) == 0)
    def _():
        mine = pltpu.make_async_copy(head_rows.at[rows_of(me, T)], gated.at[:, column], own_sem)
        keep.wait()
        mine.start()
        mine.wait()

    @pl.when(lax.rem(me, rep) != 0)
    def _():
        keep.wait()

    def settle(k, _):
        peer = lax.rem(me + k, n)

        @pl.when(lax.rem(me, rep) == 0)
        def _():
            row_copy(peer).wait_send()

        @pl.when(lax.rem(peer, rep) == 0)
        def _():
            source = peer // rep
            remote(
                head_rows.at[rows_of(me, T)], gated.at[:, pl.ds(pl.multiple_of(source * HD, HD), HD)],
                a_ss.at[peer], a_rs.at[source], "seq", peer,
            ).wait_recv()

        return 0

    lax.fori_loop(1, n, settle, 0)
    second_gather.direct(0).wait_recv()
    for k in range(1, n // 2):
        second_gather.passed(k).wait_recv()
    second_gather.finish()


def forward_scratch(n, T):
    rows = n * T
    return [
        pltpu.VMEM((rows + 8, MIXED * HD), f32), pltpu.VMEM((NH * rows, HD), f32),
        pltpu.VMEM((2, NH * rows, HD), bf16), pltpu.VMEM((2, rows, HD), bf16), pltpu.VMEM((2, rows, NH * T), bf16),
        pltpu.VMEM((2, NH * rows, HD), bf16), pltpu.VMEM((rows, HD), f32),
    ]


def run_forward(n, rep, T, lengths, bias, rate, tokens, cotangent, gain_in, w_in, w_small, taps, gain):
    rows = n * T
    return pl.pallas_call(
        functools.partial(forward_kernel, n, rep, T, 4),
        out_shape=(
            shape((T, D), bf16), shape((rows, D), bf16), shape((rows, D), bf16), shape((rows, GROUPS * HD), bf16),
            shape((rows, HD), f32), shape((rows, HD), f32), shape((2, n, HD, HD), bf16), shape((2, NH * rows, HD), bf16),
            shape((2, n, NH * T, NH * T), bf16), shape((rows, HD), bf16),
        ),
        in_specs=[SMEM] * 3 + [VMEM, ANY, VMEM, ANY, VMEM, VMEM, VMEM],
        out_specs=[VMEM, VMEM, ANY] + [VMEM] * 7,
        scratch_shapes=[
            pltpu.VMEM((T, D), bf16), pltpu.VMEM((D, GROUPS * HD), bf16), pltpu.VMEM((D, HD), bf16),
            *forward_scratch(n, T),
            DMA((GROUPS,)), DMA, DMA((n,)), DMA((H,)), *gather_sems(n), *gather_sems(n),
        ],
        compiler_params=pltpu.CompilerParams(vmem_limit_bytes=LIMIT, collective_id=1, has_side_effects=True),
        name="mixer_forward",
    )(lengths, bias, rate, tokens, cotangent, gain_in, w_in, w_small, taps, gain)


def feed_kernel(
    n, T, steps, tokens, gated, cotangent, w_out, gain_mid, w_gate, w_up, w_down,
    result, grad_residual, mid_all, gain_grad, residual, middle, total, grad_mid, own_sem, *sems,
):
    step = pl.program_id(0)
    me = lax.axis_index("seq")
    gather = Gather(n, T, middle, mid_all, sems)
    local = pltpu.make_async_copy(middle, mid_all.at[rows_of(me, T)], own_sem)

    @pl.when(step == 0)
    def _():
        peers = [gather.sib] + [lax.rem(me + 2 * k, n) for k in range(1, n // 2)]
        wait_for_all = greet("seq", peers)
        found = tokens[...].astype(f32) + nn(gated[...], w_out[...])
        residual[...] = found
        middle[...] = (found * norm_scale(found) * gain_mid[...]).astype(bf16)
        total[...] = found
        grad_mid[...] = jnp.zeros((T, D), f32)
        wait_for_all()
        gather.start()
        local.start()

    gate, up = nn(middle[...], w_gate[...]), nn(middle[...], w_up[...])
    sig = sigmoid(gate)
    silu = gate * sig
    hidden = (silu * up).astype(bf16)
    total[...] += nn(hidden, w_down[...])
    grad_hidden = nt(cotangent[...], w_down[...])
    grad_gate = (grad_hidden * up * (sig * (1.0 + gate * (1.0 - sig)))).astype(bf16)
    grad_up = (grad_hidden * silu).astype(bf16)
    grad_mid[...] += nt(grad_gate, w_gate[...]) + nt(grad_up, w_up[...])

    @pl.when(step == steps - 2)
    def _():
        gather.forward()

    @pl.when(step == steps - 1)
    def _():
        result[...] = total[...].astype(bf16)
        values = residual[...]
        back, gain_part = norm_back(values, norm_scale(values), gain_mid[...], grad_mid[...])
        gain_grad[...] = gain_part
        grad_residual[...] = cotangent[...].astype(f32) + back
        gather.direct(0).wait_recv()
        for k in range(1, n // 2):
            gather.passed(k).wait_recv()
        gather.finish()
        local.wait()


def run_feed(n, T, tokens, gated, cotangent, w_out, gain_mid, w_gate_up, w_down):
    steps = FF // TILE
    fixed = lambda *dims: pl.BlockSpec(dims, lambda i: (0, 0))
    return pl.pallas_call(
        functools.partial(feed_kernel, n, T, steps),
        grid=(steps,),
        out_shape=(shape((T, D), bf16), shape((T, D), f32), shape((n * T, D), bf16), shape((1, D), f32)),
        in_specs=[
            fixed(T, D), fixed(T, D), fixed(T, D), fixed(D, D), fixed(1, D),
            pl.BlockSpec((D, TILE), lambda i: (0, i)), pl.BlockSpec((D, TILE), lambda i: (0, i + FF // TILE)),
            pl.BlockSpec((TILE, D), lambda i: (i, 0)),
        ],
        out_specs=[fixed(T, D), fixed(T, D), ANY, fixed(1, D)],
        scratch_shapes=[
            pltpu.VMEM((T, D), f32), pltpu.VMEM((T, D), bf16), pltpu.VMEM((T, D), f32), pltpu.VMEM((T, D), f32),
            DMA, *gather_sems(n),
        ],
        compiler_params=pltpu.CompilerParams(vmem_limit_bytes=LIMIT, collective_id=2, has_side_effects=True),
        name="feed_forward",
    )(tokens, gated, cotangent, w_out, gain_mid, w_gate_up, w_gate_up, w_down)


def store_pieces(out, part, first, stream, piece):
    for i in range(part.shape[0] // piece):
        at = first // piece + i
        out[at % stream, at // stream] = part[i * piece : (i + 1) * piece].astype(bf16)


def backward_turn(
    n, T, starts, bias, rate, taps, gain, incoming_of, proj, small, mixed_in, states, news, invs,
    gp, grad_small, gconv_w, staged, xbuf, halo, gates_sum, grad_state, done, k, _,
):
    width = MIXED * HD
    lane = iota((T, HD), 1)
    place_i, place_j = iota((T, T), 0), iota((T, T), 1)
    upper = (place_j >= place_i).astype(bf16)
    under = place_j < place_i
    c = n - 1 - k
    first = pl.multiple_of(c * T, T)
    at, two = rows_of(c, T), rows_of(c, NH * T)
    gate = chunk_gates(small[at, :], bias, rate, starts, first, T)
    block = xbuf[pl.ds(first, T + 8), :]
    conv, sig, query, keys, values, scales = chunk_inputs(block, taps, gate["docs"], T)
    key_pair, query_pair = halves(keys), halves(query)
    b, hd, hd2, to_end = gate["b"], gate["hd"], gate["hd2"], gate["to_end"]
    decay2 = beside(gate["decay"], gate["decay"])
    pairs = nt(key_pair, key_pair) * gate["decays"]
    scores = nt(query_pair, key_pair) * decay2
    state = (states[0, c], states[1, c])
    state_grad = grad_state[...]
    new = kept(news, two)
    inverse = (invs[0, c], invs[1, c])
    mixed = mixed_in[at, :]
    raw = proj[at, width:].astype(f32)
    normal, scale, zsig = head_gate(mixed, raw)
    incoming = incoming_of(at)
    passed = incoming * (raw * zsig)
    gates_sum[0:1, :] += jnp.sum(passed * normal, axis=0, keepdims=True)
    grad_z = incoming * (normal * gain[...]) * (zsig * (1.0 + raw * (1.0 - zsig)))
    e = passed * gain[...]
    grad_mixed = scale * (e - normal * jnp.mean(e * normal, axis=-1, keepdims=True))
    gm = halves(grad_mixed)
    ended = halves(to_end * keys)
    grad_pair = halves(state_grad)
    grad_new = tn(halves(scores), gm) + nn(ended, grad_pair)
    grad_right = tn(inverse, halves(grad_new))
    moved = b * grad_right
    grad_state[...] = gate["whole"] * state_grad + tn(halves(hd * query), gm) - tn(halves(hd2 * keys), halves(moved))
    grad_ended = nt(new, grad_pair)
    grad_scores = nt(gm, new)
    grad_lower = jnp.where(gate["decays"] != 0.0, -nt(halves(grad_right), new), 0.0)
    from_grad = nt(gm, state)
    scored = grad_scores * decay2
    grad_query = hd * from_grad + nn(scored, key_pair[0])
    paired = (b * grad_lower) * gate["decays"]
    keyed = nn(key_pair, state)
    grad_keys = (
        tn(scored, query_pair[0]) + to_end * grad_ended - hd2 * nt(moved, state[0])
        + nn(paired, key_pair[0]) + tn(paired, key_pair[0])
    )
    lower_pairs = grad_lower * pairs
    grad_b = jnp.sum(grad_right * (values - hd2 * keyed), axis=-1, keepdims=True) + jnp.sum(
        lower_pairs, axis=-1, keepdims=True
    )
    four = b * lower_pairs
    both = grad_scores * scores
    joint = (four[:T, :T] + four[:T, T:]) + (four[T:, :T] + four[T:, T:]) + (both[:, :T] + both[:, T:])
    crossing = jnp.sum(jnp.where(under, nn_exact(upper, joint), 0.0), axis=-1, keepdims=True)
    start_part = -hd2 * jnp.sum(moved * keyed, axis=-1, keepdims=True)
    start_part = start_part[:T] + start_part[T:] + hd * jnp.sum(query * from_grad, axis=-1, keepdims=True)
    end_part = to_end * jnp.sum(grad_ended * keys, axis=-1, keepdims=True)
    end_part = end_part[:T] + end_part[T:]
    sums_in = jnp.where(lane == 0, start_part, jnp.where(lane == 1, end_part, 0.0))
    after = nn_exact(upper, sums_in)
    before = nn_exact(under.astype(bf16), sums_in)
    whole_part = gate["whole"] * jnp.sum(state_grad * (state[0].astype(f32) + state[1].astype(f32)), keepdims=True)
    grad_gate = crossing + after[:, 0:1] + before[:, 1:2] + whole_part
    beta = gate["beta"]
    grad_beta = jnp.where(lane == 0, grad_b[:T], grad_b[T:]) * (beta * (1.0 - 0.5 * beta))
    grad_decay = -grad_gate * rate * sigmoid(gate["shifted"])
    grad_logits = jnp.where(lane < NH, grad_beta, jnp.where(lane == NH, grad_decay, 0.0))
    gates_sum[1:2, :] += jnp.sum(grad_logits, axis=0, keepdims=True)
    gates_sum[2:3, :] += jnp.sum(
        jnp.where(lane == NH, grad_gate * -softplus(gate["shifted"]), 0.0), axis=0, keepdims=True
    )
    high, low_part = halves(grad_logits)
    grad_small[at, :] = (high.astype(f32) + pltpu.roll(low_part.astype(f32), SMALL, 1)).astype(bf16)
    projected_out = jnp.sum(keys * grad_keys, axis=-1, keepdims=True)
    grad_raw = (grad_keys - keys * projected_out) * scales
    slope = sig * (1.0 + conv * (1.0 - sig))
    grad_active = jnp.concatenate([grad_query, grad_raw[:T], grad_raw[T:], moved[:T], moved[T:]], axis=1)
    grad_conv = grad_active * slope
    after_block = stack2(grad_conv, halo[...])
    halo[...] = grad_conv[:8]
    position = first + iota((T, 1), 0)
    total = grad_conv * taps[CONV - 1 : CONV]
    taps_grads = [None] * CONV
    taps_grads[CONV - 1] = jnp.sum(grad_conv * block[8:], axis=0, keepdims=True)
    for lag in range(1, CONV):
        same = (doc_at(starts, position + lag) == gate["docs"][0]).astype(f32)
        total = total + after_block[lag : lag + T] * (taps[CONV - 1 - lag : CONV - lag] * same)
        same = (gate["docs"][lag] == gate["docs"][0]).astype(f32)
        taps_grads[CONV - 1 - lag] = jnp.sum(
            grad_conv * (block[8 - lag : 8 - lag + T] * same), axis=0, keepdims=True
        )
    everything = beside(total, grad_z).astype(bf16)
    gp[at, :] = everything
    for i in range(GROUPS):
        staged[c, i] = everything[:, i * HD : (i + 1) * HD]
    gconv_w[...] += jnp.concatenate(taps_grads, axis=0)
    done(c)
    return 0


def exchange(own, arrived, k, send, receive, axis, me, size):
    peer = lax.rem(me + k, size)
    return remote(own.at[peer], arrived.at[k - 1], send.at[k - 1], receive.at[k - 1], axis, peer)


def scatter_to(own, arrived, k, send, receive, me, size):
    peer = lax.rem(me + k, size)
    return remote(own.at[peer], arrived.at[me], send.at[k - 1], receive.at[k - 1], "seq", peer)


def back_kernel(
    n, m, rep, T, piece, shard, wide,
    lengths, bias_ref, rate_ref, tokens, grad_residual, gain_in, gain_mid_grad, w_small, taps_ref, gain,
    mid_any, out_any, w_gate_up, w_down, w_out, proj_any, small_any, mixed_any, states_any, news_any, invs_any,
    normed_any, rows_any, w_in_any,
    grad_input, g_in, g_out, g_gate_up, g_down, g_gain_in, g_gain_mid, g_small, g_bias, g_rate, g_taps, g_gain_head,
    mid, cot, w_gate, w_up, w_hid, w_head, proj, small, mixed, states, news, invs, normed, head_rows, w_in,
    low_all, hidden, grad_gate, grad_up, gp, grad_small, staged, back, back_small, gconv_w, xbuf, halo, gates_sum, grad_state,
    z_gu, z_gu_in, z_down, z_down_in, z_out, z_out_in, z_w, z_w_in, z_sum, z_sum_in, q_gu, q_gu_in, q_w, q_w_in, q_sum,
    l_sems, own_sems, gu_ss, gu_rs, down_ss, down_rs, out_ss, out_rs, w_ss, w_rs, sum_ss, sum_rs,
    qgu_ss, qgu_rs, qw_ss, qw_rs, qsum_ss, qsum_rs, p_ss, p_rs, s_ss, s_rs, *sems,
):
    me, my = lax.axis_index("seq"), lax.axis_index("stream")
    head = me // rep
    barrier = pltpu.get_barrier_semaphore()
    for k in range(1, n):
        pl.semaphore_signal(barrier, inc=1, device_id={"seq": lax.rem(me + k, n)}, device_id_type=MESH)
    for k in range(1, m):
        pl.semaphore_signal(barrier, inc=1, device_id={"stream": lax.rem(my + k, m)}, device_id_type=MESH)
    first_unit = me * shard
    base = (first_unit // HD - me // (n - 1)) * HD
    offset = first_unit - base
    sources = [
        mid_any, out_any, w_gate_up.at[:, pl.ds(pl.multiple_of(base, HD), wide)],
        w_gate_up.at[:, pl.ds(pl.multiple_of(FF + base, HD), wide)], w_down.at[pl.ds(pl.multiple_of(base, HD), wide)],
        w_out.at[rows_of(head, HD)], rows_any, proj_any, small_any, mixed_any, states_any, news_any, invs_any, normed_any, w_in_any,
    ]
    places = [mid, cot, w_gate, w_up, w_hid, w_head, head_rows, proj, small, mixed, states, news, invs, normed, w_in]
    roomy = len(w_in.shape) == 2
    loads = [pltpu.make_async_copy(a, b, l_sems.at[i]) for i, (a, b) in enumerate(zip(sources, places)) if i < 13 or roomy]
    for load in loads:
        load.start()
    low_all[rows_of(me, T), :] = grad_residual[...].astype(bf16)
    pl.semaphore_wait(barrier, n + m - 2)
    gather = Gather(n, T, low_all.at[rows_of(me, T)], low_all, sems)
    gather.start()

    for load in loads[:5]:
        load.wait()

    def feed_turn(i, _):
        at = rows_of(i, TILE)
        block = mid[at, :]
        gate, up = nn(block, w_gate[...]), nn(block, w_up[...])
        sig = sigmoid(gate)
        silu = gate * sig
        grad_hidden = nt(cot[at, :], w_hid[...])
        own = lambda x: pltpu.roll(x, wide - offset, 1)[:, :shard].astype(bf16)
        hidden[at, :] = own(silu * up)
        grad_gate[at, :] = own(grad_hidden * up * (sig * (1.0 + gate * (1.0 - sig))))
        grad_up[at, :] = own(grad_hidden * silu)
        return 0

    lax.fori_loop(0, n * T // TILE, feed_turn, 0)
    part = tn(hidden[...], cot[...])
    for d in range(m):
        z_down[d] = part[d * (shard // m) : (d + 1) * (shard // m)].astype(bf16)
    downs = [exchange(z_down, z_down_in, k, down_ss, down_rs, "stream", my, m) for k in range(1, m)]
    for copy in downs:
        copy.start()
    gather.forward()
    for first in range(0, D, TILE):
        block = mid[:, first : first + TILE]
        store_pieces(z_gu.at[0], tn(block, grad_gate[...]), first, m, piece)
        store_pieces(z_gu.at[1], tn(block, grad_up[...]), first, m, piece)
    ups = [exchange(z_gu.at[i], z_gu_in.at[i], k, gu_ss.at[i], gu_rs.at[i], "stream", my, m) for i in range(2) for k in range(1, m)]
    for copy in ups:
        copy.start()
    gather.direct(0).wait_recv()
    for k in range(1, n // 2):
        gather.passed(k).wait_recv()
    gather.finish()
    for load in loads[5:]:
        load.wait()
    rows = tn(head_rows[...], low_all[...])
    for share in range(rep):

        @pl.when(lax.rem(me, rep) == share)
        def _():
            for d in range(m):
                at = share * (HD // rep) + d * piece
                z_out[d] = rows[at : at + piece].astype(bf16)

    if not roomy:
        normed = mid
        late = pltpu.make_async_copy(normed_any, normed, l_sems.at[13])
        late.start()
        late.wait()
    outs = [exchange(z_out, z_out_in, k, out_ss, out_rs, "stream", my, m) for k in range(1, m)]
    for copy in outs:
        copy.start()

    width = MIXED * HD
    starts = doc_starts(lengths)
    bias, rate = bias_ref[head], rate_ref[head]
    taps = head_taps(taps_ref, head)
    xbuf[0:8, :] = jnp.zeros((8, width), f32)
    halo[...] = jnp.zeros((8, width), f32)
    gconv_w[...] = jnp.zeros(gconv_w.shape, f32)
    gates_sum[...] = jnp.zeros((8, HD), f32)
    grad_state[...] = jnp.zeros((HD, HD), f32)

    def fill(c, _):
        xbuf[pl.ds(pl.multiple_of(8 + c * T, 8), T), :] = proj[rows_of(c, T), :width].astype(f32)
        return 0

    lax.fori_loop(0, n, fill, 0)
    turn = functools.partial(
        backward_turn, n, T, starts, bias, rate, taps, gain, lambda at: nt(low_all[at, :], w_head[...]),
        proj, small, mixed, states, news, invs, gp, grad_small, gconv_w, staged, xbuf, halo, gates_sum, grad_state,
        lambda c: None,
    )
    lax.fori_loop(0, n, turn, 0)

    column = pl.ds(pl.multiple_of(head * HD, HD), HD)

    def big_copy(c):
        return remote(staged.at[c], back.at[:, :, column], p_ss.at[c], p_rs.at[head], "seq", c)

    def small_copy(c):
        return remote(grad_small.at[rows_of(c, T)], back_small.at[head], s_ss.at[c], s_rs.at[head], "seq", c)

    mine = pltpu.make_async_copy(staged.at[me], back.at[:, :, column], own_sems.at[0])
    also = pltpu.make_async_copy(grad_small.at[rows_of(me, T)], back_small.at[head], own_sems.at[1])

    @pl.when(lax.rem(me, rep) == 0)
    def _():
        for k in range(1, n):
            peer = lax.rem(me + k, n)
            big_copy(peer).start()
            small_copy(peer).start()
        mine.start()
        also.start()

    units = TILE // (piece * m)
    ins = []
    for i, first in enumerate(range(0, D, TILE)):
        store_pieces(z_w, tn(normed[:, first : first + TILE], gp[...]), first, m, piece)
        for k in range(1, m):
            peer = lax.rem(my + k, m)
            at = pl.ds(i * units, units)
            ins.append(remote(z_w.at[peer, at], z_w_in.at[k - 1, at], w_ss.at[i, k - 1], w_rs.at[i, k - 1], "stream", peer))
            ins[-1].start()
    small_t = tn(grad_small[...], normed[...])
    small_t = small_t[:SMALL] + small_t[SMALL : 2 * SMALL]

    @pl.when(lax.rem(me, rep) == 0)
    def _():
        mine.wait()
        also.wait()

    for k in range(1, n):
        peer = lax.rem(me + k, n)

        @pl.when(lax.rem(me, rep) == 0)
        def _():
            big_copy(peer).wait_send()
            small_copy(peer).wait_send()

        @pl.when(lax.rem(peer, rep) == 0)
        def _():
            source = peer // rep
            there = pl.ds(pl.multiple_of(source * HD, HD), HD)
            remote(staged.at[me], back.at[:, :, there], p_ss.at[peer], p_rs.at[source], "seq", peer).wait_recv()
            remote(
                grad_small.at[rows_of(me, T)], back_small.at[source], s_ss.at[peer], s_rs.at[source], "seq", peer
            ).wait_recv()

    lane, place = iota((HD, SMALL * H), 0), iota((HD, SMALL * H), 1)
    logits = jnp.zeros((T, SMALL * H), f32)
    for h in range(H):
        picks = ((place >> 3) == jnp.where(lane < SMALL, lane, lane - SMALL)) & (lane < 2 * SMALL) & ((place & (H - 1)) == h)
        logits = logits + nn(back_small[h], picks.astype(bf16))
    total = nt(halves(logits), halves(w_small[...]))
    for i in range(GROUPS):
        if roomy:
            block = w_in[:, i * D : (i + 1) * D]
        else:
            late = pltpu.make_async_copy(w_in_any.at[:, i * D : (i + 1) * D], w_in.at[0], l_sems.at[14])
            late.start()
            late.wait()
            block = w_in[0]
        total = total + nt(back[i], block)
    values = tokens[...].astype(f32)
    part, gain_part = norm_back(values, norm_scale(values), gain_in[...], total)
    grad_input[...] = grad_residual[...] + part

    z_sum[...] = jnp.zeros(z_sum.shape, f32)
    z_sum[0:1, :] = gain_part
    z_sum[1:2, :] = gain_mid_grad[...]
    z_sum[2 : 2 + SMALL, :] = small_t
    z_sum[5 : 5 + CONV, :width] = gconv_w[...]
    z_sum[9:12, :HD] = gates_sum[0:3, :]

    def sum_copy(k):
        peer = lax.rem(my + k, m)
        return remote(z_sum, z_sum_in.at[k - 1], sum_ss.at[k - 1], sum_rs.at[k - 1], "stream", peer)

    for k in range(1, m):
        sum_copy(k).start()

    def added(own, arrived):
        found = own[my].astype(f32)
        for k in range(1, m):
            found = found + arrived[k - 1].astype(f32)
        return found

    for copy in downs:
        copy.wait()
    g_down[...] = added(z_down, z_down_in)
    for copy in ups:
        copy.wait()
    for i in range(2):
        q_gu[i] = added(z_gu.at[i], z_gu_in.at[i]).astype(bf16)
    q_ups = [scatter_to(q_gu.at[i], q_gu_in.at[i], k, qgu_ss.at[i], qgu_rs.at[i], me, n) for i in range(2) for k in range(1, n)]
    for copy in q_ups:
        copy.start()
    for i in range(2):
        q_gu_in[i, me] = q_gu[i, me]
    for copy in outs:
        copy.wait()
    g_out[...] = added(z_out, z_out_in)
    for k in range(1, m):
        sum_copy(k).wait()
    found = z_sum[...]
    for k in range(1, m):
        found = found + z_sum_in[k - 1]
    q_sum[me] = found
    q_sums = [
        remote(q_sum.at[me], q_sum.at[me], qsum_ss.at[k - 1], qsum_rs.at[k - 1], "seq", lax.rem(me + k, n)) for k in range(1, n)
    ]
    for copy in q_sums:
        copy.start()
    for copy in ins:
        copy.wait()
    q_w[...] = added(z_w, z_w_in).astype(bf16)
    q_ins = [scatter_to(q_w, q_w_in, k, qw_ss, qw_rs, me, n) for k in range(1, n)]
    for copy in q_ins:
        copy.start()
    q_w_in[me] = q_w[me]
    for copy in q_ups:
        copy.wait()
    for i in range(2):
        for source in range(n):
            at = i * FF + source * shard
            g_gate_up[:, at : at + shard] = q_gu_in[i, source].astype(f32)
    for copy in q_sums:
        copy.wait()
    g_gain_in[...] = jnp.sum(q_sum[:, 0:1, :], axis=0)
    g_gain_mid[...] = jnp.sum(q_sum[:, 1:2, :], axis=0)
    gain_total = jnp.zeros((1, HD), f32)
    for h in range(H):
        found = q_sum[h * rep]
        for j in range(SMALL):
            g_small[j * H + h : j * H + h + 1, :] = found[2 + j : 3 + j, :]
        for i in range(MIXED):
            g_taps[:, i * D + h * HD : i * D + (h + 1) * HD] = found[5 : 5 + CONV, i * HD : (i + 1) * HD]
        gain_total = gain_total + found[9:10, :HD]
        g_bias[h] = found[10, NH]
        g_rate[h] = found[11, NH]
    g_gain_head[...] = gain_total
    for copy in q_ins:
        copy.wait()
    for h in range(H):
        found = q_w_in[h * rep].astype(f32)
        for i in range(GROUPS):
            g_in[:, i * D + h * HD : i * D + (h + 1) * HD] = found[:, i * HD : (i + 1) * HD]


def run_back(n, m, rep, T, lengths, bias, rate, tokens, grad_residual, gain_in, gain_mid_grad, w_small, taps, gain,
             mid, cot, w_gate_up, w_down, w_out, proj, small, mixed, states, news, invs, normed, head_rows, w_in):
    rows, piece, shard = n * T, D // (n * m), FF // n
    wide = -(-(shard + HD - 1) // HD) * HD
    vm, roomy = pltpu.VMEM, rows <= 1024
    return pl.pallas_call(
        functools.partial(back_kernel, n, m, rep, T, piece, shard, wide),
        out_shape=(
            shape((T, D), f32), shape((piece, GROUPS * D), f32), shape((piece, D), f32), shape((piece, 2 * FF), f32),
            shape((shard // m, D), f32), shape((1, D), f32), shape((1, D), f32), shape((SMALL * H, D), f32),
            shape((H,), f32), shape((H,), f32), shape((CONV, MIXED * D), f32), shape((1, HD), f32),
        ),
        in_specs=[SMEM] * 3 + [VMEM] * 7 + [ANY] * 14,
        out_specs=[VMEM] * 8 + [SMEM] * 2 + [VMEM] * 2,
        scratch_shapes=[
            vm((rows, D), bf16), vm((rows, D), bf16), vm((D, wide), bf16), vm((D, wide), bf16), vm((wide, D), bf16),
            vm((HD, D), bf16), vm((rows, GROUPS * HD), bf16), vm((rows, HD), f32), vm((rows, HD), f32), vm((2, n, HD, HD), bf16),
            vm((2, NH * rows, HD), bf16), vm((2, n, NH * T, NH * T), bf16), vm((rows if roomy else 16, D), bf16),
            vm((rows, HD), bf16), vm((D, GROUPS * D) if roomy else (1, D, D), bf16),
            vm((rows, D), bf16), vm((rows, shard), bf16), vm((rows, shard), bf16), vm((rows, shard), bf16),
            vm((rows, GROUPS * HD), bf16), vm((rows, HD), bf16), vm((n, GROUPS, T, HD), bf16), vm((GROUPS, T, D), bf16),
            vm((H, T, HD), bf16), vm((CONV, MIXED * HD), f32), vm((rows + 8, MIXED * HD), f32), vm((8, MIXED * HD), f32),
            vm((8, HD), f32), vm((HD, HD), f32),
            vm((2, m, n, piece, shard), bf16), vm((2, m - 1, n, piece, shard), bf16),
            vm((m, shard // m, D), bf16), vm((m - 1, shard // m, D), bf16),
            vm((m, piece, D), bf16), vm((m - 1, piece, D), bf16),
            vm((m, n, piece, GROUPS * HD), bf16), vm((m - 1, n, piece, GROUPS * HD), bf16),
            vm((16, D), f32), vm((m - 1, 16, D), f32),
            vm((2, n, piece, shard), bf16), vm((2, n, piece, shard), bf16),
            vm((n, piece, GROUPS * HD), bf16), vm((n, piece, GROUPS * HD), bf16), vm((n, 16, D), f32),
            DMA((15,)), DMA((2,)), DMA((2, m - 1)), DMA((2, m - 1)), DMA((m - 1,)), DMA((m - 1,)), DMA((m - 1,)), DMA((m - 1,)),
            DMA((D // TILE, m - 1)), DMA((D // TILE, m - 1)), DMA((m - 1,)), DMA((m - 1,)),
            DMA((2, n - 1)), DMA((2, n - 1)), DMA((n - 1,)), DMA((n - 1,)), DMA((n - 1,)), DMA((n - 1,)),
            DMA((n,)), DMA((H,)), DMA((n,)), DMA((H,)), *gather_sems(n),
        ],
        compiler_params=pltpu.CompilerParams(vmem_limit_bytes=(60 if roomy else 62) * 1024 * 1024, collective_id=3, has_side_effects=True),
        name="backward",
    )(lengths, bias, rate, tokens, grad_residual, gain_in, gain_mid_grad, w_small, taps, gain,
      mid, cot, w_gate_up, w_down, w_out, proj, small, mixed, states, news, invs, normed, head_rows, w_in)


def on_device(tokens, grad_out, doc_lengths, gain_in, in_weight, small_weight, gate_bias, decay_rate, conv_weight,
              gain_head, out_weight, gain_mid, gate_up_weight, down_weight):
    seq, stream = lax.axis_size("seq"), lax.axis_size("stream")
    rep = seq // H
    T = tokens.shape[1]
    gain = gain_head.reshape(1, HD)
    gain_in, gain_mid = gain_in.reshape(1, D), gain_mid.reshape(1, D)
    rows, cotangent = tokens[0], grad_out[0]
    gated, normed, out_all, proj, small, mixed, states, news, invs, head_rows = run_forward(
        seq, rep, T, doc_lengths, gate_bias, decay_rate, rows, cotangent, gain_in, in_weight, small_weight, conv_weight, gain
    )
    result, grad_residual, mid_all, grad_gain_mid = run_feed(
        seq, T, rows, gated, cotangent, out_weight, gain_mid, gate_up_weight, down_weight
    )
    grad_input, g_in, g_out, g_gate_up, g_down, g_gain_in, g_gain_mid, g_small, g_bias, g_rate, g_taps, g_gain_head = run_back(
        seq, stream, rep, T, doc_lengths, gate_bias, decay_rate, rows, grad_residual, gain_in, grad_gain_mid, small_weight,
        conv_weight, gain, mid_all, out_all, gate_up_weight, down_weight, out_weight, proj, small, mixed, states, news, invs,
        normed, head_rows, in_weight,
    )
    return (
        result[None], grad_input[None], g_gain_in.reshape(D), g_in, g_small.T, g_bias, g_rate, g_taps,
        g_gain_head.reshape(HD), g_out, g_gain_mid.reshape(D), g_gate_up, g_down,
    )


def solution(mesh):
    rows, whole, split = P("stream", "seq", None), P(), P(("seq", "stream"), None)
    return jax.shard_map(
        on_device,
        mesh=mesh,
        in_specs=(rows, rows, P("stream", None)) + (whole,) * 11,
        out_specs=(rows, rows, whole, split, whole, whole, whole, whole, whole, split, whole, split, split),
        check_vma=False,
    )
```

time: 406 us -> 206 us (0.51); the launches traced: 400 us -> 205 us
  Pallas kernels: 46.5 us -> 192 us
  blocking collectives: 91.6 us -> 0 us
  waiting for transfers between devices: 73.6 us -> 0 us
  matrix products: 69.5 us -> 0 us
  local copies, waits for them, and re-layouts: 63.2 us -> 12.4 us
  starting transfers between devices: 26.6 us -> 0 us
  between operations: 16.3 us -> 0.77 us
  other arithmetic: 12.9 us -> 0 us
    pallas_call x2 -> x3, Pallas kernels: 46.5 us -> 192 us  [the longest x1 121 us: run_back(): pl.pallas_call(functools.partial(back_kernel, n, m, rep, T, piece, shard,...]
    all_gather x1 -> x0, blocking collectives: 91.6 us -> none  [on_device(): every = lax.all_gather(flat, ('seq', 'stream'))]
    dot_general x20 -> x0, matrix products: 69.5 us -> none  [the longest x19 67.9 us: mm(): return jnp.einsum(dims, a, b, preferred_element_type=f32)]
    unnamed x8 -> x0, waiting for transfers between devices: 29.1 us -> none
    all_gather x4 -> x0, waiting for transfers between devices: 21.9 us -> none  [the longest x1 18.9 us: on_device(): low_all = lax.all_gather(grad_residual.astype(bf16), 'seq', tiled=True)]
    all_to_all x4 -> x0, starting transfers between devices: 15.7 us -> none  [the longest x1 4.45 us: on_device(): lax.all_to_all(gp.reshape(seq, T, (GROUPS + 1) * HD), 'seq', 0, 0)[::rep]]
    reduce_scatter x2 -> x0, waiting for transfers between devices: 14.3 us -> none  [the longest x1 14.3 us: on_device(): lax.psum_scatter(mm(hidden_s, out_all, 'ji,jk->ik').astype(bf16), 'stream...]
    unnamed x93 -> x36, local copies, waits for them, and re-layouts: 26.4 us -> 12.4 us
  transfers between devices with their start and end apart: 11 -> 0, of which waited for: 7 -> 0; matrix products, arithmetic and copies ran while one was open for 33% -> 0% of each run, Pallas kernels for 12% -> 0%
where the time goes in v2:
time: 206 us; the launch traced here: 205 us
  Pallas kernels  192 us (93%)
  local copies, waits for them, and re-layouts  12.4 us (6%)
    pallas_call x1, Pallas kernels, run_back(): pl.pallas_call(functools.partial(back_kernel, n, m, rep, T, piece, shard,...  121 us
    pallas_call x1, Pallas kernels, run_forward(): pl.pallas_call(functools.partial(forward_kernel, n, rep, T, 4), out_shape...  47.5 us
    pallas_call x1, Pallas kernels, run_feed(): pl.pallas_call(functools.partial(feed_kernel, n, T, steps), grid=(steps,)...  23.6 us
    unnamed x36, local copies, waits for them, and re-layouts  12.4 us

profile of v2, /device:TPU:0, one launch (start us, length us, event | category | flops | bytes accessed | tf_op | source)
XLA Modules:
  0.0 205.1 jit_solution(12360330611430406214)
XLA Ops:
  0.6 1.9 copy.27.w_small
  2.5 47.5 %mixer_forward.1 = (bf16[128,1024]{1,0:T(8,128)(2,1)}, bf16[1024,1024]{1,0:T(8,128)(2,1)}, bf16[1024,1024]{1,0:T(8,128)(2,1)}, bf16[1024,768]{1,0:T(8,128)(2,1)}...) custom-call(s32[1,8]{1,0:T(1,128)} %lengths.3, ...), custom_call_target="tpu_custom_call" | custom-call | tf_op jit(solution)/shard_map/mixer_forward/pallas_call | solution.py:440
  50.0 23.6 %feed_forward.1 = (bf16[128,1024]{1,0:T(8,128)(2,1)}, f32[128,1024]{1,0:T(8,128)}, bf16[1024,1024]{1,0:T(8,128)(2,1)}, f32[1,1024]{1,0:T(1,128)}) custom-call(bf16[128,1024]{1,0:T(8,128)(2,1)} %bitcast.12, bf16[128,1024]{1,0:T(8,128)(2,1)} %get-tuple-element.39.gated, bf16[128,1024]{1,0:T(8,128)(2,1)} %bitcast.15, bf16[1024,1024]{1,0:T(8,128)(2,1)} %w_out.3, ...), custom_call_target="tpu_custom_call" | custom-call | tf_op jit(solution)/shard_map/feed_forward/pallas_call | solution.py:512
  73.7 0.0 copy-start.3
  73.7 120.8 %backward.1 = (f32[128,1024]{1,0:T(8,128)}, f32[32,6144]{1,0:T(8,128)}, f32[32,1024]{1,0:T(8,128)}, f32[32,5632]{1,0:T(8,128)}, f32[88,1024]{1,0:T(8,128)}, /*in...) custom-call(s32[1,8]{1,0:T(1,128)} %lengths.3, ...), custom_call_target="tpu_custom_call" | custom-call | tf_op jit(solution)/shard_map/backward/pallas_call | solution.py:927
  194.5 0.0 copy-start
  194.6 0.0 copy-start.5
  194.6 0.0 copy-start.10
  194.6 0.0 copy-start.9
  194.6 0.0 copy-start.6
  194.6 0.0 copy-start.8
  194.6 0.0 copy-start.4
  194.6 0.0 copy-start.7
  194.6 0.0 copy-start.1
  194.6 0.0 copy-done.3
  194.6 0.7 copy.42
  195.3 1.9 copy.43
  197.3 1.3 copy.44
  198.6 0.0 copy-done
  198.6 0.9 copy.45
  199.4 0.0 copy-done.5
  199.4 0.6 copy.46
  200.1 0.5 copy.47
  200.6 0.5 copy.48
  201.1 0.6 copy.49
  201.8 0.5 copy.50
  202.3 0.0 copy-done.4
  202.3 0.7 copy.51
  202.9 0.6 copy.52
  203.5 0.9 copy.53
  204.4 0.0 copy-done.2
  204.4 0.7 copy.54
  (7 shorter events, 0.0 us)
Async XLA Ops:
  73.7 120.9 %copy-start.3 = (bf16[128,1024]{1,0:T(8,128)(2,1)S(1)}, bf16[128,1024]{1,0:T(8,128)(2,1)}, u32[]{:S(2)}) copy-start(bf16[128,1024]{1,0:T(8,128)(2,1)} %get-tuple-element.40) | copy-start | bytes 786436
  194.5 4.0 %copy-start = (f32[32,6144]{1,0:T(8,128)S(1)}, f32[32,6144]{1,0:T(8,128)}, u32[]{:S(2)}) copy-start(f32[32,6144]{1,0:T(8,128)} %get-tuple-element.81) | copy-start | bytes 2359300
  194.6 4.9 %copy-start.5 = (f32[24,1024]{1,0:T(8,128)S(1)}, f32[24,1024]{1,0:T(8,128)}, u32[]{:S(2)}) copy-start(f32[24,1024]{1,0:T(8,128)} %get-tuple-element.56) | copy-start | bytes 294916
  194.6 5.5 %copy-start.10 = (f32[8]{0:T(128)S(1)}, f32[8]{0:T(128)}, u32[]{:S(2)}) copy-start(f32[8]{0:T(128)} %get-tuple-element.83) | copy-start | bytes 100
  194.6 6.0 %copy-start.9 = (f32[8]{0:T(128)S(1)}, f32[8]{0:T(128)}, u32[]{:S(2)}) copy-start(f32[8]{0:T(128)} %get-tuple-element.84) | copy-start | bytes 100
  194.6 6.5 %copy-start.6 = (f32[4,5120]{1,0:T(4,128)S(1)}, f32[4,5120]{1,0:T(4,128)}, u32[]{:S(2)}) copy-start(f32[4,5120]{1,0:T(4,128)} %get-tuple-element.85) | copy-start | bytes 245764
  194.6 7.2 %copy-start.8 = (f32[1,128]{1,0:T(1,128)S(1)}, f32[1,128]{1,0:T(1,128)}, u32[]{:S(2)}) copy-start(f32[1,128]{1,0:T(1,128)} %get-tuple-element.60) | copy-start | bytes 1540
  194.6 7.7 %copy-start.4 = (f32[32,1024]{1,0:T(8,128)S(1)}, f32[32,1024]{1,0:T(8,128)}, u32[]{:S(2)}) copy-start(f32[32,1024]{1,0:T(8,128)} %get-tuple-element.87) | copy-start | bytes 393220
  194.6 8.3 %copy-start.7 = (f32[1,1024]{1,0:T(1,128)S(1)}, f32[1,1024]{1,0:T(1,128)}, u32[]{:S(2)}) copy-start(f32[1,1024]{1,0:T(1,128)} %get-tuple-element.62) | copy-start | bytes 12292
  194.6 8.9 %copy-start.1 = (f32[32,5632]{1,0:T(8,128)S(1)}, f32[32,5632]{1,0:T(8,128)}, u32[]{:S(2)}) copy-start(f32[32,5632]{1,0:T(8,128)} %get-tuple-element.89) | copy-start | bytes 2162692
  195.3 9.0 %copy-start.2 = (f32[88,1024]{1,0:T(8,128)S(1)}, f32[88,1024]{1,0:T(8,128)}, u32[]{:S(2)}) copy-start(f32[88,1024]{1,0:T(8,128)} %get-tuple-element.90) | copy-start | bytes 1081348

commit v3 on v2

--- a/solution.py
+++ b/solution.py
@@ -535,8 +535,8 @@
 
 
 def backward_turn(
-    n, T, starts, bias, rate, taps, gain, incoming_of, proj, small, mixed_in, states, news, invs,
-    gp, grad_small, gconv_w, staged, xbuf, halo, gates_sum, grad_state, done, k, _,
+    n, T, head, starts, bias, rate, taps, gain, incoming_of, proj, small, states, fetch,
+    gp, grad_small, gconv_w, xbuf, halo, gates_sum, grad_state, done, k, _,
 ):
     width = MIXED * HD
     lane = iota((T, HD), 1)
@@ -556,9 +556,7 @@
     scores = nt(query_pair, key_pair) * decay2
     state = (states[0, c], states[1, c])
     state_grad = grad_state[...]
-    new = kept(news, two)
-    inverse = (invs[0, c], invs[1, c])
-    mixed = mixed_in[at, :]
+    new, inverse, mixed = fetch(c)
     raw = proj[at, width:].astype(f32)
     normal, scale, zsig = head_gate(mixed, raw)
     incoming = incoming_of(at)
@@ -603,16 +601,18 @@
     before = nn_exact(under.astype(bf16), sums_in)
     whole_part = gate["whole"] * jnp.sum(state_grad * (state[0].astype(f32) + state[1].astype(f32)), keepdims=True)
     grad_gate = crossing + after[:, 0:1] + before[:, 1:2] + whole_part
-    beta = gate["beta"]
-    grad_beta = jnp.where(lane == 0, grad_b[:T], grad_b[T:]) * (beta * (1.0 - 0.5 * beta))
-    grad_decay = -grad_gate * rate * sigmoid(gate["shifted"])
-    grad_logits = jnp.where(lane < NH, grad_beta, jnp.where(lane == NH, grad_decay, 0.0))
-    gates_sum[1:2, :] += jnp.sum(grad_logits, axis=0, keepdims=True)
-    gates_sum[2:3, :] += jnp.sum(
-        jnp.where(lane == NH, grad_gate * -softplus(gate["shifted"]), 0.0), axis=0, keepdims=True
-    )
-    high, low_part = halves(grad_logits)
-    grad_small[at, :] = (high.astype(f32) + pltpu.roll(low_part.astype(f32), SMALL, 1)).astype(bf16)
+    shifted = gate["shifted"]
+    grad_beta = [grad_b[i * T : (i + 1) * T] * (gate["beta"][:, i : i + 1] * (1.0 - 0.5 * gate["beta"][:, i : i + 1])) for i in range(NH)]
+    grad_decay = (-grad_gate * rate * sigmoid(shifted))[:, NH : NH + 1]
+    which = lane >> 3
+    logit = jnp.where(which == 0, grad_beta[0], jnp.where(which == 1, grad_beta[1], grad_decay))
+    grad_logits = jnp.where((lane < SMALL * H) & ((lane & (H - 1)) == head), logit, 0.0)
+    gates_sum[1:2, :] += jnp.sum(jnp.where(lane == NH, grad_decay, 0.0), axis=0, keepdims=True)
+    gates_sum[2:3, :] += jnp.sum(jnp.where(lane == NH, grad_gate * -softplus(shifted), 0.0), axis=0, keepdims=True)
+    high = grad_logits.astype(bf16).astype(f32)
+    grad_small[at, :] = (
+        high + pltpu.roll(grad_logits - high, SMALL * H, 1) + pltpu.roll(high, 2 * SMALL * H, 1)
+    ).astype(bf16)
     projected_out = jnp.sum(keys * grad_keys, axis=-1, keepdims=True)
     grad_raw = (grad_keys - keys * projected_out) * scales
     slope = sig * (1.0 + conv * (1.0 - sig))
@@ -633,16 +633,126 @@
         )
     everything = beside(total, grad_z).astype(bf16)
     gp[at, :] = everything
-    for i in range(GROUPS):
-        staged[c, i] = everything[:, i * HD : (i + 1) * HD]
     gconv_w[...] += jnp.concatenate(taps_grads, axis=0)
-    done(c)
+    done(k)
     return 0
 
 
-def exchange(own, arrived, k, send, receive, axis, me, size):
-    peer = lax.rem(me + k, size)
-    return remote(own.at[peer], arrived.at[k - 1], send.at[k - 1], receive.at[k - 1], axis, peer)
+class Chain:
+    def __init__(self, own, up_in, down_in, sems, my, m):
+        self.own, self.up_in, self.down_in = own, up_in, down_in
+        self.us, self.ur, self.ds, self.dr = sems
+        self.my, self.m = my, m
+
+    def up(self, q):
+        slot = q - self.my
+        return self.own(self.my + self.m - 1 - q), self.up_in(slot), slot, self.my + 1, self.us, self.ur
+
+    def down(self, q):
+        slot = q - (self.m - 1 - self.my)
+        return self.own(self.my - (self.m - 1 - q)), self.down_in(slot), slot, self.my - 1, self.ds, self.dr
+
+    def copy(self, hop):
+        own, arrived, slot, peer, send, receive = hop
+        return remote(own, arrived, send.at[slot], receive.at[slot], "stream", peer)
+
+    def start(self):
+        for q in range(self.m - 1):
+
+            @pl.when(self.my == 0)
+            def _():
+                self.copy(self.up(q)).start()
+
+            @pl.when(self.my == self.m - 1)
+            def _():
+                self.copy(self.down(q)).start()
+
+    def tick(self, q):
+        for inner, way in (
+            ((self.my > 0) & (self.my <= q), self.up),
+            ((self.my < self.m - 1) & (self.my >= self.m - 1 - q), self.down),
+        ):
+
+            @pl.when(inner)
+            def _():
+                hop = way(q)
+                self.copy(hop).wait_recv()
+                hop[0][...] = (hop[0][...].astype(f32) + hop[1][...].astype(f32)).astype(bf16)
+                self.copy(hop).start()
+
+    def finish(self, write):
+        last = self.m - 1
+
+        @pl.when(self.my > 0)
+        def _():
+            slot = last - self.my
+            remote(self.own(self.my), self.up_in(slot), self.us.at[slot], self.ur.at[slot], "stream", self.my - 1).wait_recv()
+
+        @pl.when(self.my < last)
+        def _():
+            slot = self.my
+            remote(self.own(self.my), self.down_in(slot), self.ds.at[slot], self.dr.at[slot], "stream", self.my + 1).wait_recv()
+
+        mine = self.own(self.my)
+
+        @pl.when((self.my > 0) & (self.my < last))
+        def _():
+            write(mine[...].astype(f32) + self.up_in(last - self.my)[...].astype(f32) + self.down_in(self.my)[...].astype(f32))
+
+        @pl.when(self.my == last)
+        def _():
+            write(mine[...].astype(f32) + self.up_in(0)[...].astype(f32))
+
+        @pl.when(self.my == 0)
+        def _():
+            write(mine[...].astype(f32) + self.down_in(0)[...].astype(f32))
+
+    def settle(self):
+        for q in range(self.m - 1):
+
+            @pl.when(self.my <= q)
+            def _():
+                self.copy(self.up(q)).wait_send()
+
+            @pl.when(self.my >= self.m - 1 - q)
+            def _():
+                self.copy(self.down(q)).wait_send()
+
+
+class Sums:
+    def __init__(self, own, arrived, every, sems, me, my, n, m):
+        self.own, self.arrived, self.every = own, arrived, every
+        self.zs, self.zr, self.ss, self.rs = sems
+        self.me, self.my, self.n, self.m = me, my, n, m
+
+    def across(self, k):
+        peer = lax.rem(self.my + k, self.m)
+        return remote(self.own, self.arrived.at[k - 1], self.zs.at[k - 1], self.zr.at[k - 1], "stream", peer)
+
+    def along(self, k):
+        block = self.every.at[self.me]
+        return remote(block, block, self.ss.at[k - 1], self.rs.at[k - 1], "seq", lax.rem(self.me + k, self.n))
+
+    def start(self):
+        for k in range(1, self.m):
+            self.across(k).start()
+
+    def add(self):
+        total = self.own[...]
+        for k in range(1, self.m):
+            self.across(k).wait()
+            total = total + self.arrived[k - 1]
+        self.every[self.me] = total
+        for k in range(1, self.n):
+            self.along(k).start()
+
+    def settle(self):
+        for k in range(1, self.n):
+            self.along(k).wait()
+
+
+def chain_sems(*lead):
+    return [DMA(lead) for _ in range(4)]
 
 
 def scatter_to(own, arrived, k, send, receive, me, size):
@@ -653,17 +763,19 @@
 def back_kernel(
     n, m, rep, T, piece, shard, wide,
     lengths, bias_ref, rate_ref, tokens, grad_residual, gain_in, gain_mid_grad, w_small, taps_ref, gain,
-    mid_any, out_any, w_gate_up, w_down, w_out, proj_any, small_any, mixed_any, states_any, news_any, invs_any,
-    normed_any, rows_any, w_in_any,
-    grad_input, g_in, g_out, g_gate_up, g_down, g_gain_in, g_gain_mid, g_small, g_bias, g_rate, g_taps, g_gain_head,
-    mid, cot, w_gate, w_up, w_hid, w_head, proj, small, mixed, states, news, invs, normed, head_rows, w_in,
-    low_all, hidden, grad_gate, grad_up, gp, grad_small, staged, back, back_small, gconv_w, xbuf, halo, gates_sum, grad_state,
-    z_gu, z_gu_in, z_down, z_down_in, z_out, z_out_in, z_w, z_w_in, z_sum, z_sum_in, q_gu, q_gu_in, q_w, q_w_in, q_sum,
-    l_sems, own_sems, gu_ss, gu_rs, down_ss, down_rs, out_ss, out_rs, w_ss, w_rs, sum_ss, sum_rs,
-    qgu_ss, qgu_rs, qw_ss, qw_rs, qsum_ss, qsum_rs, p_ss, p_rs, s_ss, s_rs, *sems,
+    mid_any, out_any, w_gate_up, w_down, w_out, rows_any, proj_any, small_any, mixed_any, states_any, news_any, invs_any,
+    normed_any, w_in_any,
+    grad_input, q_w_in, g_out, q_gu_in, g_down, q_sum, r_sum,
+    mid, cot, w_gate, w_up, w_hid, w_head, head_rows, proj, small, mixed, states, news, invs, normed, w_in, w_wide,
+    low_all, hidden, grad_gate, grad_up, gp, grad_small, gconv_w, xbuf, halo, gates_sum, grad_state,
+    z_gu, z_gu_up, z_gu_down, z_down, z_down_up, z_down_down, z_out, z_out_up, z_out_down, z_w, z_w_up, z_w_down,
+    z_sum, z_sum_in, y_sum, y_sum_in, q_gu, q_w, part_own, part_out, part_in, chip_out, chip_in,
+    l_sems, i_sems, gu_us, gu_ur, gu_ds, gu_dr, dn_us, dn_ur, dn_ds, dn_dr, ou_us, ou_ur, ou_ds, ou_dr, w_us, w_ur, w_ds, w_dr,
+    sum_ss, sum_rs, qgu_ss, qgu_rs, qw_ss, qw_rs, qsum_ss, qsum_rs, p_ss, p_rs, c_ss, c_rs, *sems,
 ):
     me, my = lax.axis_index("seq"), lax.axis_index("stream")
-    head = me // rep
+    head, chip, side = me // rep, me // 2, lax.rem(me, 2)
+    sib = me + 1 - 2 * side
     barrier = pltpu.get_barrier_semaphore()
     for k in range(1, n):
         pl.semaphore_signal(barrier, inc=1, device_id={"seq": lax.rem(me + k, n)}, device_id_type=MESH)
@@ -675,11 +787,14 @@
     sources = [
         mid_any, out_any, w_gate_up.at[:, pl.ds(pl.multiple_of(base, HD), wide)],
         w_gate_up.at[:, pl.ds(pl.multiple_of(FF + base, HD), wide)], w_down.at[pl.ds(pl.multiple_of(base, HD), wide)],
-        w_out.at[rows_of(head, HD)], rows_any, proj_any, small_any, mixed_any, states_any, news_any, invs_any, normed_any, w_in_any,
+        w_out.at[rows_of(head, HD)], rows_any, proj_any, small_any, mixed_any, states_any, news_any, invs_any, normed_any,
     ]
-    places = [mid, cot, w_gate, w_up, w_hid, w_head, head_rows, proj, small, mixed, states, news, invs, normed, w_in]
-    roomy = len(w_in.shape) == 2
-    loads = [pltpu.make_async_copy(a, b, l_sems.at[i]) for i, (a, b) in enumerate(zip(sources, places)) if i < 13 or roomy]
+    places = [mid, cot, w_gate, w_up, w_hid, w_head, head_rows, proj, small, mixed, states, news, invs, normed]
+    roomy = len(normed.shape) == 2
+    loads = [pltpu.make_async_copy(a, b, l_sems.at[i]) for i, (a, b) in enumerate(zip(sources, places)) if i not in (9, 11, 12, 13) or roomy]
+    for i in range(GROUPS):
+        column = pl.ds(pl.multiple_of(i * D + head * HD, HD), HD)
+        loads.append(pltpu.make_async_copy(w_in_any.at[:, column], w_in.at[:, i * HD : (i + 1) * HD], i_sems.at[i]))
     for load in loads:
         load.start()
     low_all[rows_of(me, T), :] = grad_residual[...].astype(bf16)
@@ -704,20 +819,27 @@
         return 0
 
     lax.fori_loop(0, n * T // TILE, feed_turn, 0)
+    downs = Chain(lambda d: z_down.at[d], lambda i: z_down_up.at[i], lambda i: z_down_down.at[i], (dn_us, dn_ur, dn_ds, dn_dr), my, m)
+    ups = [
+        Chain(
+            lambda d, j=j: z_gu.at[j, d], lambda i, j=j: z_gu_up.at[j, i], lambda i, j=j: z_gu_down.at[j, i],
+            (gu_us.at[j], gu_ur.at[j], gu_ds.at[j], gu_dr.at[j]), my, m,
+        )
+        for j in range(2)
+    ]
     part = tn(hidden[...], cot[...])
     for d in range(m):
         z_down[d] = part[d * (shard // m) : (d + 1) * (shard // m)].astype(bf16)
-    downs = [exchange(z_down, z_down_in, k, down_ss, down_rs, "stream", my, m) for k in range(1, m)]
-    for copy in downs:
-        copy.start()
+    downs.start()
     gather.forward()
-    for first in range(0, D, TILE):
-        block = mid[:, first : first + TILE]
-        store_pieces(z_gu.at[0], tn(block, grad_gate[...]), first, m, piece)
-        store_pieces(z_gu.at[1], tn(block, grad_up[...]), first, m, piece)
-    ups = [exchange(z_gu.at[i], z_gu_in.at[i], k, gu_ss.at[i], gu_rs.at[i], "stream", my, m) for i in range(2) for k in range(1, m)]
-    for copy in ups:
-        copy.start()
+    for j, grads in enumerate((grad_gate, grad_up)):
+        for first in range(0, D, TILE):
+            store_pieces(z_gu.at[j], tn(mid[:, first : first + TILE], grads[...]), first, m, piece)
+        ups[j].start()
+    w_wide[...] = jnp.zeros((D, HD), bf16)
+    w_high, w_low = halves(w_small[...])
+    for i, wide_part in enumerate((w_high, w_high, w_low)):
+        w_wide[:, i * SMALL * H : (i + 1) * SMALL * H] = wide_part
     gather.direct(0).wait_recv()
     for k in range(1, n // 2):
         gather.passed(k).wait_recv()
@@ -733,14 +855,13 @@
                 at = share * (HD // rep) + d * piece
                 z_out[d] = rows[at : at + piece].astype(bf16)
 
+    outs = Chain(lambda d: z_out.at[d], lambda i: z_out_up.at[i], lambda i: z_out_down.at[i], (ou_us, ou_ur, ou_ds, ou_dr), my, m)
+    outs.start()
     if not roomy:
         normed = mid
         late = pltpu.make_async_copy(normed_any, normed, l_sems.at[13])
         late.start()
         late.wait()
-    outs = [exchange(z_out, z_out_in, k, out_ss, out_rs, "stream", my, m) for k in range(1, m)]
-    for copy in outs:
-        copy.start()
 
     width = MIXED * HD
     starts = doc_starts(lengths)
@@ -757,207 +878,273 @@
         return 0
 
     lax.fori_loop(0, n, fill, 0)
+
+    def sibling_copy(j):
+        return remote(part_out.at[j], part_in.at[j], p_ss.at[j], p_rs.at[j], "seq", sib)
+
+    def owner_copy(j):
+        return remote(chip_out.at[j], chip_in.at[chip], c_ss.at[j], c_rs.at[chip], "seq", 2 * j + side)
+
+    def form(j):
+        at = rows_of(j, 2 * T)
+        found = nt(gp[at, :], w_in[...]) + nt(grad_small[at, :], w_wide[...])
+        if rep > 1:
+            found = found * (lax.rem(me, rep) == 0).astype(f32)
+        for i in range(2):
+
+            @pl.when(side == i)
+            def _():
+                part_own[j] = found[i * T : (i + 1) * T].astype(part_own.dtype)
+                part_out[j] = found[(1 - i) * T : (2 - i) * T].astype(bf16)
+
+        sibling_copy(j).start()
+
+    def join(j):
+        sibling_copy(j).wait_recv()
+        found = part_own[j].astype(f32) + part_in[j].astype(f32)
+        part_own[j] = found.astype(part_own.dtype)
+        chip_out[j] = found.astype(bf16)
+
+        @pl.when(chip != j)
+        def _():
+            owner_copy(j).start()
+
+    hops = [(chain, q) for chain in (downs, *ups) for q in range(1, m - 1)]
+
+    def after_turn(k):
+        c = n - 1 - k
+
+        @pl.when(lax.rem(k, 2) == 1)
+        def _():
+            form(c // 2)
+
+            @pl.when(k > 1)
+            def _():
+                join(c // 2 + 1)
+
+        for i, (chain, q) in enumerate(hops):
+
+            @pl.when(k == 3 * i // 2)
+            def _():
+                chain.tick(q)
+
+    def fetch(c):
+        if roomy:
+            return kept(news, rows_of(c, NH * T)), (invs[0, c], invs[1, c]), mixed[rows_of(c, T), :]
+        late = [
+            pltpu.make_async_copy(news_any.at[:, rows_of(c, NH * T)], news, l_sems.at[11]),
+            pltpu.make_async_copy(invs_any.at[:, pl.ds(c, 1)], invs, l_sems.at[12]),
+            pltpu.make_async_copy(mixed_any.at[rows_of(c, T)], mixed, l_sems.at[9]),
+        ]
+        for load in late:
+            load.start()
+        for load in late:
+            load.wait()
+        return (news[0], news[1]), (invs[0, 0], invs[1, 0]), mixed[...]
+
     turn = functools.partial(
-        backward_turn, n, T, starts, bias, rate, taps, gain, lambda at: nt(low_all[at, :], w_head[...]),
-        proj, small, mixed, states, news, invs, gp, grad_small, gconv_w, staged, xbuf, halo, gates_sum, grad_state,
-        lambda c: None,
+        backward_turn, n, T, head, starts, bias, rate, taps, gain, lambda at: nt(low_all[at, :], w_head[...]),
+        proj, small, states, fetch, gp, grad_small, gconv_w, xbuf, halo, gates_sum, grad_state, after_turn,
     )
     lax.fori_loop(0, n, turn, 0)
-
-    column = pl.ds(pl.multiple_of(head * HD, HD), HD)
-
-    def big_copy(c):
-        return remote(staged.at[c], back.at[:, :, column], p_ss.at[c], p_rs.at[head], "seq", c)
-
-    def small_copy(c):
-        return remote(grad_small.at[rows_of(c, T)], back_small.at[head], s_ss.at[c], s_rs.at[head], "seq", c)
-
-    mine = pltpu.make_async_copy(staged.at[me], back.at[:, :, column], own_sems.at[0])
-    also = pltpu.make_async_copy(grad_small.at[rows_of(me, T)], back_small.at[head], own_sems.at[1])
-
-    @pl.when(lax.rem(me, rep) == 0)
-    def _():
-        for k in range(1, n):
-            peer = lax.rem(me + k, n)
-            big_copy(peer).start()
-            small_copy(peer).start()
-        mine.start()
-        also.start()
 
     units = TILE // (piece * m)
     ins = []
     for i, first in enumerate(range(0, D, TILE)):
         store_pieces(z_w, tn(normed[:, first : first + TILE], gp[...]), first, m, piece)
-        for k in range(1, m):
-            peer = lax.rem(my + k, m)
-            at = pl.ds(i * units, units)
-            ins.append(remote(z_w.at[peer, at], z_w_in.at[k - 1, at], w_ss.at[i, k - 1], w_rs.at[i, k - 1], "stream", peer))
-            ins[-1].start()
+        at = pl.ds(i * units, units)
+        ins.append(
+            Chain(
+                lambda d, at=at: z_w.at[d, at], lambda j, at=at: z_w_up.at[j, at], lambda j, at=at: z_w_down.at[j, at],
+                (w_us.at[i], w_ur.at[i], w_ds.at[i], w_dr.at[i]), my, m,
+            )
+        )
+        ins[-1].start()
+    join(0)
     small_t = tn(grad_small[...], normed[...])
-    small_t = small_t[:SMALL] + small_t[SMALL : 2 * SMALL]
-
-    @pl.when(lax.rem(me, rep) == 0)
-    def _():
-        mine.wait()
-        also.wait()
-
-    for k in range(1, n):
-        peer = lax.rem(me + k, n)
-
-        @pl.when(lax.rem(me, rep) == 0)
-        def _():
-            big_copy(peer).wait_send()
-            small_copy(peer).wait_send()
-
-        @pl.when(lax.rem(peer, rep) == 0)
-        def _():
-            source = peer // rep
-            there = pl.ds(pl.multiple_of(source * HD, HD), HD)
-            remote(staged.at[me], back.at[:, :, there], p_ss.at[peer], p_rs.at[source], "seq", peer).wait_recv()
-            remote(
-                grad_small.at[rows_of(me, T)], back_small.at[source], s_ss.at[peer], s_rs.at[source], "seq", peer
-            ).wait_recv()
-
-    lane, place = iota((HD, SMALL * H), 0), iota((HD, SMALL * H), 1)
-    logits = jnp.zeros((T, SMALL * H), f32)
-    for h in range(H):
-        picks = ((place >> 3) == jnp.where(lane < SMALL, lane, lane - SMALL)) & (lane < 2 * SMALL) & ((place & (H - 1)) == h)
-        logits = logits + nn(back_small[h], picks.astype(bf16))
-    total = nt(halves(logits), halves(w_small[...]))
-    for i in range(GROUPS):
-        if roomy:
-            block = w_in[:, i * D : (i + 1) * D]
-        else:
-            late = pltpu.make_async_copy(w_in_any.at[:, i * D : (i + 1) * D], w_in.at[0], l_sems.at[14])
-            late.start()
-            late.wait()
-            block = w_in[0]
-        total = total + nt(back[i], block)
+    small_t = small_t[: SMALL * H] + small_t[SMALL * H : 2 * SMALL * H]
+    z_sum[0:1, :] = gain_mid_grad[...]
+    for i in range(SMALL):
+        z_sum[1 + i : 2 + i, :] = jnp.sum(small_t[i * H : (i + 1) * H], axis=0, keepdims=True)
+    z_sum[4:8, :width] = gconv_w[...]
+    for i in range(3):
+        z_sum[4 + i : 5 + i, width : width + HD] = gates_sum[i : i + 1, :]
+    z_sum[7:8, width : width + HD] = jnp.zeros((1, HD), f32)
+    z_sum[4:8, width + HD :] = jnp.zeros((4, D - width - HD), f32)
+    first_sums = Sums(z_sum, z_sum_in, q_sum, (sum_ss.at[0], sum_rs.at[0], qsum_ss.at[0], qsum_rs.at[0]), me, my, n, m)
+    first_sums.start()
+    for i, (chain, q) in enumerate(hops):
+        if 3 * i // 2 >= n:
+            chain.tick(q)
+
+    def write_down(x):
+        g_down[...] = x
+
+    def write_out(x):
+        g_out[...] = x
+
+    downs.finish(write_down)
+    q_ups = []
+    for j in range(2):
+
+        def write_up(x, j=j):
+            q_gu[j] = x.astype(bf16)
+
+        ups[j].finish(write_up)
+        q_ups += [scatter_to(q_gu.at[j], q_gu_in.at[j], k, qgu_ss.at[j], qgu_rs.at[j], me, n) for k in range(1, n)]
+    for copy in q_ups:
+        copy.start()
+    for j in range(2):
+        q_gu_in[j, me] = q_gu[j, me]
+    for q in range(1, m - 1):
+        outs.tick(q)
+    for chain in ins[:2]:
+        for q in range(1, m - 1):
+            chain.tick(q)
+    first_sums.add()
+
+    total = part_own[chip].astype(f32)
+    for k in range(1, n // 2):
+        other = lax.rem(chip + k, n // 2)
+        remote(chip_out.at[other], chip_in.at[other], c_ss.at[other], c_rs.at[other], "seq", 2 * other + side).wait_recv()
+        total = total + chip_in[other].astype(f32)
     values = tokens[...].astype(f32)
     part, gain_part = norm_back(values, norm_scale(values), gain_in[...], total)
     grad_input[...] = grad_residual[...] + part
 
-    z_sum[...] = jnp.zeros(z_sum.shape, f32)
-    z_sum[0:1, :] = gain_part
-    z_sum[1:2, :] = gain_mid_grad[...]
-    z_sum[2 : 2 + SMALL, :] = small_t
-    z_sum[5 : 5 + CONV, :width] = gconv_w[...]
-    z_sum[9:12, :HD] = gates_sum[0:3, :]
-
-    def sum_copy(k):
-        peer = lax.rem(my + k, m)
-        return remote(z_sum, z_sum_in.at[k - 1], sum_ss.at[k - 1], sum_rs.at[k - 1], "stream", peer)
-
-    for k in range(1, m):
-        sum_copy(k).start()
-
-    def added(own, arrived):
-        found = own[my].astype(f32)
-        for k in range(1, m):
-            found = found + arrived[k - 1].astype(f32)
-        return found
-
-    for copy in downs:
-        copy.wait()
-    g_down[...] = added(z_down, z_down_in)
-    for copy in ups:
-        copy.wait()
-    for i in range(2):
-        q_gu[i] = added(z_gu.at[i], z_gu_in.at[i]).astype(bf16)
-    q_ups = [scatter_to(q_gu.at[i], q_gu_in.at[i], k, qgu_ss.at[i], qgu_rs.at[i], me, n) for i in range(2) for k in range(1, n)]
-    for copy in q_ups:
-        copy.start()
-    for i in range(2):
-        q_gu_in[i, me] = q_gu[i, me]
-    for copy in outs:
-        copy.wait()
-    g_out[...] = added(z_out, z_out_in)
-    for k in range(1, m):
-        sum_copy(k).wait()
-    found = z_sum[...]
-    for k in range(1, m):
-        found = found + z_sum_in[k - 1]
-    q_sum[me] = found
-    q_sums = [
-        remote(q_sum.at[me], q_sum.at[me], qsum_ss.at[k - 1], qsum_rs.at[k - 1], "seq", lax.rem(me + k, n)) for k in range(1, n)
-    ]
-    for copy in q_sums:
-        copy.start()
-    for copy in ins:
-        copy.wait()
-    q_w[...] = added(z_w, z_w_in).astype(bf16)
-    q_ins = [scatter_to(q_w, q_w_in, k, qw_ss, qw_rs, me, n) for k in range(1, n)]
-    for copy in q_ins:
-        copy.start()
+    y_sum[...] = gain_part
+    last_sums = Sums(y_sum, y_sum_in, r_sum, (sum_ss.at[1], sum_rs.at[1], qsum_ss.at[1], qsum_rs.at[1]), me, my, n, m)
+    last_sums.start()
+    q_ins = []
+    for i, chain in enumerate(ins):
+        if i > 1:
+            for q in range(1, m - 1):
+                chain.tick(q)
+        if i == 2:
+            outs.finish(write_out)
+
+        def write_in(x, i=i):
+            q_w[i * units : (i + 1) * units] = x.astype(bf16)
+
+        chain.finish(write_in)
+        for j in range(i * units, (i + 1) * units):
+
+            @pl.when(me != j)
+            def _():
+                remote(q_w.at[j], q_w_in.at[me], qw_ss.at[j], qw_rs.at[me], "seq", j).start()
+
+        if i == 2:
+            last_sums.add()
     q_w_in[me] = q_w[me]
+    for chain in (downs, *ups, outs, *ins):
+        chain.settle()
+
+    def settle(j, _):
+        sibling_copy(j).wait_send()
+
+        @pl.when(chip != j)
+        def _():
+            owner_copy(j).wait_send()
+
+        return 0
+
+    lax.fori_loop(0, n // 2, settle, 0)
+    first_sums.settle()
+    last_sums.settle()
     for copy in q_ups:
         copy.wait()
+    for k in range(1, n):
+        peer = lax.rem(me + k, n)
+        remote(q_w.at[peer], q_w_in.at[me], qw_ss.at[peer], qw_rs.at[me], "seq", peer).wait_send()
+        remote(q_w.at[peer], q_w_in.at[peer], qw_ss.at[peer], qw_rs.at[peer], "seq", peer).wait_recv()
+
+
+def run_back(n, m, rep, T, lengths, bias, rate, tokens, grad_residual, gain_in, gain_mid_grad, w_small, taps, gain,
+             mid, cot, w_gate_up, w_down, w_out, head_rows, proj, small, mixed, states, news, invs, normed, w_in):
+    rows, piece, shard = n * T, D // (n * m), FF // n
+    wide = -(-(shard + HD - 1) // HD) * HD
+    vm, roomy = pltpu.VMEM, rows <= 1024
+    band = GROUPS * HD
+
+    def chained(*dims, lead=()):
+        return [vm((*lead, m, *dims), bf16), vm((*lead, m - 1, *dims), bf16), vm((*lead, m - 1, *dims), bf16)]
+
+    return pl.pallas_call(
+        functools.partial(back_kernel, n, m, rep, T, piece, shard, wide),
+        out_shape=(
+            shape((T, D), f32), shape((n, piece, band), bf16), shape((piece, D), f32), shape((2, n, piece, shard), bf16),
+            shape((shard // m, D), f32), shape((n, 8, D), f32), shape((n, 1, D), f32),
+        ),
+        in_specs=[SMEM] * 3 + [VMEM] * 7 + [ANY] * 14,
+        out_specs=[VMEM] * 7,
+        scratch_shapes=[
+            vm((rows, D), bf16), vm((rows, D), bf16), vm((D, wide), bf16), vm((D, wide), bf16), vm((wide, D), bf16),
+            vm((HD, D), bf16), vm((rows, HD), bf16), vm((rows, band), bf16), vm((rows, HD), f32), vm((rows if roomy else T, HD), f32),
+            vm((2, n, HD, HD), bf16), vm((2, NH * (rows if roomy else T), HD), bf16), vm((2, n if roomy else 1, NH * T, NH * T), bf16),
+            vm((rows, D) if roomy else (1, 16, HD), bf16), vm((D, band), bf16), vm((D, HD), bf16),
+            vm((rows, D), bf16), vm((rows, shard), bf16), vm((rows, shard), bf16), vm((rows, shard), bf16),
+            vm((rows, band), bf16), vm((rows, HD), bf16), vm((CONV, MIXED * HD), f32), vm((rows + 8, MIXED * HD), f32),
+            vm((8, MIXED * HD), f32), vm((8, HD), f32), vm((HD, HD), f32),
+            *chained(n, piece, shard, lead=(2,)), *chained(shard // m, D), *chained(piece, D), *chained(n, piece, band),
+            vm((8, D), f32), vm((m - 1, 8, D), f32), vm((1, D), f32), vm((m - 1, 1, D), f32), vm((2, n, piece, shard), bf16), vm((n, piece, band), bf16),
+            vm((n // 2, T, D), f32 if roomy else bf16), *[vm((n // 2, T, D), bf16)] * 4,
+            DMA((14,)), DMA((GROUPS,)), *chain_sems(2, m - 1), *chain_sems(m - 1), *chain_sems(m - 1),
+            *chain_sems(D // TILE, m - 1), DMA((2, m - 1)), DMA((2, m - 1)), DMA((2, n - 1)), DMA((2, n - 1)), DMA((n,)), DMA((n,)),
+            DMA((2, n - 1)), DMA((2, n - 1)),
+            *[DMA((n // 2,))] * 4, *gather_sems(n),
+        ],
+        compiler_params=pltpu.CompilerParams(vmem_limit_bytes=(60 if roomy else 63) * 1024 * 1024, collective_id=3, has_side_effects=True),
+        name="backward",
+    )(lengths, bias, rate, tokens, grad_residual, gain_in, gain_mid_grad, w_small, taps, gain,
+      mid, cot, w_gate_up, w_down, w_out, head_rows, proj, small, mixed, states, news, invs, normed, w_in)
+
+
+def output_kernel(
+    n, rep, shard, result_in, grad_input_in, w_parts, out_part, gu_parts, down_part, sums, last,
+    result, grad_input, g_in, g_out, g_gate_up, g_down, g_gain_in, g_gain_mid, g_small, g_bias, g_rate, g_taps, g_gain_head,
+):
+    result[...] = result_in[...]
+    grad_input[...] = grad_input_in[...]
+    g_out[...] = out_part[...]
+    g_down[...] = down_part[...]
     for i in range(2):
         for source in range(n):
             at = i * FF + source * shard
-            g_gate_up[:, at : at + shard] = q_gu_in[i, source].astype(f32)
-    for copy in q_sums:
-        copy.wait()
-    g_gain_in[...] = jnp.sum(q_sum[:, 0:1, :], axis=0)
-    g_gain_mid[...] = jnp.sum(q_sum[:, 1:2, :], axis=0)
+            g_gate_up[:, at : at + shard] = gu_parts[i, source].astype(f32)
+    g_gain_in[...] = jnp.sum(last[...], axis=0)
+    g_gain_mid[...] = jnp.sum(sums[:, 0:1, :], axis=0)
+    width = MIXED * HD
     gain_total = jnp.zeros((1, HD), f32)
     for h in range(H):
-        found = q_sum[h * rep]
+        found = sums[h * rep]
+        part = w_parts[h * rep].astype(f32)
         for j in range(SMALL):
-            g_small[j * H + h : j * H + h + 1, :] = found[2 + j : 3 + j, :]
+            g_small[j * H + h : j * H + h + 1, :] = found[1 + j : 2 + j, :]
         for i in range(MIXED):
-            g_taps[:, i * D + h * HD : i * D + (h + 1) * HD] = found[5 : 5 + CONV, i * HD : (i + 1) * HD]
-        gain_total = gain_total + found[9:10, :HD]
-        g_bias[h] = found[10, NH]
-        g_rate[h] = found[11, NH]
+            g_taps[:, i * D + h * HD : i * D + (h + 1) * HD] = found[4 : 4 + CONV, i * HD : (i + 1) * HD]
+        for i in range(GROUPS):
+            g_in[:, i * D + h * HD : i * D + (h + 1) * HD] = part[:, i * HD : (i + 1) * HD]
+        gain_total = gain_total + found[4:5, width : width + HD]
+        g_bias[h] = found[5, width + NH]
+        g_rate[h] = found[6, width + NH]
     g_gain_head[...] = gain_total
-    for copy in q_ins:
-        copy.wait()
-    for h in range(H):
-        found = q_w_in[h * rep].astype(f32)
-        for i in range(GROUPS):
-            g_in[:, i * D + h * HD : i * D + (h + 1) * HD] = found[:, i * HD : (i + 1) * HD]
-
-
-def run_back(n, m, rep, T, lengths, bias, rate, tokens, grad_residual, gain_in, gain_mid_grad, w_small, taps, gain,
-             mid, cot, w_gate_up, w_down, w_out, proj, small, mixed, states, news, invs, normed, head_rows, w_in):
-    rows, piece, shard = n * T, D // (n * m), FF // n
-    wide = -(-(shard + HD - 1) // HD) * HD
-    vm, roomy = pltpu.VMEM, rows <= 1024
+
+
+def run_output(n, rep, *parts):
+    result, grad_input, w_parts, out_part, gu_parts, down_part, sums, last = parts
+    piece, shard = out_part.shape[0], gu_parts.shape[-1]
     return pl.pallas_call(
-        functools.partial(back_kernel, n, m, rep, T, piece, shard, wide),
+        functools.partial(output_kernel, n, rep, shard),
         out_shape=(
-            shape((T, D), f32), shape((piece, GROUPS * D), f32), shape((piece, D), f32), shape((piece, 2 * FF), f32),
-            shape((shard // m, D), f32), shape((1, D), f32), shape((1, D), f32), shape((SMALL * H, D), f32),
-            shape((H,), f32), shape((H,), f32), shape((CONV, MIXED * D), f32), shape((1, HD), f32),
+            shape(result.shape, bf16), shape(grad_input.shape, f32), shape((piece, GROUPS * D), f32), shape((piece, D), f32),
+            shape((piece, 2 * FF), f32), shape(down_part.shape, f32), shape((1, D), f32), shape((1, D), f32),
+            shape((SMALL * H, D), f32), shape((H,), f32), shape((H,), f32), shape((CONV, MIXED * D), f32), shape((1, HD), f32),
         ),
-        in_specs=[SMEM] * 3 + [VMEM] * 7 + [ANY] * 14,
-        out_specs=[VMEM] * 8 + [SMEM] * 2 + [VMEM] * 2,
-        scratch_shapes=[
-            vm((rows, D), bf16), vm((rows, D), bf16), vm((D, wide), bf16), vm((D, wide), bf16), vm((wide, D), bf16),
-            vm((HD, D), bf16), vm((rows, GROUPS * HD), bf16), vm((rows, HD), f32), vm((rows, HD), f32), vm((2, n, HD, HD), bf16),
-            vm((2, NH * rows, HD), bf16), vm((2, n, NH * T, NH * T), bf16), vm((rows if roomy else 16, D), bf16),
-            vm((rows, HD), bf16), vm((D, GROUPS * D) if roomy else (1, D, D), bf16),
-            vm((rows, D), bf16), vm((rows, shard), bf16), vm((rows, shard), bf16), vm((rows, shard), bf16),
-            vm((rows, GROUPS * HD), bf16), vm((rows, HD), bf16), vm((n, GROUPS, T, HD), bf16), vm((GROUPS, T, D), bf16),
-            vm((H, T, HD), bf16), vm((CONV, MIXED * HD), f32), vm((rows + 8, MIXED * HD), f32), vm((8, MIXED * HD), f32),
-            vm((8, HD), f32), vm((HD, HD), f32),
-            vm((2, m, n, piece, shard), bf16), vm((2, m - 1, n, piece, shard), bf16),
-            vm((m, shard // m, D), bf16), vm((m - 1, shard // m, D), bf16),
-            vm((m, piece, D), bf16), vm((m - 1, piece, D), bf16),
-            vm((m, n, piece, GROUPS * HD), bf16), vm((m - 1, n, piece, GROUPS * HD), bf16),
-            vm((16, D), f32), vm((m - 1, 16, D), f32),
-            vm((2, n, piece, shard), bf16), vm((2, n, piece, shard), bf16),
-            vm((n, piece, GROUPS * HD), bf16), vm((n, piece, GROUPS * HD), bf16), vm((n, 16, D), f32),
-            DMA((15,)), DMA((2,)), DMA((2, m - 1)), DMA((2, m - 1)), DMA((m - 1,)), DMA((m - 1,)), DMA((m - 1,)), DMA((m - 1,)),
-            DMA((D // TILE, m - 1)), DMA((D // TILE, m - 1)), DMA((m - 1,)), DMA((m - 1,)),
-            DMA((2, n - 1)), DMA((2, n - 1)), DMA((n - 1,)), DMA((n - 1,)), DMA((n - 1,)), DMA((n - 1,)),
-            DMA((n,)), DMA((H,)), DMA((n,)), DMA((H,)), *gather_sems(n),
-        ],
-        compiler_params=pltpu.CompilerParams(vmem_limit_bytes=(60 if roomy else 62) * 1024 * 1024, collective_id=3, has_side_effects=True),
-        name="backward",
-    )(lengths, bias, rate, tokens, grad_residual, gain_in, gain_mid_grad, w_small, taps, gain,
-      mid, cot, w_gate_up, w_down, w_out, proj, small, mixed, states, news, invs, normed, head_rows, w_in)
+        in_specs=[VMEM] * 8,
+        out_specs=[VMEM] * 9 + [SMEM] * 2 + [VMEM] * 2,
+        compiler_params=pltpu.CompilerParams(vmem_limit_bytes=LIMIT),
+        name="outputs",
+    )(*parts)
 
 
 def on_device(tokens, grad_out, doc_lengths, gain_in, in_weight, small_weight, gate_bias, decay_rate, conv_weight,
@@ -974,10 +1161,13 @@
     result, grad_residual, mid_all, grad_gain_mid = run_feed(
         seq, T, rows, gated, cotangent, out_weight, gain_mid, gate_up_weight, down_weight
     )
-    grad_input, g_in, g_out, g_gate_up, g_down, g_gain_in, g_gain_mid, g_small, g_bias, g_rate, g_taps, g_gain_head = run_back(
+    parts = run_back(
         seq, stream, rep, T, doc_lengths, gate_bias, decay_rate, rows, grad_residual, gain_in, grad_gain_mid, small_weight,
-        conv_weight, gain, mid_all, out_all, gate_up_weight, down_weight, out_weight, proj, small, mixed, states, news, invs,
-        normed, head_rows, in_weight,
+        conv_weight, gain, mid_all, out_all, gate_up_weight, down_weight, out_weight, head_rows, proj, small, mixed, states,
+        news, invs, normed, in_weight,
+    )
+    result, grad_input, g_in, g_out, g_gate_up, g_down, g_gain_in, g_gain_mid, g_small, g_bias, g_rate, g_taps, g_gain_head = (
+        run_output(seq, rep, result, *parts)
     )
     return (
         result[None], grad_input[None], g_gain_in.reshape(D), g_in, g_small.T, g_bias, g_rate, g_taps,

time: 206 us -> 182 us (0.88)
  Pallas kernels: 192 us -> 177 us
  local copies, waits for them, and re-layouts: 12.4 us -> 1.89 us
    pallas_call x1, Pallas kernels: 121 us -> 103 us  [run_back(): pl.pallas_call(functools.partial(back_kernel, n, m, rep, T, piece, shard,...]
    unnamed x36 -> x1, local copies, waits for them, and re-layouts: 12.4 us -> 1.89 us
    pallas_call x0 -> x1, Pallas kernels: none -> 3.34 us  [run_output(): pl.pallas_call(functools.partial(output_kernel, n, rep, shard), out_shape...]
where the time goes in v3:
time: 182 us; the launch traced here: 180 us
  Pallas kernels  177 us (97%)
  local copies, waits for them, and re-layouts  1.89 us (1%)
    pallas_call x1, Pallas kernels, run_back(): pl.pallas_call(functools.partial(back_kernel, n, m, rep, T, piece, shard,...  103 us
    pallas_call x1, Pallas kernels, run_forward(): pl.pallas_call(functools.partial(forward_kernel, n, rep, T, 4), out_shape...  47.4 us
    pallas_call x1, Pallas kernels, run_feed(): pl.pallas_call(functools.partial(feed_kernel, n, T, steps), grid=(steps,)...  23.7 us

profile of v3, /device:TPU:0, one launch (start us, length us, event | category | flops | bytes accessed | tf_op | source)
XLA Modules:
  0.0 180.2 jit_solution(14425857978361044324)
XLA Ops:
  0.6 1.9 %copy.27.w_small = f32[1024,24]{1,0:T(8,128)} copy(f32[1024,24]{0,1:T(8,128)} %param.19) | data formatting | bytes 196608 | tf_op args[5]
  2.5 47.4 %mixer_forward.1 = (bf16[128,1024]{1,0:T(8,128)(2,1)}, bf16[1024,1024]{1,0:T(8,128)(2,1)}, bf16[1024,1024]{1,0:T(8,128)(2,1)}, bf16[1024,768]{1,0:T(8,128)(2,1)}...) custom-call(s32[1,8]{1,0:T(1,128)} %lengths.3, ...), custom_call_target="tpu_custom_call" | custom-call | tf_op jit(solution)/shard_map/mixer_forward/pallas_call | solution.py:440
  50.0 23.7 %feed_forward.1 = (bf16[128,1024]{1,0:T(8,128)(2,1)}, f32[128,1024]{1,0:T(8,128)}, bf16[1024,1024]{1,0:T(8,128)(2,1)}, f32[1,1024]{1,0:T(1,128)}) custom-call(bf16[128,1024]{1,0:T(8,128)(2,1)} %bitcast.12, bf16[128,1024]{1,0:T(8,128)(2,1)} %get-tuple-element.47.gated, bf16[128,1024]{1,0:T(8,128)(2,1)} %bitcast.15, bf16[1024,1024]{1,0:T(8,128)(2,1)} %w_out.3, ...), custom_call_target="tpu_custom_call" | custom-call | tf_op jit(solution)/shard_map/feed_forward/pallas_call | solution.py:512
  73.7 103.0 %backward.1 = (f32[128,1024]{1,0:T(8,128)}, bf16[8,32,768]{2,1,0:T(8,128)(2,1)}, f32[32,1024]{1,0:T(8,128)}, bf16[2,8,32,352]{3,2,1,0:T(8,128)(2,1)}, f32[88,102...) custom-call(s32[1,8]{1,0:T(1,128)} %lengths.3, f32[8]{0:T(128)} %bias_ref.3, f32[8]{0:T(128)} %rate_ref.3, ...), custom_call_target="tpu_custom_call" | custom-call | tf_op jit(solution)/shard_map/backward/pallas_call | solution.py:1072
  176.7 3.3 %outputs.1 = (bf16[128,1024]{1,0:T(8,128)(2,1)}, f32[128,1024]{1,0:T(8,128)}, f32[32,6144]{1,0:T(8,128)}, f32[32,1024]{1,0:T(8,128)}, f32[32,5632]{1,0:T(8,128)}...) custom-call(bf16[128,1024]{1,0:T(8,128)(2,1)} %get-tuple-element.48., ...), custom_call_target="tpu_custom_call" | custom-call | tf_op jit(solution)/shard_map/outputs/pallas_call | solution.py:1136

commit v4 on v3

--- a/solution.py
+++ b/solution.py
@@ -143,32 +143,73 @@
     return pltpu.make_async_remote_copy(src, dst, send, receive, device_id={axis: peer}, device_id_type=MESH)
 
 
+def flipped(chip, bits, chips):
+    total, place = 0, 1
+    while place < chips:
+        total = total + place * lax.rem(chip // place + bits // place, 2)
+        place *= 2
+    return total
+
+
 class Gather:
     def __init__(self, n, T, src, dst, sems):
         self.n, self.T, self.src, self.dst = n, T, src, dst
         self.ss, self.rs, self.fs, self.fr = sems
         self.me = lax.axis_index("seq")
-        self.sib = self.me + 1 - 2 * lax.rem(self.me, 2)
+        self.chip, self.side = self.me // 2, lax.rem(self.me, 2)
+        self.sib = self.me + 1 - 2 * self.side
+        order = sorted(range(1, n // 2), key=lambda k: k.bit_count())
+        self.early = [k for k in order if k.bit_count() == 1]
+        self.late = [k for k in order if k.bit_count() > 1]
 
     def at(self, device):
         return self.dst.at[rows_of(device, self.T)]
 
+    def partner(self, k):
+        return 2 * flipped(self.chip, k, self.n // 2) + self.side
+
     def direct(self, k):
-        peer = self.sib if k == 0 else lax.rem(self.me + 2 * k, self.n)
+        peer = self.sib if k == 0 else self.partner(k)
         return remote(self.src, self.at(self.me), self.ss.at[k], self.rs.at[k], "seq", peer)
 
     def passed(self, k):
-        block = self.at(lax.rem(self.me - 2 * k + self.n, self.n))
+        block = self.at(self.partner(k))
         return remote(block, block, self.fs.at[k], self.fr.at[k], "seq", self.sib)
 
+    def relay(self, k):
+        top = 1 << (k.bit_length() - 1)
+        for side, last in ((0, top), (1, k & -k)):
+
+            @pl.when(self.side == side)
+            def _():
+                block = self.at(self.partner(k - last))
+                remote(block, block, self.ss.at[k], self.rs.at[k], "seq", self.partner(last)).start()
+
     def start(self):
-        for k in (*range(1, self.n // 2), 0):
+        for k in (*self.early, 0):
             self.direct(k).start()
 
+    def pass_on(self, k):
+        self.direct(k).wait_recv()
+        self.passed(k).start()
+
     def forward(self):
+        for k in self.early:
+            self.pass_on(k)
+        for k in self.late:
+            if k.bit_count() == 2:
+                self.relay(k)
+
+    def forward_late(self):
+        for k in self.late:
+            if k.bit_count() > 2:
+                self.relay(k)
+            self.pass_on(k)
+
+    def arrive(self):
+        self.direct(0).wait_recv()
         for k in range(1, self.n // 2):
-            self.direct(k).wait_recv()
-            self.passed(k).start()
+            self.passed(k).wait_recv()
 
     def finish(self):
         for k in range(self.n // 2):
@@ -266,14 +307,12 @@
     return jnp.concatenate(cuts, axis=1)
 
 
-def intra_turn(T, per, starts, bias, rate, taps, small, xbuf, invs, ubuf, wbuf, qbuf, pbuf, dbuf, gates, turn, _):
+def intra_turn(T, starts, bias, rate, taps, small, block_of, invs, ubuf, wbuf, qbuf, pbuf, dbuf, gates, chunks):
     held, lowers = [], []
-    for i in range(per):
-        c = turn * per + i
+    for c in chunks:
         first = pl.multiple_of(c * T, T)
         gate = chunk_gates(small[pl.ds(first, T), :], bias, rate, starts, first, T)
-        block = xbuf[pl.ds(first, T + 8), :]
-        conv, sig, query, keys, values, scales = chunk_inputs(block, taps, gate["docs"], T)
+        conv, sig, query, keys, values, scales = chunk_inputs(block_of(c), taps, gate["docs"], T)
         key_pair = halves(keys)
         lowers.append(gate["b"] * (nt(key_pair, key_pair) * gate["decays"]))
         held.append((c, gate, query, keys, key_pair, values))
@@ -290,7 +329,6 @@
         keep(pbuf, at, nt(query_pair, key_pair) * beside(gate["decay"], gate["decay"]))
         keep(dbuf, two, gate["to_end"] * keys)
         gates[at, :] = jnp.where(iota((T, HD), 1) == 0, gate["hd"], gate["whole"])
-    return 0
 
 
 def across_turn(T, gain, proj, mixed_out, states, news, head_rows, ubuf, wbuf, qbuf, pbuf, dbuf, gates, done, c, state):
@@ -310,14 +348,21 @@
     return gate[0:1, 1:2] * state + tn(kept(dbuf, two), new_pair)
 
 
+def widened(w_wide, parts):
+    w_wide[...] = jnp.zeros((HD, D), bf16)
+    for i, part in enumerate(parts):
+        w_wide[32 * i : 32 * i + SMALL * H, :] = part
+
+
 def forward_kernel(
-    n, rep, T, per, lengths, bias_ref, rate_ref, tokens, cotangent, gain_in, w_in, w_small, taps_ref, gain,
+    n, rep, T, lengths, bias_ref, rate_ref, tokens, cotangent, gain_in, w_in, w_small, taps_ref, gain,
     gated, normed, out_all, proj, small, mixed_out, states, news, invs, head_rows,
-    own, w_head, w_wide, xbuf, ubuf, wbuf, qbuf, pbuf, dbuf, gates,
-    w_sems, own_sem, a_ss, a_rs, *sems,
+    own, tails, w_head, w_wide, tail_rows, xbuf, ubuf, wbuf, qbuf, pbuf, dbuf, gates,
+    w_sems, own_sems, a_ss, a_rs, t_ss, t_rs, *sems,
 ):
     me = lax.axis_index("seq")
     head = me // rep
+    chips = n // 2
     wait_for_all = greet("seq", [lax.rem(me + k, n) for k in range(1, n)])
     width = MIXED * HD
     loads = [
@@ -330,58 +375,105 @@
         load.start()
     values = tokens[...].astype(f32)
     own[...] = (values * norm_scale(values) * gain_in[...]).astype(bf16)
-    local = pltpu.make_async_copy(own, normed.at[rows_of(me, T)], own_sem)
+    local = pltpu.make_async_copy(own, normed.at[rows_of(me, T)], own_sems.at[0])
     local.start()
     wait_for_all()
     first_gather = Gather(n, T, own, normed, sems[:4])
-    first_gather.start()
     second_gather = Gather(n, T, cotangent, out_all, sems[4:8])
+    keep_out = pltpu.make_async_copy(cotangent, out_all.at[rows_of(me, T)], own_sems.at[2])
+    keep_out.start()
+    chip, side = first_gather.chip, first_gather.side
+    last = own.at[T - 16 : T]
+
+    def tail_copy(k):
+        return remote(last, tails.at[chip], t_ss.at[k], t_rs.at[chip], "seq", lax.rem(me + k, n))
+
+    mine = pltpu.make_async_copy(last, tails.at[chip], own_sems.at[1])
+    early, late = first_gather.early, first_gather.late
+
+    @pl.when(side == 1)
+    def _():
+        for k in range(1, n):
+            tail_copy(k).start()
+        mine.start()
+
+    for k in (0, *early):
+        first_gather.direct(k).start()
 
     starts = doc_starts(lengths)
     bias, rate = bias_ref[head], rate_ref[head]
     taps = head_taps(taps_ref, head)
-    xbuf[0:8, :] = jnp.zeros((8, width), f32)
-    w_wide[...] = jnp.zeros((D, HD), bf16)
-    chosen = jnp.where((iota((D, SMALL * H), 1) & (H - 1)) == head, w_small[...], 0.0)
-    for i, piece in enumerate(thirds(chosen)):
-        w_wide[:, i * SMALL * H : (i + 1) * SMALL * H] = piece
-    group = iota((HD, HD), 0) >> 3
-    lane = iota((HD, HD), 1)
-    picks = ((group == lane) | (group == lane + SMALL) | (group == lane + 2 * SMALL)) & (lane < SMALL)
+    widened(w_wide, thirds(jnp.where((iota((SMALL * H, D), 0) & (H - 1)) == head, w_small[...], 0.0)))
+    group, lane = iota((HD, HD), 0), iota((HD, HD), 1)
+    picks = (((group & 31) >> 3) == lane) & (group < 96) & (lane < SMALL)
     picks = picks.astype(bf16)
     for load in loads:
         load.wait()
     local.wait()
-    for k in range(n // 2):
-        if k == 1:
-            first_gather.forward()
-        if k:
-            first_gather.passed(k).wait_recv()
-        else:
-            first_gather.direct(0).wait_recv()
-        at = rows_of(lax.rem(me // 2 - k + n // 2, n // 2), 2 * T)
+
+    @pl.when(side == 1)
+    def _():
+        mine.wait()
+        for k in range(1, n):
+            tail_copy(k).wait_send()
+
+    for j in range(chips):
+
+        @pl.when(me != 2 * j + 1)
+        def _():
+            remote(last, tails.at[j], t_ss.at[0], t_rs.at[j], "seq", lax.rem(me + 1, n)).wait_recv()
+
+    found = nn(tails[...].reshape(chips * 16, D), w_head[...]).astype(bf16).astype(f32)
+    tail_rows[...] = found[:, :width]
+    size = T + 8
+
+    def block_of(c):
+        return xbuf[pl.ds(pl.multiple_of(c * size, 8), size), :]
+
+    def project(pair):
+        at = rows_of(pair, 2 * T)
         block = normed[at, :]
         result = nn(block, w_head[...]).astype(bf16)
         proj[at, :] = result
-        xbuf[pl.ds(pl.multiple_of(8 + lax.rem(me // 2 - k + n // 2, n // 2) * (2 * T), 8), 2 * T), :] = result[:, :width].astype(f32)
-        raw = thirds(nn(block, w_wide[...]))
+        raw = thirds(nt(block, w_wide[...]))
         small[at, :] = nn(raw[0], picks) + (nn(raw[1], picks) + nn(raw[2], picks))
+        mixing = result[:, :width].astype(f32)
+        before = lax.rem(pair + chips - 1, chips)
+        halo = tail_rows[pl.ds(pl.multiple_of(before * 16 + 8, 8), 8), :]
+        base = pl.multiple_of(pair * (2 * size), 8)
+        xbuf[pl.ds(base, 8), :] = jnp.where(pair > 0, halo, 0.0)
+        xbuf[pl.ds(pl.multiple_of(base + 8, 8), T), :] = mixing[:T]
+        xbuf[pl.ds(pl.multiple_of(base + size, 8), T + 8), :] = mixing[T - 8 :]
+
+    first_gather.direct(0).wait_recv()
+    for group in [(0,)] + [(*ks[i : i + 2],) for ks in (early, late) for i in range(0, len(ks), 2)]:
+        if group[0] == early[0]:
+            first_gather.forward()
+        elif late and group[0] == late[0]:
+            first_gather.forward_late()
+            second_gather.start()
+        for k in group:
+            if k:
+                first_gather.passed(k).wait_recv()
+        pairs = [flipped(chip, k, chips) for k in group]
+        for pair in pairs:
+            project(pair)
+        intra_turn(
+            T, starts, bias, rate, taps, small, block_of, invs, ubuf, wbuf, qbuf, pbuf, dbuf, gates,
+            [2 * pair + i for pair in pairs for i in range(2)],
+        )
+
     first_gather.finish()
-    keep = pltpu.make_async_copy(cotangent, out_all.at[rows_of(me, T)], own_sem)
-    keep.start()
-    second_gather.start()
-
-    intra = functools.partial(
-        intra_turn, T, per, starts, bias, rate, taps, small, xbuf, invs, ubuf, wbuf, qbuf, pbuf, dbuf, gates
-    )
-    lax.fori_loop(0, n // per, intra, 0)
-    second_gather.forward()
     column = pl.ds(pl.multiple_of(head * HD, HD), HD)
 
     def row_copy(c):
         return remote(head_rows.at[rows_of(c, T)], gated.at[:, column], a_ss.at[c], a_rs.at[head], "seq", c)
 
     def send_rows(c):
+        @pl.when(c == n // 4)
+        def _():
+            second_gather.forward()
+
         @pl.when((c != me) & (lax.rem(me, rep) == 0))
         def _():
             row_copy(c).start()
@@ -393,14 +485,12 @@
 
     @pl.when(lax.rem(me, rep) == 0)
     def _():
-        mine = pltpu.make_async_copy(head_rows.at[rows_of(me, T)], gated.at[:, column], own_sem)
-        keep.wait()
-        mine.start()
-        mine.wait()
-
-    @pl.when(lax.rem(me, rep) != 0)
-    def _():
-        keep.wait()
+        kept_rows = pltpu.make_async_copy(head_rows.at[rows_of(me, T)], gated.at[:, column], own_sems.at[0])
+        kept_rows.start()
+        kept_rows.wait()
+
+    keep_out.wait()
+    second_gather.forward_late()
 
     def settle(k, _):
         peer = lax.rem(me + k, n)
@@ -420,16 +510,14 @@
         return 0
 
     lax.fori_loop(1, n, settle, 0)
-    second_gather.direct(0).wait_recv()
-    for k in range(1, n // 2):
-        second_gather.passed(k).wait_recv()
+    second_gather.arrive()
     second_gather.finish()
 
 
 def forward_scratch(n, T):
     rows = n * T
     return [
-        pltpu.VMEM((rows + 8, MIXED * HD), f32), pltpu.VMEM((NH * rows, HD), f32),
+        pltpu.VMEM((rows + 8 * n, MIXED * HD), f32), pltpu.VMEM((NH * rows, HD), f32),
         pltpu.VMEM((2, NH * rows, HD), bf16), pltpu.VMEM((2, rows, HD), bf16), pltpu.VMEM((2, rows, NH * T), bf16),
         pltpu.VMEM((2, NH * rows, HD), bf16), pltpu.VMEM((rows, HD), f32),
     ]
@@ -438,18 +526,19 @@
 def run_forward(n, rep, T, lengths, bias, rate, tokens, cotangent, gain_in, w_in, w_small, taps, gain):
     rows = n * T
     return pl.pallas_call(
-        functools.partial(forward_kernel, n, rep, T, 4),
+        functools.partial(forward_kernel, n, rep, T),
         out_shape=(
             shape((T, D), bf16), shape((rows, D), bf16), shape((rows, D), bf16), shape((rows, GROUPS * HD), bf16),
             shape((rows, HD), f32), shape((rows, HD), f32), shape((2, n, HD, HD), bf16), shape((2, NH * rows, HD), bf16),
             shape((2, n, NH * T, NH * T), bf16), shape((rows, HD), bf16),
         ),
-        in_specs=[SMEM] * 3 + [VMEM, ANY, VMEM, ANY, VMEM, VMEM, VMEM],
+        in_specs=[SMEM] * 3 + [VMEM, VMEM, VMEM, ANY, VMEM, VMEM, VMEM],
         out_specs=[VMEM, VMEM, ANY] + [VMEM] * 7,
         scratch_shapes=[
-            pltpu.VMEM((T, D), bf16), pltpu.VMEM((D, GROUPS * HD), bf16), pltpu.VMEM((D, HD), bf16),
+            pltpu.VMEM((T, D), bf16), pltpu.VMEM((n // 2, 16, D), bf16), pltpu.VMEM((D, GROUPS * HD), bf16),
+            pltpu.VMEM((HD, D), bf16), pltpu.VMEM((n * 8, MIXED * HD), f32),
             *forward_scratch(n, T),
-            DMA((GROUPS,)), DMA, DMA((n,)), DMA((H,)), *gather_sems(n), *gather_sems(n),
+            DMA((GROUPS,)), DMA((3,)), DMA((n,)), DMA((H,)), DMA((n,)), DMA((n // 2,)), *gather_sems(n), *gather_sems(n),
         ],
         compiler_params=pltpu.CompilerParams(vmem_limit_bytes=LIMIT, collective_id=1, has_side_effects=True),
         name="mixer_forward",
@@ -467,7 +556,7 @@
 
     @pl.when(step == 0)
     def _():
-        peers = [gather.sib] + [lax.rem(me + 2 * k, n) for k in range(1, n // 2)]
+        peers = [gather.sib] + [gather.partner(k) for k in range(1, n // 2)]
         wait_for_all = greet("seq", peers)
         found = tokens[...].astype(f32) + nn(gated[...], w_out[...])
         residual[...] = found
@@ -488,9 +577,11 @@
     grad_up = (grad_hidden * silu).astype(bf16)
     grad_mid[...] += nt(grad_gate, w_gate[...]) + nt(grad_up, w_up[...])
 
-    @pl.when(step == steps - 2)
-    def _():
-        gather.forward()
+    for at, what in ((5, gather.forward), (8, gather.forward_late)):
+
+        @pl.when(step == at)
+        def _():
+            what()
 
     @pl.when(step == steps - 1)
     def _():
@@ -499,9 +590,7 @@
         back, gain_part = norm_back(values, norm_scale(values), gain_mid[...], grad_mid[...])
         gain_grad[...] = gain_part
         grad_residual[...] = cotangent[...].astype(f32) + back
-        gather.direct(0).wait_recv()
-        for k in range(1, n // 2):
-            gather.passed(k).wait_recv()
+        gather.arrive()
         gather.finish()
         local.wait()
 
@@ -611,7 +700,7 @@
     gates_sum[2:3, :] += jnp.sum(jnp.where(lane == NH, grad_gate * -softplus(shifted), 0.0), axis=0, keepdims=True)
     high = grad_logits.astype(bf16).astype(f32)
     grad_small[at, :] = (
-        high + pltpu.roll(grad_logits - high, SMALL * H, 1) + pltpu.roll(high, 2 * SMALL * H, 1)
+        high + pltpu.roll(grad_logits - high, 32, 1) + pltpu.roll(high, 64, 1)
     ).astype(bf16)
     projected_out = jnp.sum(keys * grad_keys, axis=-1, keepdims=True)
     grad_raw = (grad_keys - keys * projected_out) * scales
@@ -795,7 +884,7 @@
     for i in range(GROUPS):
         column = pl.ds(pl.multiple_of(i * D + head * HD, HD), HD)
         loads.append(pltpu.make_async_copy(w_in_any.at[:, column], w_in.at[:, i * HD : (i + 1) * HD], i_sems.at[i]))
-    for load in loads:
+    for load in loads[:5]:
         load.start()
     low_all[rows_of(me, T), :] = grad_residual[...].astype(bf16)
     pl.semaphore_wait(barrier, n + m - 2)
@@ -804,6 +893,8 @@
 
     for load in loads[:5]:
         load.wait()
+    for load in loads[5:]:
+        load.start()
 
     def feed_turn(i, _):
         at = rows_of(i, TILE)
@@ -833,16 +924,14 @@
     downs.start()
     gather.forward()
     for j, grads in enumerate((grad_gate, grad_up)):
+        if j:
+            gather.forward_late()
         for first in range(0, D, TILE):
             store_pieces(z_gu.at[j], tn(mid[:, first : first + TILE], grads[...]), first, m, piece)
         ups[j].start()
-    w_wide[...] = jnp.zeros((D, HD), bf16)
     w_high, w_low = halves(w_small[...])
-    for i, wide_part in enumerate((w_high, w_high, w_low)):
-        w_wide[:, i * SMALL * H : (i + 1) * SMALL * H] = wide_part
-    gather.direct(0).wait_recv()
-    for k in range(1, n // 2):
-        gather.passed(k).wait_recv()
+    widened(w_wide, (w_high, w_high, w_low))
+    gather.arrive()
     gather.finish()
     for load in loads[5:]:
         load.wait()
@@ -887,7 +976,7 @@
 
     def form(j):
         at = rows_of(j, 2 * T)
-        found = nt(gp[at, :], w_in[...]) + nt(grad_small[at, :], w_wide[...])
+        found = nt(gp[at, :], w_in[...]) + nn(grad_small[at, :], w_wide[...])
         if rep > 1:
             found = found * (lax.rem(me, rep) == 0).astype(f32)
         for i in range(2):
@@ -918,9 +1007,9 @@
         def _():
             form(c // 2)
 
-            @pl.when(k > 1)
-            def _():
-                join(c // 2 + 1)
+        @pl.when((lax.rem(k, 2) == 0) & (k > 0))
+        def _():
+            join((c + 1) // 2)
 
         for i, (chain, q) in enumerate(hops):
 
@@ -948,6 +1037,19 @@
     )
     lax.fori_loop(0, n, turn, 0)
 
+    small_t = tn(grad_small[...], normed[...])
+    small_t = small_t[: SMALL * H] + small_t[32 : 32 + SMALL * H]
+    z_sum[0:1, :] = gain_mid_grad[...]
+    for i in range(SMALL):
+        z_sum[1 + i : 2 + i, :] = jnp.sum(small_t[i * H : (i + 1) * H], axis=0, keepdims=True)
+    z_sum[4:8, :width] = gconv_w[...]
+    for i in range(3):
+        z_sum[4 + i : 5 + i, width : width + HD] = gates_sum[i : i + 1, :]
+    z_sum[7:8, width : width + HD] = jnp.zeros((1, HD), f32)
+    z_sum[4:8, width + HD :] = jnp.zeros((4, D - width - HD), f32)
+    first_sums = Sums(z_sum, z_sum_in, q_sum, (sum_ss.at[0], sum_rs.at[0], qsum_ss.at[0], qsum_rs.at[0]), me, my, n, m)
+    first_sums.start()
+
     units = TILE // (piece * m)
     ins = []
     for i, first in enumerate(range(0, D, TILE)):
@@ -960,19 +1062,8 @@
             )
         )
         ins[-1].start()
-    join(0)
-    small_t = tn(grad_small[...], normed[...])
-    small_t = small_t[: SMALL * H] + small_t[SMALL * H : 2 * SMALL * H]
-    z_sum[0:1, :] = gain_mid_grad[...]
-    for i in range(SMALL):
-        z_sum[1 + i : 2 + i, :] = jnp.sum(small_t[i * H : (i + 1) * H], axis=0, keepdims=True)
-    z_sum[4:8, :width] = gconv_w[...]
-    for i in range(3):
-        z_sum[4 + i : 5 + i, width : width + HD] = gates_sum[i : i + 1, :]
-    z_sum[7:8, width : width + HD] = jnp.zeros((1, HD), f32)
-    z_sum[4:8, width + HD :] = jnp.zeros((4, D - width - HD), f32)
-    first_sums = Sums(z_sum, z_sum_in, q_sum, (sum_ss.at[0], sum_rs.at[0], qsum_ss.at[0], qsum_rs.at[0]), me, my, n, m)
-    first_sums.start()
+        if i == 0:
+            join(0)
     for i, (chain, q) in enumerate(hops):
         if 3 * i // 2 >= n:
             chain.tick(q)
@@ -984,57 +1075,56 @@
         g_out[...] = x
 
     downs.finish(write_down)
-    q_ups = []
     for j in range(2):
 
         def write_up(x, j=j):
-            q_gu[j] = x.astype(bf16)
+            q_gu[:, j] = x.astype(bf16)
 
         ups[j].finish(write_up)
-        q_ups += [scatter_to(q_gu.at[j], q_gu_in.at[j], k, qgu_ss.at[j], qgu_rs.at[j], me, n) for k in range(1, n)]
+    q_ups = [scatter_to(q_gu, q_gu_in, k, qgu_ss, qgu_rs, me, n) for k in range(1, n)]
     for copy in q_ups:
         copy.start()
-    for j in range(2):
-        q_gu_in[j, me] = q_gu[j, me]
+    q_gu_in[me] = q_gu[me]
     for q in range(1, m - 1):
         outs.tick(q)
-    for chain in ins[:2]:
-        for q in range(1, m - 1):
-            chain.tick(q)
-    first_sums.add()
-
-    total = part_own[chip].astype(f32)
-    for k in range(1, n // 2):
-        other = lax.rem(chip + k, n // 2)
-        remote(chip_out.at[other], chip_in.at[other], c_ss.at[other], c_rs.at[other], "seq", 2 * other + side).wait_recv()
-        total = total + chip_in[other].astype(f32)
-    values = tokens[...].astype(f32)
-    part, gain_part = norm_back(values, norm_scale(values), gain_in[...], total)
-    grad_input[...] = grad_residual[...] + part
-
-    y_sum[...] = gain_part
-    last_sums = Sums(y_sum, y_sum_in, r_sum, (sum_ss.at[1], sum_rs.at[1], qsum_ss.at[1], qsum_rs.at[1]), me, my, n, m)
-    last_sums.start()
-    q_ins = []
-    for i, chain in enumerate(ins):
-        if i > 1:
-            for q in range(1, m - 1):
-                chain.tick(q)
-        if i == 2:
-            outs.finish(write_out)
-
-        def write_in(x, i=i):
+    y_sum_in_use = (sum_ss.at[1], sum_rs.at[1], qsum_ss.at[1], qsum_rs.at[1])
+    last_sums = Sums(y_sum, y_sum_in, r_sum, y_sum_in_use, me, my, n, m)
+
+    def input_gradient():
+        total = part_own[chip].astype(f32)
+        for k in range(1, n // 2):
+            other = lax.rem(chip + k, n // 2)
+            remote(chip_out.at[other], chip_in.at[other], c_ss.at[other], c_rs.at[other], "seq", 2 * other + side).wait_recv()
+            total = total + chip_in[other].astype(f32)
+        values = tokens[...].astype(f32)
+        part, gain_part = norm_back(values, norm_scale(values), gain_in[...], total)
+        grad_input[...] = grad_residual[...] + part
+        y_sum[...] = gain_part
+        last_sums.start()
+
+    def deliver(i):
+        def write_in(x):
             q_w[i * units : (i + 1) * units] = x.astype(bf16)
 
-        chain.finish(write_in)
+        ins[i].finish(write_in)
         for j in range(i * units, (i + 1) * units):
 
             @pl.when(me != j)
             def _():
                 remote(q_w.at[j], q_w_in.at[me], qw_ss.at[j], qw_rs.at[me], "seq", j).start()
 
+    first_sums.add()
+    for i, chain in enumerate(ins):
+        for q in range(1, m - 1):
+            chain.tick(q)
+        if i:
+            deliver(i - 1)
+        if i == 1:
+            outs.finish(write_out)
         if i == 2:
-            last_sums.add()
+            input_gradient()
+    deliver(len(ins) - 1)
+    last_sums.add()
     q_w_in[me] = q_w[me]
     for chain in (downs, *ups, outs, *ins):
         chain.settle()
@@ -1072,7 +1162,7 @@
     return pl.pallas_call(
         functools.partial(back_kernel, n, m, rep, T, piece, shard, wide),
         out_shape=(
-            shape((T, D), f32), shape((n, piece, band), bf16), shape((piece, D), f32), shape((2, n, piece, shard), bf16),
+            shape((T, D), f32), shape((n, piece, band), bf16), shape((piece, D), f32), shape((n, 2, piece, shard), bf16),
             shape((shard // m, D), f32), shape((n, 8, D), f32), shape((n, 1, D), f32),
         ),
         in_specs=[SMEM] * 3 + [VMEM] * 7 + [ANY] * 14,
@@ -1081,15 +1171,15 @@
             vm((rows, D), bf16), vm((rows, D), bf16), vm((D, wide), bf16), vm((D, wide), bf16), vm((wide, D), bf16),
             vm((HD, D), bf16), vm((rows, HD), bf16), vm((rows, band), bf16), vm((rows, HD), f32), vm((rows if roomy else T, HD), f32),
             vm((2, n, HD, HD), bf16), vm((2, NH * (rows if roomy else T), HD), bf16), vm((2, n if roomy else 1, NH * T, NH * T), bf16),
-            vm((rows, D) if roomy else (1, 16, HD), bf16), vm((D, band), bf16), vm((D, HD), bf16),
+            vm((rows, D) if roomy else (1, 16, HD), bf16), vm((D, band), bf16), vm((HD, D), bf16),
             vm((rows, D), bf16), vm((rows, shard), bf16), vm((rows, shard), bf16), vm((rows, shard), bf16),
             vm((rows, band), bf16), vm((rows, HD), bf16), vm((CONV, MIXED * HD), f32), vm((rows + 8, MIXED * HD), f32),
             vm((8, MIXED * HD), f32), vm((8, HD), f32), vm((HD, HD), f32),
             *chained(n, piece, shard, lead=(2,)), *chained(shard // m, D), *chained(piece, D), *chained(n, piece, band),
-            vm((8, D), f32), vm((m - 1, 8, D), f32), vm((1, D), f32), vm((m - 1, 1, D), f32), vm((2, n, piece, shard), bf16), vm((n, piece, band), bf16),
+            vm((8, D), f32), vm((m - 1, 8, D), f32), vm((1, D), f32), vm((m - 1, 1, D), f32), vm((n, 2, piece, shard), bf16), vm((n, piece, band), bf16),
             vm((n // 2, T, D), f32 if roomy else bf16), *[vm((n // 2, T, D), bf16)] * 4,
             DMA((14,)), DMA((GROUPS,)), *chain_sems(2, m - 1), *chain_sems(m - 1), *chain_sems(m - 1),
-            *chain_sems(D // TILE, m - 1), DMA((2, m - 1)), DMA((2, m - 1)), DMA((2, n - 1)), DMA((2, n - 1)), DMA((n,)), DMA((n,)),
+            *chain_sems(D // TILE, m - 1), DMA((2, m - 1)), DMA((2, m - 1)), DMA((n - 1,)), DMA((n - 1,)), DMA((n,)), DMA((n,)),
             DMA((2, n - 1)), DMA((2, n - 1)),
             *[DMA((n // 2,))] * 4, *gather_sems(n),
         ],
@@ -1110,7 +1200,7 @@
     for i in range(2):
         for source in range(n):
             at = i * FF + source * shard
-            g_gate_up[:, at : at + shard] = gu_parts[i, source].astype(f32)
+            g_gate_up[:, at : at + shard] = gu_parts[source, i].astype(f32)
     g_gain_in[...] = jnp.sum(last[...], axis=0)
     g_gain_mid[...] = jnp.sum(sums[:, 0:1, :], axis=0)
     width = MIXED * HD
@@ -1154,7 +1244,7 @@
     T = tokens.shape[1]
     gain = gain_head.reshape(1, HD)
     gain_in, gain_mid = gain_in.reshape(1, D), gain_mid.reshape(1, D)
-    rows, cotangent = tokens[0], grad_out[0]
+    rows, cotangent, small_weight = tokens[0], grad_out[0], small_weight.T
     gated, normed, out_all, proj, small, mixed, states, news, invs, head_rows = run_forward(
         seq, rep, T, doc_lengths, gate_bias, decay_rate, rows, cotangent, gain_in, in_weight, small_weight, conv_weight, gain
     )

time: 182 us -> 170 us (0.934)
  Pallas kernels: 177 us -> 168 us
  local copies, waits for them, and re-layouts: 1.89 us -> 0 us
    pallas_call x1, Pallas kernels: 103 us -> 95.5 us  [run_back(): pl.pallas_call(functools.partial(back_kernel, n, m, rep, T, piece, shard,...]
    unnamed x1 -> x0, local copies, waits for them, and re-layouts: 1.89 us -> none
where the time goes in v4:
time: 170 us; the launch traced here: 169 us
  Pallas kernels  168 us (99%)
    pallas_call x1, Pallas kernels, run_back(): pl.pallas_call(functools.partial(back_kernel, n, m, rep, T, piece, shard,...  95.5 us
    pallas_call x1, Pallas kernels, run_forward(): pl.pallas_call(functools.partial(forward_kernel, n, rep, T), out_shape=(s...  46.3 us
    pallas_call x1, Pallas kernels, run_feed(): pl.pallas_call(functools.partial(feed_kernel, n, T, steps), grid=(steps,)...  23.3 us

profile of v4, /device:TPU:0, one launch (start us, length us, event | category | flops | bytes accessed | tf_op | source)
XLA Modules:
  0.0 169.2 jit_solution(3732381495442467347)
XLA Ops:
  0.6 46.3 %mixer_forward.1 = (bf16[128,1024]{1,0:T(8,128)(2,1)}, bf16[1024,1024]{1,0:T(8,128)(2,1)}, bf16[1024,1024]{1,0:T(8,128)(2,1)}, bf16[1024,768]{1,0:T(8,128)(2,1)}...) custom-call(s32[1,8]{1,0:T(1,128)} %lengths.3, ...), custom_call_target="tpu_custom_call" | custom-call | tf_op jit(solution)/shard_map/mixer_forward/pallas_call | solution.py:528
  46.9 23.3 %feed_forward.1 = (bf16[128,1024]{1,0:T(8,128)(2,1)}, f32[128,1024]{1,0:T(8,128)}, bf16[1024,1024]{1,0:T(8,128)(2,1)}, f32[1,1024]{1,0:T(1,128)}) custom-call(bf16[128,1024]{1,0:T(8,128)(2,1)} %bitcast.13, bf16[128,1024]{1,0:T(8,128)(2,1)} %get-tuple-element.47.gated, bf16[128,1024]{1,0:T(8,128)(2,1)} %bitcast.16, bf16[1024,1024]{1,0:T(8,128)(2,1)} %w_out.3, ...), custom_call_target="tpu_custom_call" | custom-call | tf_op jit(solution)/shard_map/feed_forward/pallas_call | solution.py:601
  70.2 95.5 %backward.1 = (f32[128,1024]{1,0:T(8,128)}, bf16[8,32,768]{2,1,0:T(8,128)(2,1)}, f32[32,1024]{1,0:T(8,128)}, bf16[8,2,32,352]{3,2,1,0:T(8,128)(2,1)}, f32[88,102...) custom-call(s32[1,8]{1,0:T(1,128)} %lengths.3, f32[8]{0:T(128)} %bias_ref.3, f32[8]{0:T(128)} %rate_ref.3, ...), custom_call_target="tpu_custom_call" | custom-call | tf_op jit(solution)/shard_map/backward/pallas_call | solution.py:1162
  165.7 3.3 %outputs.1 = (bf16[128,1024]{1,0:T(8,128)(2,1)}, f32[128,1024]{1,0:T(8,128)}, f32[32,6144]{1,0:T(8,128)}, f32[32,1024]{1,0:T(8,128)}, f32[32,5632]{1,0:T(8,128)}...) custom-call(bf16[128,1024]{1,0:T(8,128)(2,1)} %get-tuple-element.48., ...), custom_call_target="tpu_custom_call" | custom-call | tf_op jit(solution)/shard_map/outputs/pallas_call | solution.py:1226
